TPU v7x, 32 devices: a whole 2x2x4 slice. The times are simulated.
32 devices in a mesh: gy: 16 (over z, y, x), gx: 2 (over core).
Axes of the slice: x: 2, y: 2, z: 4, core: 2. Of those that a mesh axis runs over, the one named last changes fastest.
Arguments:
- state: float32 [3, 8, 512, 512], P(None, None, 'gy', 'gx'), may hold values from -6 to 6
- parent_rows: bfloat16 [2048, 24, 256], P(('gy', 'gx')), may hold values from -6 to 6
- dest: int32 [2048, 1], P(('gy', 'gx')), may hold values from 0 to 15; in each aligned block of 64 rows (0 to 63, 64 to 127, ...) at most 8 rows name the same one
- pick: int32 [2048], P(('gy', 'gx')), may hold values from 0 to 63
- offset: int32 [2048], P(('gy', 'gx')), may hold values from 0 to 31
- wet: int32 [512, 512], P('gy', 'gx'), may hold values 0 or 1
Outputs:
- state_out: float32 [3, 8, 512, 512], P(None, None, 'gy', 'gx')
- profile: float32 [3, 512], P(None, 'gy')
Inputs may be any that keep to these rules, and one draw needn't show every extreme that they name: `dest`: among the 64 rows of one device at most 8 name the same tile, a bound that some block reaches.
All inputs are finite; a program needn't handle non-finite values. No bound on the sum of `wet` on one device may be relied on, other than what follows from the above.
Results may differ from a plain program's by a relative error of at most 0.0003.
Values may be sent and summed in bfloat16 or wider, within the bound.
No kernel may reach another device: no remote copies, remote signals or barrier semaphores. Data moves between devices by JAX's collectives and lax.ppermute only.
A program may use at most 64 MiB of HBM per device.

v0:
```python
import jax
import jax.numpy as jnp
from jax import lax
from jax.sharding import PartitionSpec as P

SEND = 64
STEPS = 3


KH = 0.2
KZ = 0.05
ADV = 0.25
PG = 0.5
GAMMA = 0.5
DISPERSE = 2.0


def padded_2(cells, sides, width):
    for axis, dim in sides:
        count = lax.axis_size(axis)
        ends = count - 1
        head = lax.slice_in_dim(cells, 0, width, axis=dim)
        tail = lax.slice_in_dim(cells, cells.shape[dim] - width, cells.shape[dim], axis=dim)
        cells = jnp.concatenate(
            [
                lax.ppermute(tail, axis, [(i, (i + 1) % count) for i in range(ends)]),
                cells,
                lax.ppermute(head, axis, [((i + 1) % count, i) for i in range(ends)]),
            ],
            axis=dim,
        )
    return cells


def advance(padded, force, count, mask):
    centre = padded[:, :, 1:-1, 1:-1]
    east = padded[:, :, 1:-1, 2:]
    west = padded[:, :, 1:-1, :-2]
    north = padded[:, :, 2:, 1:-1]
    south = padded[:, :, :-2, 1:-1]
    lap = east + west + north + south - 4.0 * centre
    upper = jnp.concatenate([centre[:, 1:], centre[:, -1:]], axis=1)
    lower = jnp.concatenate([centre[:, :1], centre[:, :-1]], axis=1)
    lapz = upper + lower - 2.0 * centre
    ddx = 0.5 * (east[0] - west[0])
    ddy = 0.5 * (north[0] - south[0])
    tracer, across, along = (centre[0], centre[1], centre[2])
    tnew = tracer + KH * lap[0] + KZ * lapz[0] - ADV * (across * ddx + along * ddy)
    unew = across + KH * lap[1] + KZ * lapz[1] - PG * ddx
    vnew = along + KH * lap[2] + KZ * lapz[2] - PG * ddy
    relax = 1.0 / (1.0 + GAMMA * count)
    tnew = (tnew + GAMMA * force[0]) * relax
    unew = unew * relax
    vnew = (vnew + GAMMA * force[1]) * relax
    return jnp.stack([tnew, unew, vnew]) * mask


def per_device(state, parent_rows, dest, pick, offset, wet):
    levels = state.shape[1]
    tile_rows = state.shape[2]
    tile_cols = state.shape[3]
    senders = lax.axis_size("gy")
    capacity = 2 * SEND // senders
    slots = senders * capacity
    target = dest[:, 0]
    order = jnp.arange(SEND, dtype=jnp.int32)
    same = (target[None, :] == target[:, None]) & (order[None, :] < order[:, None])
    rank = jnp.sum(same.astype(jnp.int32), axis=1)
    slot_of = target * capacity + rank
    select = (slot_of[None, :] == jnp.arange(slots, dtype=jnp.int32)[:, None]).astype(jnp.float32)
    picking = (pick[:, None] == order[None, :]).astype(jnp.float32)
    chosen = jnp.dot(select, picking, preferred_element_type=jnp.float32).astype(jnp.bfloat16)
    outgoing = jnp.dot(chosen, parent_rows.reshape(SEND, -1), preferred_element_type=jnp.float32)
    outgoing = outgoing.astype(jnp.bfloat16).reshape(senders, capacity, 3 * levels, tile_cols)
    labels = jnp.dot(select, (offset + 1).astype(jnp.float32), preferred_element_type=jnp.float32)
    labels = labels.astype(jnp.bfloat16).reshape(senders, capacity)
    arrived, arrived_labels = (
        lax.all_to_all(outgoing, "gy", split_axis=0, concat_axis=0, tiled=True),
        lax.all_to_all(labels, "gy", split_axis=0, concat_axis=0, tiled=True),
    )
    row_ids = (jnp.arange(tile_rows, dtype=jnp.int32) + 1).astype(jnp.float32)
    landing = (
        arrived_labels.reshape(slots).astype(jnp.float32)[None, :] == row_ids[:, None]
    ).astype(jnp.float32)
    force = jnp.dot(
        landing.astype(jnp.bfloat16), arrived.reshape(slots, -1), preferred_element_type=jnp.float32
    )
    force = jnp.transpose(force.reshape(tile_rows, 3, levels, tile_cols), (1, 2, 0, 3))
    row_count = jnp.sum(landing, axis=1)
    count = jnp.broadcast_to(row_count[:, None], (tile_rows, tile_cols))
    mask = wet.astype(jnp.float32)
    current = state
    for step in range(STEPS):
        padded = padded_2(current, (("gy", 2), ("gx", 3)), 1)
        current = advance(padded, force, count, mask)
    tracer = current[0]
    along = current[2]
    stokes = force[2] / (1.0 + count)
    rim = padded_2(tracer, (("gy", 1),), 1)
    ddy = 0.5 * (rim[:, 2:] - rim[:, :-2])
    third = -DISPERSE * jnp.sum(ddy, axis=(0, 2))
    partial_value = jnp.stack(
        [jnp.sum(along * tracer, axis=(0, 2)), jnp.sum(stokes * tracer, axis=(0, 2)), third]
    )
    summed = lax.psum(partial_value, "gx")
    entries = 3 * tile_rows * senders
    squares = lax.psum(jnp.sum(summed * summed), "gy")
    scale = jnp.sqrt(squares / entries + 1e-06)
    return (current, summed / scale)


def solution(mesh):
    in_specs = (
        P(None, None, "gy", "gx"),
        P(("gy", "gx"), None, None),
        P(("gy", "gx"), None),
        P(("gy", "gx")),
        P(("gy", "gx")),
        P("gy", "gx"),
    )
    out_specs = (P(None, None, "gy", "gx"), P(None, "gy"))
    return jax.shard_map(
        per_device, mesh=mesh, in_specs=in_specs, out_specs=out_specs, check_vma=False
    )
```

profile of v0, /device:TPU:0, one launch (start us, length us, event | category | flops | bytes accessed | tf_op | source)
XLA Modules:
  0.0 161.5 jit_solution(3175956114810485390)
XLA Ops:
  0.6 0.9 convert_reduce_fusion
  1.6 0.7 multiply_add_fusion
  2.2 0.8 fusion
  3.0 0.7 all_to_all.12
  3.7 8.3 %all-to-all-start = ((bf16[16,1,8]{2,1,0:T(2,128)(2,1)}), bf16[16,1,8]{2,1,0:T(2,128)(2,1)S(1)}, u32[]{:S(2)}, u32[]{:S(2)}) async-start(bf16[16,1,8]{2,1,0:T(2,128)(2,1)} %all_to_all.12), calls=%async_computation | async-start | bytes 16384 | tf_op jit(solution)/shard_map/all_to_all | solution.py:79
  12.1 1.3 copy.17
  13.4 0.9 convolution_convert_fusion
  14.2 1.5 copy.14
  15.8 3.5 %all-to-all-done = bf16[16,1,8]{2,1,0:T(2,128)(2,1)S(1)} async-done(((bf16[16,1,8]{2,1,0:T(2,128)(2,1)}), bf16[16,1,8]{2,1,0:T(2,128)(2,1)S(1)}, u32[]{:S(2)}, u32[]{:S(2)}) %all-to-all-start) | async-done | bytes 288 | tf_op jit(solution)/shard_map/all_to_all | solution.py:79
  19.2 3.7 %all-to-all-start.1 = ((bf16[16,8,24,256]{3,2,1,0:T(8,128)(2,1)}), bf16[16,8,24,256]{3,2,1,0:T(8,128)(2,1)S(1)}, u32[]{:S(2)}, u32[]{:S(2)}) async-start(bf16[16,8,24,256]{3,2,1,0:T(8,128)(2,1)} %copy.14), calls=%async_computation.1 | async-start | bytes 3145728 | tf_op jit(solution)/shard_map/all_to_all | solution.py:78
  23.0 3.7 %collective-permute-start = (f32[3,8,1,256]{3,2,1,0:T(1,128)S(1)}, f32[3,8,1,256]{3,2,1,0:T(1,128)S(1)}, u32[]{:S(2)}, u32[]{:S(2)}) collective-permute-start(f32[3,8,1,256]{3,2,1,0:T(1,128)S(1)} %get-tuple-element.50), channel_id=1, source_target_pairs={{0,2},{2,4},{4,6},{6,8},{8,10},{10,12},{12,14},{14,16},{16,18},{18... | collective-permute-start | bytes 73736 | tf_op jit(solution)/shard_map/ppermute | solution.py:26
  26.7 1.3 collective-permute-start.1
  28.1 1.0 constant_dynamic-update-slice_fusion
  29.1 1.0 fusion.99
  30.4 2.1 %collective-permute-done.1 = f32[3,8,1,256]{3,2,1,0:T(1,128)S(1)} collective-permute-done((f32[3,8,1,256]{3,2,1,0:T(1,128)S(1)}, f32[3,8,1,256]{3,2,1,0:T(1,128)S(1)}, u32[]{:S(2)}, u32[]{:S(2)}) %collective-permute-start.1) | collective-permute-done | bytes 24608 | tf_op jit(solution)/shard_map/ppermute | solution.py:28
  32.6 1.1 fusion.90
  33.7 1.3 collective-permute-start.2
  35.0 4.6 %collective-permute-start.3 = (f32[3,8,34,1]{3,2,1,0:T(8,128)}, f32[3,8,34,1]{3,2,1,0:T(8,128)}, u32[]{:S(2)}, u32[]{:S(2)}) collective-permute-start(f32[3,8,34,1]{3,2,1,0:T(8,128)} %get-tuple-element.24), channel_id=1, source_target_pairs={{0,1},{2,3},{4,5},{6,7},{8,9},{10,11},{12,13},{14,15},{16,17},{18,... | collective-permute-start | bytes 9800 | tf_op jit(solution)/shard_map/ppermute | solution.py:26
  39.6 1.7 %dynamic-update-slice.1 = f32[3,8,33,256]{3,2,1,0:T(8,128)} dynamic-update-slice(f32[3,8,33,256]{3,2,1,0:T(8,128)} %constant_dynamic-update-slice_fusion, f32[3,8,1,256]{3,2,1,0:T(1,128)S(1)} %collective-permute-done.1, s32[]{} %constant.62, s32[]{} %constant.62, s32[]{} %constant.63, s32[]{} %constant.62) | dynamic-update-slice | bytes 49156 | tf_op jit(solution)/shard_map/concatenate | solution.py:24
  41.3 2.0 %pad_maximum_fusion = (f32[3,8,34,257]{3,2,1,0:T(8,128)S(1)}, f32[3,8,34,257]{3,2,1,0:T(8,128)S(1)}) fusion(f32[3,8,34,1]{3,2,1,0:T(8,128)} %collective-permute-done.2, f32[3,8,1,256]{3,2,1,0:T(1,128)S(1)} %collective-permute-done.1, f32[3,8,32,256]{3,2,1,0:T(8,128)S(1)} %copy-done, f32[3,8,1,256]{3,2,1,0:T(1,128)S(1)} %collective-permute-done, ...), kind=kLoop, calls=%fused_computation.1 | loop fusion | flops 1258272 | bytes 2519808 | tf_op jit(solution)/shard_map/concatenate | solution.py:24
  43.4 1.7 %fusion.13 = (f32[3,8,32,256]{3,2,1,0:T(8,128)}, f32[3,8,32,256]{3,2,1,0:T(8,128)}) fusion(f32[3,8,1,256]{3,2,1,0:T(1,128)S(1)} %collective-permute-done, f32[3,8,32,256]{3,2,1,0:T(8,128)S(1)} %copy-done, f32[3,8,33,256]{3,2,1,0:T(8,128)S(1)} %copy-done.1, f32[3,8,34,257]{3,2,1,0:T(8,128)S(1)} %get-tuple-element.30, ...), kind=kLoop, calls=%fused_computation.36 | loop fusion | flops 2162688 | bytes 6316032 | tf_op jit(solution)/shard_map/sub | solution.py:41
  45.1 11.6 %all-to-all-done.1 = bf16[16,8,24,256]{3,2,1,0:T(8,128)(2,1)S(1)} async-done(((bf16[16,8,24,256]{3,2,1,0:T(8,128)(2,1)}), bf16[16,8,24,256]{3,2,1,0:T(8,128)(2,1)S(1)}, u32[]{:S(2)}, u32[]{:S(2)}) %all-to-all-start.1) | async-done | bytes 1572896 | tf_op jit(solution)/shard_map/all_to_all | solution.py:78
  56.7 1.5 copy.18
  58.2 1.9 %copy.15 = bf16[6144,128]{1,0:T(8,128)(2,1)S(1)} copy(bf16[6144,128]{0,1:T(8,128)(2,1)} %bitcast.53) | data formatting | bytes 3145728 | tf_op jit(solution)/shard_map/dot_general | solution.py:85
  60.2 0.7 convolution_bitcast_fusion
  61.5 1.5 fusion.67
  63.4 2.6 %collective-permute-start.4 = (f32[3,8,1,256]{3,2,1,0:T(1,128)S(1)}, f32[3,8,1,256]{3,2,1,0:T(1,128)S(1)}, u32[]{:S(2)}, u32[]{:S(2)}) collective-permute-start(f32[3,8,1,256]{3,2,1,0:T(1,128)S(1)} %get-tuple-element.42), channel_id=1, source_target_pairs={{0,2},{2,4},{4,6},{6,8},{8,10},{10,12},{12,14},{14,16},{16,18},{18... | collective-permute-start | bytes 73736 | tf_op jit(solution)/shard_map/ppermute | solution.py:26
  66.0 1.3 collective-permute-start.5
  67.5 5.7 %collective-permute-done.5 = f32[3,8,1,256]{3,2,1,0:T(1,128)S(1)} collective-permute-done((f32[3,8,1,256]{3,2,1,0:T(1,128)S(1)}, f32[3,8,1,256]{3,2,1,0:T(1,128)S(1)}, u32[]{:S(2)}, u32[]{:S(2)}) %collective-permute-start.5) | collective-permute-done | bytes 24608 | tf_op jit(solution)/shard_map/ppermute | solution.py:28
  73.5 1.3 collective-permute-start.6
  74.8 3.1 %collective-permute-start.7 = (f32[3,8,34,1]{3,2,1,0:T(8,128)S(1)}, f32[3,8,34,1]{3,2,1,0:T(8,128)S(1)}, u32[]{:S(2)}, u32[]{:S(2)}) collective-permute-start(f32[3,8,34,1]{3,2,1,0:T(8,128)S(1)} %get-tuple-element.22), channel_id=1, source_target_pairs={{0,1},{2,3},{4,5},{6,7},{8,9},{10,11},{12,13},{14,15},{16,17},{18,... | collective-permute-start | bytes 9800 | tf_op jit(solution)/shard_map/ppermute | solution.py:26
  77.9 1.4 collective-permute-done.7
  79.3 0.7 pad_maximum_fusion.1
  80.0 0.6 fusion.8
  81.4 6.6 %collective-permute-start.8 = (f32[3,8,1,256]{3,2,1,0:T(1,128)S(1)}, f32[3,8,1,256]{3,2,1,0:T(1,128)S(1)}, u32[]{:S(2)}, u32[]{:S(2)}) collective-permute-start(f32[3,8,1,256]{3,2,1,0:T(1,128)S(1)} %get-tuple-element.34), channel_id=1, source_target_pairs={{0,2},{2,4},{4,6},{6,8},{8,10},{10,12},{12,14},{14,16},{16,18},{18... | collective-permute-start | bytes 73736 | tf_op jit(solution)/shard_map/ppermute | solution.py:26
  88.0 1.3 collective-permute-start.9
  89.5 6.5 %collective-permute-done.9 = f32[3,8,1,256]{3,2,1,0:T(1,128)S(1)} collective-permute-done((f32[3,8,1,256]{3,2,1,0:T(1,128)S(1)}, f32[3,8,1,256]{3,2,1,0:T(1,128)S(1)}, u32[]{:S(2)}, u32[]{:S(2)}) %collective-permute-start.9) | collective-permute-done | bytes 24608 | tf_op jit(solution)/shard_map/ppermute | solution.py:28
  96.3 1.3 collective-permute-start.10
  97.6 3.1 %collective-permute-start.11 = (f32[3,8,34,1]{3,2,1,0:T(8,128)S(1)}, f32[3,8,34,1]{3,2,1,0:T(8,128)S(1)}, u32[]{:S(2)}, u32[]{:S(2)}) collective-permute-start(f32[3,8,34,1]{3,2,1,0:T(8,128)S(1)} %get-tuple-element.20), channel_id=1, source_target_pairs={{0,1},{2,3},{4,5},{6,7},{8,9},{10,11},{12,13},{14,15},{16,17},{18,... | collective-permute-start | bytes 9800 | tf_op jit(solution)/shard_map/ppermute | solution.py:26
  100.8 1.4 collective-permute-done.11
  102.2 0.7 pad_maximum_fusion.2
  102.9 0.6 fusion.3
  104.3 1.3 collective-permute-start.12
  105.6 6.4 %collective-permute-start.13 = (f32[8,1,256]{2,1,0:T(1,128)S(1)}, f32[8,1,256]{2,1,0:T(1,128)S(1)}, u32[]{:S(2)}, u32[]{:S(2)}) collective-permute-start(f32[8,1,256]{2,1,0:T(1,128)S(1)} %get-tuple-element.56), channel_id=1, source_target_pairs={{0,2},{2,4},{4,6},{6,8},{8,10},{10,12},{12,14},{14,16},{16,18},{18... | collective-permute-start | bytes 24584 | tf_op jit(solution)/shard_map/ppermute | solution.py:26
  112.2 1.1 collective-permute-done.13
  113.5 2.5 %psum.14 = f32[3,32]{1,0:T(4,128)S(1)} all-reduce(f32[3,32]{1,0:T(4,128)S(1)} %pad_maximum_fusion.13), channel_id=1, replica_groups=mesh['gy'=16,'gx'=2] {'gx'}, use_global_device_ids=true, to_apply=%region_5.0 | all-reduce | flops 96 | bytes 768 | tf_op jit(solution)/shard_map/psum | solution.py:105
  116.0 0.6 multiply_reduce_fusion
  116.6 43.7 %psum.15 = f32[]{:T(128)} all-reduce(f32[]{:T(128)} %multiply_reduce_fusion), channel_id=1, replica_groups=mesh['gy'=16,'gx'=2] {'gy'}, use_global_device_ids=true, to_apply=%region_7.0 | all-reduce | flops 1 | bytes 8 | tf_op jit(solution)/shard_map/psum | solution.py:107
  (58 shorter events, 5.0 us)
Async XLA Ops:
  0.6 12.7 %copy-start.7 = (s32[64]{0:T(128)S(1)}, s32[64]{0:T(128)}, u32[]{:S(2)}) copy-start(s32[64]{0:T(128)} %param.9) | copy-start | bytes 772
  3.7 15.5 %all-to-all-start = ((bf16[16,1,8]{2,1,0:T(2,128)(2,1)}), bf16[16,1,8]{2,1,0:T(2,128)(2,1)S(1)}, u32[]{:S(2)}, u32[]{:S(2)}) async-start(bf16[16,1,8]{2,1,0:T(2,128)(2,1)} %all_to_all.12), calls=%async_computation | async-start | bytes 16384 | tf_op jit(solution)/shard_map/all_to_all | solution.py:79
  15.8 7.2 %copy-start = (f32[3,8,32,256]{3,2,1,0:T(8,128)S(1)}, f32[3,8,32,256]{3,2,1,0:T(8,128)}, u32[]{:S(2)}) copy-start(f32[3,8,32,256]{3,2,1,0:T(8,128)} %param.6) | copy-start | bytes 2359300
  15.8 12.2 %copy-start.6 = (s32[32,256]{1,0:T(8,128)S(1)}, s32[32,256]{1,0:T(8,128)}, u32[]{:S(2)}) copy-start(s32[32,256]{1,0:T(8,128)} %param.11) | copy-start | bytes 98308
  19.2 37.4 %all-to-all-start.1 = ((bf16[16,8,24,256]{3,2,1,0:T(8,128)(2,1)}), bf16[16,8,24,256]{3,2,1,0:T(8,128)(2,1)S(1)}, u32[]{:S(2)}, u32[]{:S(2)}) async-start(bf16[16,8,24,256]{3,2,1,0:T(8,128)(2,1)} %copy.14), calls=%async_computation.1 | async-start | bytes 3145728 | tf_op jit(solution)/shard_map/all_to_all | solution.py:78
  23.0 7.4 %collective-permute-start = (f32[3,8,1,256]{3,2,1,0:T(1,128)S(1)}, f32[3,8,1,256]{3,2,1,0:T(1,128)S(1)}, u32[]{:S(2)}, u32[]{:S(2)}) collective-permute-start(f32[3,8,1,256]{3,2,1,0:T(1,128)S(1)} %get-tuple-element.50), channel_id=1, source_target_pairs={{0,2},{2,4},{4,6},{6,8},{8,10},{10,12},{12,14},{14,16},{16,18},{18... | collective-permute-start | bytes 73736 | tf_op jit(solution)/shard_map/ppermute | solution.py:26
  26.7 5.7 %collective-permute-start.1 = (f32[3,8,1,256]{3,2,1,0:T(1,128)S(1)}, f32[3,8,1,256]{3,2,1,0:T(1,128)S(1)}, u32[]{:S(2)}, u32[]{:S(2)}) collective-permute-start(f32[3,8,1,256]{3,2,1,0:T(1,128)S(1)} %get-tuple-element.49), channel_id=1, source_target_pairs={{2,0},{4,2},{6,4},{8,6},{10,8},{12,10},{14,12},{16,14},{18,16},{20... | collective-permute-start | bytes 73736 | tf_op jit(solution)/shard_map/ppermute | solution.py:28
  33.7 7.6 %collective-permute-start.2 = (f32[3,8,34,1]{3,2,1,0:T(8,128)}, f32[3,8,34,1]{3,2,1,0:T(8,128)}, u32[]{:S(2)}, u32[]{:S(2)}) collective-permute-start(f32[3,8,34,1]{3,2,1,0:T(8,128)} %get-tuple-element.23), channel_id=1, source_target_pairs={{1,0},{3,2},{5,4},{7,6},{9,8},{11,10},{13,12},{15,14},{17,16},{19,... | collective-permute-start | bytes 9800 | tf_op jit(solution)/shard_map/ppermute | solution.py:28
  35.0 6.3 %collective-permute-start.3 = (f32[3,8,34,1]{3,2,1,0:T(8,128)}, f32[3,8,34,1]{3,2,1,0:T(8,128)}, u32[]{:S(2)}, u32[]{:S(2)}) collective-permute-start(f32[3,8,34,1]{3,2,1,0:T(8,128)} %get-tuple-element.24), channel_id=1, source_target_pairs={{0,1},{2,3},{4,5},{6,7},{8,9},{10,11},{12,13},{14,15},{16,17},{18,... | collective-permute-start | bytes 9800 | tf_op jit(solution)/shard_map/ppermute | solution.py:26
  41.3 2.0 %copy-start.1 = (f32[3,8,33,256]{3,2,1,0:T(8,128)S(1)}, f32[3,8,33,256]{3,2,1,0:T(8,128)}, u32[]{:S(2)}) copy-start(f32[3,8,33,256]{3,2,1,0:T(8,128)} %dynamic-update-slice.1) | copy-start | bytes 2433028
  41.3 2.1 %copy-start.5 = (f32[3,7,32,256]{3,2,1,0:T(8,128)S(1)}, f32[3,7,32,256]{3,2,1,0:T(8,128)}, u32[]{:S(2)}) copy-start(f32[3,7,32,256]{3,2,1,0:T(8,128)} %get-tuple-element.54) | copy-start | bytes 2064388
  60.1 1.1 copy-start.3
  60.1 1.4 copy-start.4
  63.4 4.1 %collective-permute-start.4 = (f32[3,8,1,256]{3,2,1,0:T(1,128)S(1)}, f32[3,8,1,256]{3,2,1,0:T(1,128)S(1)}, u32[]{:S(2)}, u32[]{:S(2)}) collective-permute-start(f32[3,8,1,256]{3,2,1,0:T(1,128)S(1)} %get-tuple-element.42), channel_id=1, source_target_pairs={{0,2},{2,4},{4,6},{6,8},{8,10},{10,12},{12,14},{14,16},{16,18},{18... | collective-permute-start | bytes 73736 | tf_op jit(solution)/shard_map/ppermute | solution.py:26
  66.0 7.2 %collective-permute-start.5 = (f32[3,8,1,256]{3,2,1,0:T(1,128)S(1)}, f32[3,8,1,256]{3,2,1,0:T(1,128)S(1)}, u32[]{:S(2)}, u32[]{:S(2)}) collective-permute-start(f32[3,8,1,256]{3,2,1,0:T(1,128)S(1)} %get-tuple-element.41), channel_id=1, source_target_pairs={{2,0},{4,2},{6,4},{8,6},{10,8},{12,10},{14,12},{16,14},{18,16},{20... | collective-permute-start | bytes 73736 | tf_op jit(solution)/shard_map/ppermute | solution.py:28
  73.5 4.4 %collective-permute-start.6 = (f32[3,8,34,1]{3,2,1,0:T(8,128)S(1)}, f32[3,8,34,1]{3,2,1,0:T(8,128)S(1)}, u32[]{:S(2)}, u32[]{:S(2)}) collective-permute-start(f32[3,8,34,1]{3,2,1,0:T(8,128)S(1)} %get-tuple-element.21), channel_id=1, source_target_pairs={{1,0},{3,2},{5,4},{7,6},{9,8},{11,10},{13,12},{15,14},{17,16},{19,... | collective-permute-start | bytes 9800 | tf_op jit(solution)/shard_map/ppermute | solution.py:28
  74.8 4.5 %collective-permute-start.7 = (f32[3,8,34,1]{3,2,1,0:T(8,128)S(1)}, f32[3,8,34,1]{3,2,1,0:T(8,128)S(1)}, u32[]{:S(2)}, u32[]{:S(2)}) collective-permute-start(f32[3,8,34,1]{3,2,1,0:T(8,128)S(1)} %get-tuple-element.22), channel_id=1, source_target_pairs={{0,1},{2,3},{4,5},{6,7},{8,9},{10,11},{12,13},{14,15},{16,17},{18,... | collective-permute-start | bytes 9800 | tf_op jit(solution)/shard_map/ppermute | solution.py:26
  81.4 8.1 %collective-permute-start.8 = (f32[3,8,1,256]{3,2,1,0:T(1,128)S(1)}, f32[3,8,1,256]{3,2,1,0:T(1,128)S(1)}, u32[]{:S(2)}, u32[]{:S(2)}) collective-permute-start(f32[3,8,1,256]{3,2,1,0:T(1,128)S(1)} %get-tuple-element.34), channel_id=1, source_target_pairs={{0,2},{2,4},{4,6},{6,8},{8,10},{10,12},{12,14},{14,16},{16,18},{18... | collective-permute-start | bytes 73736 | tf_op jit(solution)/shard_map/ppermute | solution.py:26
  88.0 8.0 %collective-permute-start.9 = (f32[3,8,1,256]{3,2,1,0:T(1,128)S(1)}, f32[3,8,1,256]{3,2,1,0:T(1,128)S(1)}, u32[]{:S(2)}, u32[]{:S(2)}) collective-permute-start(f32[3,8,1,256]{3,2,1,0:T(1,128)S(1)} %get-tuple-element.33), channel_id=1, source_target_pairs={{2,0},{4,2},{6,4},{8,6},{10,8},{12,10},{14,12},{16,14},{18,16},{20... | collective-permute-start | bytes 73736 | tf_op jit(solution)/shard_map/ppermute | solution.py:28
  96.3 4.4 %collective-permute-start.10 = (f32[3,8,34,1]{3,2,1,0:T(8,128)S(1)}, f32[3,8,34,1]{3,2,1,0:T(8,128)S(1)}, u32[]{:S(2)}, u32[]{:S(2)}) collective-permute-start(f32[3,8,34,1]{3,2,1,0:T(8,128)S(1)} %get-tuple-element.19), channel_id=1, source_target_pairs={{1,0},{3,2},{5,4},{7,6},{9,8},{11,10},{13,12},{15,14},{17,16},{19,... | collective-permute-start | bytes 9800 | tf_op jit(solution)/shard_map/ppermute | solution.py:28
  97.6 4.5 %collective-permute-start.11 = (f32[3,8,34,1]{3,2,1,0:T(8,128)S(1)}, f32[3,8,34,1]{3,2,1,0:T(8,128)S(1)}, u32[]{:S(2)}, u32[]{:S(2)}) collective-permute-start(f32[3,8,34,1]{3,2,1,0:T(8,128)S(1)} %get-tuple-element.20), channel_id=1, source_target_pairs={{0,1},{2,3},{4,5},{6,7},{8,9},{10,11},{12,13},{14,15},{16,17},{18,... | collective-permute-start | bytes 9800 | tf_op jit(solution)/shard_map/ppermute | solution.py:26
  104.2 57.3 %copy-start.2 = (f32[3,8,32,256]{3,2,1,0:T(8,128)}, f32[3,8,32,256]{3,2,1,0:T(8,128)S(1)}, u32[]{:S(2)}) copy-start(f32[3,8,32,256]{3,2,1,0:T(8,128)S(1)} %maximum_multiply_fusion.2) | copy-start | bytes 2359300
  104.3 7.9 %collective-permute-start.12 = (f32[8,1,256]{2,1,0:T(1,128)S(1)}, f32[8,1,256]{2,1,0:T(1,128)S(1)}, u32[]{:S(2)}, u32[]{:S(2)}) collective-permute-start(f32[8,1,256]{2,1,0:T(1,128)S(1)} %get-tuple-element.55), channel_id=1, source_target_pairs={{2,0},{4,2},{6,4},{8,6},{10,8},{12,10},{14,12},{16,14},{18,16},{20... | collective-permute-start | bytes 24584 | tf_op jit(solution)/shard_map/ppermute | solution.py:28
  105.6 7.7 %collective-permute-start.13 = (f32[8,1,256]{2,1,0:T(1,128)S(1)}, f32[8,1,256]{2,1,0:T(1,128)S(1)}, u32[]{:S(2)}, u32[]{:S(2)}) collective-permute-start(f32[8,1,256]{2,1,0:T(1,128)S(1)} %get-tuple-element.56), channel_id=1, source_target_pairs={{0,2},{2,4},{4,6},{6,8},{8,10},{10,12},{12,14},{14,16},{16,18},{18... | collective-permute-start | bytes 24584 | tf_op jit(solution)/shard_map/ppermute | solution.py:26
where the time goes:
time: 162 us
  starting transfers between devices  51.1 us (32%)
  blocking collectives  46.1 us (28%)
  waiting for transfers between devices  33.3 us (21%)
  local copies, waits for them, and re-layouts  13.5 us (8%)
  other arithmetic  13.4 us (8%)
  matrix products  2.32 us (1%)
  between operations  1.8 us (1%)
    psum x1, blocking collectives, per_device(): squares = lax.psum(jnp.sum(summed * summed), 'gy')  43.7 us
    ppermute x7, starting transfers between devices, padded_2(): lax.ppermute(tail, axis, [(i, (i + 1) % count) for i in range(ends)])  30 us
    ppermute x7, waiting for transfers between devices, padded_2(): lax.ppermute(head, axis, [((i + 1) % count, i) for i in range(ends)])  14.2 us
    all_to_all x1, waiting for transfers between devices, per_device(): lax.all_to_all(outgoing, 'gy', split_axis=0, concat_axis=0, tiled=True)  11.6 us
    ppermute x7, starting transfers between devices, padded_2(): lax.ppermute(head, axis, [((i + 1) % count, i) for i in range(ends)])  9.03 us
    all_to_all x1, starting transfers between devices, per_device(): lax.all_to_all(labels, 'gy', split_axis=0, concat_axis=0, tiled=True)  8.31 us
    unnamed x19, local copies, waits for them, and re-layouts  4.54 us
    ppermute x7, waiting for transfers between devices, padded_2(): lax.ppermute(tail, axis, [(i, (i + 1) % count) for i in range(ends)])  4.03 us
  transfers between devices with their start and end apart: 16, of which 8 were waited for; matrix products, arithmetic and copies ran while one was open for 8% of the time, Pallas kernels for 0%

commit v1 on v0

v1 whole, which is shorter than its diff:
```python
import functools

import jax
import jax.numpy as jnp
from jax import lax
from jax.experimental import pallas as pl
from jax.experimental.pallas import tpu as pltpu
from jax.sharding import PartitionSpec as P

SEND = 64
STEPS = 3

KH = 0.2
KZ = 0.05
ADV = 0.25
PG = 0.5
GAMMA = 0.5
DISPERSE = 2.0

EDGE = 3
RIM = 4
LANES = 128
VMEM_LIMIT = 48 * 1024 * 1024


def call(body, out_shape, flops=0, moved=0, **more):
    return pl.pallas_call(
        body,
        out_shape=out_shape,
        compiler_params=pltpu.CompilerParams(vmem_limit_bytes=VMEM_LIMIT),
        cost_estimate=pl.CostEstimate(flops=flops, bytes_accessed=moved, transcendentals=0),
        **more,
    )


def iota(shape, dim):
    return lax.broadcasted_iota(jnp.int32, shape, dim)


def gather_body(capacity, slots, dest_ref, pick_ref, offset_ref, rows_ref, out_ref):
    send, planes, cols = rows_ref.shape
    dest = dest_ref[...]
    eye = iota((send, send), 0) == iota((send, send), 1)
    dest_column = jnp.sum(jnp.where(eye, dest, 0), axis=1, keepdims=True)
    earlier = (dest_column == dest) & (iota((send, send), 0) < iota((send, send), 1))
    rank = jnp.sum(earlier.astype(jnp.int32), axis=0, keepdims=True)
    slot_of = dest * capacity + rank
    taken = iota((slots, send), 0) == slot_of
    source = jnp.sum(jnp.where(taken, pick_ref[...] + 1, 0), axis=1, keepdims=True) - 1
    label = jnp.sum(jnp.where(taken, offset_ref[...] + 1, 0), axis=1, keepdims=True)
    group = 8
    lane = iota((slots, send * group), 1)
    select = jnp.concatenate(
        [(lane == source * group + j).astype(jnp.float32).astype(jnp.bfloat16) for j in range(group)], axis=0
    )
    for g in range(planes // group):
        block = rows_ref[:, g * group : (g + 1) * group, :].reshape(send * group, cols)
        got = jnp.dot(select, block, preferred_element_type=jnp.float32).astype(jnp.bfloat16)
        for j in range(group):
            at = (g * group + j) * cols
            out_ref[:, at : at + cols] = got[j * slots : (j + 1) * slots]
    out_ref[:, planes * cols :] = jnp.broadcast_to(label, (slots, LANES)).astype(jnp.float32).astype(jnp.bfloat16)


def landing_body(planes, cols, arrived_ref, force_ref, edge_ref):
    slots = arrived_ref.shape[0]
    rows = force_ref.shape[1]
    width = planes * cols
    label = arrived_ref[:, width:].astype(jnp.float32)
    landing = (label == (iota((slots, LANES), 1) + 1).astype(jnp.float32)).astype(jnp.float32)
    landing = landing.T[:rows].astype(jnp.bfloat16)
    count = jnp.dot(landing, jnp.ones((slots, LANES), jnp.bfloat16), preferred_element_type=jnp.float32)
    lane = iota((rows, LANES), 1)
    moving = 2 * planes // 3
    edge = count
    for j in range(planes):
        force = jnp.dot(landing, arrived_ref[:, j * cols : (j + 1) * cols], preferred_element_type=jnp.float32)
        force_ref[j] = force
        if j < moving:
            at = EDGE * j
            first = pltpu.roll(force[:, :LANES], at, 1)
            edge = jnp.where((lane >= at) & (lane < at + EDGE), first, edge)
            at = EDGE * (moving + j)
            last = pltpu.roll(force[:, cols - LANES :], (at + EDGE) % LANES, 1)
            edge = jnp.where((lane >= at) & (lane < at + EDGE), last, edge)
    edge_ref[...] = edge


def outer_body(force_ref, edge_ref, *refs):
    sides, (up_ref, down_ref) = refs[:-2], refs[-2:]
    rows, cols = force_ref.shape[1:]
    moving = up_ref.shape[0] - 2
    up_ref[:moving] = force_ref[:moving, rows - RIM :]
    down_ref[:moving] = force_ref[:moving, :RIM]
    parts = [edge_ref[...]] + [side[...] for side in sides]
    parts = parts + [jnp.zeros_like(parts[0])] * (4 - len(parts))
    for k in range(2):
        pair = jnp.concatenate(parts[2 * k : 2 * k + 2], axis=1)
        up_ref[moving + k] = pair[rows - RIM :]
        down_ref[moving + k] = pair[:RIM]


def extend_body(state_ref, wet_ref, north_ref, south_ref, out_ref, first_ref, last_ref):
    planes, rows, cols = state_ref.shape
    total = rows + 2 * RIM
    lane = iota((total, LANES), 1)
    first = jnp.zeros((total, LANES), jnp.float32)
    last = jnp.zeros((total, LANES), jnp.float32)
    for j in range(planes + 1):
        own = state_ref[j] if j < planes else wet_ref[...].astype(jnp.float32)
        whole = jnp.concatenate([own, jnp.concatenate([north_ref[j], south_ref[j]], axis=0)], axis=0)
        out_ref[j] = whole
        at = EDGE * j
        keep = (lane >= at) & (lane < at + EDGE)
        first = jnp.where(keep, pltpu.roll(whole[:, :LANES], at, 1), first)
        last = jnp.where(keep, pltpu.roll(whole[:, cols - LANES :], (at + EDGE) % LANES, 1), last)
    first_ref[...] = first
    last_ref[...] = last


def side_tile(west, west_at, east, east_at):
    lane = iota(west.shape, 1)
    right = pltpu.roll(east, (LANES - east_at) % LANES, 1)
    left = pltpu.roll(west, (2 * LANES - EDGE - west_at) % LANES, 1)
    return jnp.where(lane < EDGE, right, jnp.where(lane >= LANES - EDGE, left, 0.0))


def around(field):
    rows, cols = field.shape
    return (
        pltpu.roll(field, cols - 1, 1),
        pltpu.roll(field, 1, 1),
        pltpu.roll(field, rows - 1, 0),
        pltpu.roll(field, 1, 0),
    )


def moved(load, levels, z):
    upper, lower = min(z + 1, levels - 1), max(z - 1, 0)
    results = []
    tracer, across, along = (load(f * levels + z) for f in range(3))
    east, west, north, south = around(tracer)
    ddx, ddy = 0.5 * (east - west), 0.5 * (north - south)
    extra = (ADV * (across * ddx + along * ddy), PG * ddx, PG * ddy)
    for f, centre in enumerate((tracer, across, along)):
        sides = (east, west, north, south) if f == 0 else around(centre)
        lap = (sides[0] + sides[1]) + (sides[2] + sides[3]) - 4.0 * centre
        lapz = load(f * levels + upper) + load(f * levels + lower) - 2.0 * centre
        results.append(centre + KH * lap + KZ * lapz - extra[f])
    return results


def first_body(ext_ref, west_ref, east_ref, out_ref, mask_ref, full_ref):
    planes = ext_ref.shape[0] - 1
    levels = planes // 3
    cols = ext_ref.shape[2]
    west, east = west_ref[...], east_ref[...]
    for j in range(planes + 1):
        tile = side_tile(west, EDGE * j, east, EDGE * j)
        if j == planes:
            mask_ref[:, :cols] = ext_ref[j]
            mask_ref[:, cols:] = tile
        else:
            full_ref[j, :, :cols] = ext_ref[j]
            full_ref[j, :, cols:] = tile
    for z in range(levels):
        for f, value in enumerate(moved(lambda j: full_ref[j], levels, z)):
            out_ref[f * levels + z] = value


def steps_body(sides, devices, first_ref, mask_ref, force_ref, edge_ref, north_ref, south_ref, *refs):
    side_refs = refs[:sides]
    state_ref, parts_ref, push_ref, one_ref, two_ref = refs[sides:]
    planes, total, wide = first_ref.shape
    levels = planes // 3
    rows, cols = force_ref.shape[1:]
    moving = 2 * levels
    mask = mask_ref[...]

    def joined(index):
        return jnp.concatenate([north_ref[index], south_ref[index]], axis=0)

    own_edge = edge_ref[...]
    pairs = [joined(moving), joined(moving + 1)]
    outer = [pairs[k // 2][:, (k % 2) * LANES : (k % 2 + 1) * LANES] for k in range(3)]
    edges = [jnp.concatenate([side[...], outer[1 + k]], axis=0) for k, side in enumerate(side_refs)]
    west, east = edges[0], edges[-1]
    own = jnp.concatenate([own_edge, outer[0]], axis=0)

    def counts(edge):
        return jnp.broadcast_to(edge[:, LANES - 1 :], (total, LANES))

    lane = iota((total, LANES), 1)
    count_side = jnp.where(lane < LANES // 2, counts(east), counts(west))
    count = jnp.concatenate([counts(own)] * (cols // LANES) + [count_side], axis=1)
    relax = mask / (1.0 + GAMMA * count)
    half = GAMMA * relax

    for j in range(moving):
        tile = side_tile(west, EDGE * (moving + j), east, EDGE * j)
        whole = jnp.concatenate([force_ref[j], joined(j)], axis=0)
        push_ref[j, :, :cols] = whole * half[:, :cols]
        push_ref[j, :, cols:] = tile * half[:, cols:]

    def finish(values, z):
        tracer, across, along = values
        return (tracer * relax + push_ref[z], across * relax, along * relax + push_ref[levels + z])

    for z in range(levels):
        for f, value in enumerate(finish([first_ref[f * levels + z] for f in range(3)], z)):
            one_ref[f * levels + z] = value
    for z in range(levels):
        for f, value in enumerate(finish(moved(lambda j: one_ref[j], levels, z), z)):
            two_ref[f * levels + z] = value
    share = 1.0 / (1.0 + count[:rows, :1])
    sums = [jnp.zeros((rows, cols), jnp.float32) for _ in range(3)]
    for z in range(levels):
        values = finish(moved(lambda j: two_ref[j], levels, z), z)
        for f, value in enumerate(values):
            state_ref[f * levels + z] = value[:rows, :cols]
        tracer = values[0]
        inner = tracer[:rows, :cols]
        ddy = pltpu.roll(tracer, total - 1, 0)[:rows, :cols] - pltpu.roll(tracer, 1, 0)[:rows, :cols]
        sums[0] = sums[0] + values[2][:rows, :cols] * inner
        sums[1] = sums[1] + force_ref[moving + z] * inner
        sums[2] = sums[2] + ddy
    raw = [jnp.sum(value, axis=1, keepdims=True) for value in sums]
    raw = [raw[0], raw[1] * share, raw[2] * (-0.5 * DISPERSE)]
    row, lane = iota((rows, LANES), 0), iota((rows, LANES), 1)
    packed = jnp.zeros((rows, LANES), jnp.float32)
    for q in range(3):
        packed = packed + jnp.where(lane == q * rows + row, raw[q], 0.0)
    packed = jnp.sum(packed, axis=0, keepdims=True)
    parts_ref[...] = jnp.broadcast_to(packed, (devices, LANES))


def profile_body(across, along, me_ref, parts_ref, out_ref):
    rows = out_ref.shape[1]
    parts = parts_ref[...]
    devices = parts.shape[0]
    total = parts
    for k in range(1, across):
        total = total + pltpu.roll(parts, devices - k, 0)
    row = iota(parts.shape, 0)
    squares = jnp.sum(jnp.where(row % across == 0, total * total, 0.0), keepdims=True)
    scale = jnp.sqrt(squares / (3 * rows * along) + 1e-06)
    mine = jnp.sum(jnp.where(row == me_ref[0] * across, total, 0.0), axis=0, keepdims=True) / scale
    for q in range(3):
        out_ref[q : q + 1, :] = mine[:, q * rows : (q + 1) * rows]


def per_device(state, parent_rows, dest, pick, offset, wet):
    fields, levels, rows, cols = state.shape
    planes = fields * levels
    moving = 2 * levels
    along, across = lax.axis_size("gy"), lax.axis_size("gx")
    capacity = 2 * SEND // along
    slots = along * capacity
    total, wide = rows + 2 * RIM, cols + LANES
    f32 = jnp.float32
    northward = [(i, i + 1) for i in range(along - 1)]
    southward = [(i + 1, i) for i in range(along - 1)]
    eastward = [(i, i + 1) for i in range(across - 1)]
    westward = [(i + 1, i) for i in range(across - 1)]

    payload = call(
        functools.partial(gather_body, capacity, slots),
        jax.ShapeDtypeStruct((slots, planes * cols + LANES), jnp.bfloat16),
        flops=2 * 8 * slots * SEND * planes * cols,
        moved=2 * (SEND + slots) * planes * cols,
    )(dest.reshape(1, SEND), pick.reshape(1, SEND), offset.reshape(1, SEND), parent_rows)
    arrived = lax.all_to_all(payload, "gy", split_axis=0, concat_axis=0, tiled=True)

    cells = state.reshape(planes, rows, cols)
    mask = wet.astype(f32)[None]
    to_north = jnp.concatenate([cells[:, rows - RIM :], mask[:, rows - RIM :]], axis=0)
    to_south = jnp.concatenate([cells[:, :RIM], mask[:, :RIM]], axis=0)
    from_south = lax.ppermute(to_north, "gy", northward)
    from_north = lax.ppermute(to_south, "gy", southward)
    ext, first, last = call(
        extend_body,
        (
            jax.ShapeDtypeStruct((planes + 1, total, cols), f32),
            jax.ShapeDtypeStruct((total, LANES), f32),
            jax.ShapeDtypeStruct((total, LANES), f32),
        ),
        moved=8 * planes * total * cols,
    )(cells, wet, from_north, from_south)
    from_west = lax.ppermute(last, "gx", eastward)
    from_east = lax.ppermute(first, "gx", westward)
    begun, ext_mask = call(
        first_body,
        (jax.ShapeDtypeStruct((planes, total, wide), f32), jax.ShapeDtypeStruct((total, wide), f32)),
        flops=20 * planes * total * wide,
        moved=8 * planes * total * wide,
        scratch_shapes=[pltpu.VMEM((planes, total, wide), f32)],
    )(ext, from_west, from_east)

    force, edge = call(
        functools.partial(landing_body, planes, cols),
        (jax.ShapeDtypeStruct((planes, rows, cols), f32), jax.ShapeDtypeStruct((rows, LANES), f32)),
        flops=2 * rows * slots * planes * cols,
        moved=2 * slots * planes * cols + 4 * rows * planes * cols,
    )(arrived)
    if across == 2:
        sides = [lax.ppermute(edge, "gx", [(0, 1), (1, 0)])]
    else:
        sides = [lax.ppermute(edge, "gx", eastward), lax.ppermute(edge, "gx", westward)]
    outer = jax.ShapeDtypeStruct((moving + 2, RIM, cols), f32)
    up, down = call(outer_body, (outer, outer), moved=16 * moving * RIM * cols)(force, edge, *sides)
    below = lax.ppermute(up, "gy", northward)
    above = lax.ppermute(down, "gy", southward)
    new_state, parts = call(
        functools.partial(steps_body, len(sides), along * across),
        (jax.ShapeDtypeStruct((planes, rows, cols), f32), jax.ShapeDtypeStruct((along * across, LANES), f32)),
        flops=60 * planes * total * wide,
        moved=8 * planes * total * wide,
        scratch_shapes=[
            pltpu.VMEM((moving, total, wide), f32),
            pltpu.VMEM((planes, total, wide), f32),
            pltpu.VMEM((planes, total, wide), f32),
        ],
    )(begun, ext_mask, force, edge, above, below, *sides)
    every = lax.all_to_all(parts, ("gy", "gx"), split_axis=0, concat_axis=0, tiled=True)
    me = lax.axis_index("gy").astype(jnp.int32).reshape(1)
    profile = call(
        functools.partial(profile_body, across, along),
        jax.ShapeDtypeStruct((3, rows), f32),
        in_specs=[pl.BlockSpec(memory_space=pltpu.SMEM), pl.BlockSpec(memory_space=pltpu.VMEM)],
    )(me, every)
    return new_state.reshape(state.shape), profile


def solution(mesh):
    in_specs = (
        P(None, None, "gy", "gx"),
        P(("gy", "gx"), None, None),
        P(("gy", "gx"), None),
        P(("gy", "gx")),
        P(("gy", "gx")),
        P("gy", "gx"),
    )
    out_specs = (P(None, None, "gy", "gx"), P(None, "gy"))
    return jax.shard_map(
        per_device, mesh=mesh, in_specs=in_specs, out_specs=out_specs, check_vma=False
    )
```

time: 162 us -> 83.3 us (0.51)
  blocking collectives: 46.1 us -> 0 us
  starting transfers between devices: 51.1 us -> 31.5 us
  other arithmetic: 13.4 us -> 0.06 us
  local copies, waits for them, and re-layouts: 13.5 us -> 3.14 us
  Pallas kernels: 0 us -> 8.54 us
  waiting for transfers between devices: 33.3 us -> 38.8 us
  matrix products: 2.32 us -> 0 us
    psum x2 -> x0, blocking collectives: 46.1 us -> none  [the longest x1 43.7 us: per_device(): squares = lax.psum(jnp.sum(summed * summed), 'gy')]
    ppermute x14 -> x7, starting transfers between devices: 39 us -> 14.6 us  [the longest x1 4.55 us: per_device(): from_south = lax.ppermute(to_north, 'gy', northward)]
    all_to_all x2, waiting for transfers between devices: 15 us -> 35.9 us  [the longest x1 28.7 us: per_device(): lax.all_to_all(payload, 'gy', split_axis=0, concat_axis=0, tiled=True)]
    ppermute x14 -> x7, waiting for transfers between devices: 18.3 us -> 2.96 us  [the longest x1 1.77 us: per_device(): from_east = lax.ppermute(first, 'gx', westward)]
    pallas_call x0 -> x7, Pallas kernels: none -> 8.54 us  [the longest x1 3.29 us: per_device(): call(functools.partial(steps_body, len(sides), along * across), (jax.Shap...]
    all_to_all x2, starting transfers between devices: 12 us -> 16.9 us  [the longest x1 8.5 us: per_device(): lax.all_to_all(parts, ('gy', 'gx'), split_axis=0, concat_axis=0, tiled=True)]
    concatenate x6 -> x2, other arithmetic: 3.87 us -> 0.05 us  [the longest x1 0.03 us: per_device(): to_south = jnp.concatenate([cells[:, :RIM], mask[:, :RIM]], axis=0)]
    mul x10 -> x0, other arithmetic: 3.14 us -> none  [the longest x3 2.14 us: advance(): tnew = (tnew + GAMMA * force[0]) * relax]
  transfers between devices with their start and end apart: 16 -> 9, of which waited for: 8 -> 4; matrix products, arithmetic and copies ran while one was open for 8% -> 0% of each run, Pallas kernels for 0% -> 3%
where the time goes in v1:
time: 83.3 us; the launch traced here: 82.9 us
  waiting for transfers between devices  38.8 us (47%)
  starting transfers between devices  31.5 us (38%)
  Pallas kernels  8.54 us (10%)
  local copies, waits for them, and re-layouts  3.14 us (4%)
    all_to_all x1, waiting for transfers between devices, per_device(): lax.all_to_all(payload, 'gy', split_axis=0, concat_axis=0, tiled=True)  28.7 us
    all_to_all x1, starting transfers between devices, per_device(): lax.all_to_all(parts, ('gy', 'gx'), split_axis=0, concat_axis=0, tiled=True)  8.5 us
    all_to_all x1, starting transfers between devices, per_device(): lax.all_to_all(payload, 'gy', split_axis=0, concat_axis=0, tiled=True)  8.44 us
    all_to_all x1, waiting for transfers between devices, per_device(): lax.all_to_all(parts, ('gy', 'gx'), split_axis=0, concat_axis=0, tiled=True)  7.14 us
    ppermute x1, starting transfers between devices, per_device(): from_south = lax.ppermute(to_north, 'gy', northward)  4.55 us
    ppermute x1, starting transfers between devices, per_device(): below = lax.ppermute(up, 'gy', northward)  4.55 us
    pallas_call x1, Pallas kernels, per_device(): call(functools.partial(steps_body, len(sides), along * across), (jax.Shap...  3.29 us
    unnamed x12, local copies, waits for them, and re-layouts  3.1 us
  transfers between devices with their start and end apart: 9, of which 4 were waited for; matrix products, arithmetic and copies ran while one was open for 0% of the time, Pallas kernels for 3%

profile of v1, /device:TPU:0, one launch (start us, length us, event | category | flops | bytes accessed | tf_op | source)
XLA Modules:
  0.0 82.9 jit_solution(6017636183286907297)
XLA Ops:
  0.6 0.0 copy-start.2
  0.6 1.1 %copy-done.2 = bf16[64,24,256]{2,1,0:T(8,128)(2,1)S(1)} copy-done((bf16[64,24,256]{2,1,0:T(8,128)(2,1)S(1)}, bf16[64,24,256]{2,1,0:T(8,128)(2,1)}, u32[]{:S(2)}) %copy-start.2) | copy-done | bytes 786456
  1.8 0.0 copy-start.3
  1.8 0.7 copy-done.3
  2.4 0.0 copy-start.4
  2.4 0.7 copy-done.4
  3.1 0.0 copy-start.5
  3.1 0.7 copy-done.5
  3.7 2.3 %shard_map.79 = bf16[128,6272]{1,0:T(8,128)(2,1)} custom-call(s32[1,64]{1,0:T(1,128)S(1)} %bitcast.18, s32[1,64]{1,0:T(1,128)S(1)} %bitcast.19, s32[1,64]{1,0:T(1,128)S(1)} %bitcast.20, bf16[64,24,256]{2,1,0:T(8,128)(2,1)S(1)} %copy-done.2), custom_call_target="tpu_custom_call" | custom-call | flops 805306368 | bytes 2359296 | tf_op jit(solution)/shard_map/pallas_call | solution.py:266
  6.1 0.0 copy-start.1
  6.1 0.0 copy-start
  6.1 8.4 %all-to-all-start = ((bf16[16,8,6272]{2,1,0:T(8,128)(2,1)}), bf16[16,8,6272]{2,1,0:T(8,128)(2,1)S(1)}, u32[]{:S(2)}, u32[]{:S(2)}) async-start(bf16[16,8,6272]{2,1,0:T(8,128)(2,1)} %bitcast.5), calls=%async_computation | async-start | bytes 3211264 | tf_op jit(solution)/shard_map/all_to_all | solution.py:272
  14.5 0.0 copy-done.1
  14.6 0.0 copy-done
  14.7 1.3 %collective-permute-start = (f32[25,4,256]{2,1,0:T(4,128)S(1)}, f32[25,4,256]{2,1,0:T(4,128)S(1)}, u32[]{:S(2)}, u32[]{:S(2)}) collective-permute-start(f32[25,4,256]{2,1,0:T(4,128)S(1)} %pad_maximum_fusion), channel_id=1, source_target_pairs={{2,0},{4,2},{6,4},{8,6},{10,8},{12,10},{14,12},{16,14},{18,16},{20... | collective-permute-start | bytes 307208 | tf_op jit(solution)/shard_map/ppermute | solution.py:279
  16.0 4.6 %collective-permute-start.1 = (f32[25,4,256]{2,1,0:T(4,128)S(1)}, f32[25,4,256]{2,1,0:T(4,128)S(1)}, u32[]{:S(2)}, u32[]{:S(2)}) collective-permute-start(f32[25,4,256]{2,1,0:T(4,128)S(1)} %pad_maximum_fusion.1), channel_id=1, source_target_pairs={{0,2},{2,4},{4,6},{6,8},{8,10},{10,12},{12,14},{14,16},{16,18},{18... | collective-permute-start | bytes 307208 | tf_op jit(solution)/shard_map/ppermute | solution.py:278
  20.5 28.7 %all-to-all-done = bf16[16,8,6272]{2,1,0:T(8,128)(2,1)S(1)} async-done(((bf16[16,8,6272]{2,1,0:T(8,128)(2,1)}), bf16[16,8,6272]{2,1,0:T(8,128)(2,1)S(1)}, u32[]{:S(2)}, u32[]{:S(2)}) %all-to-all-start) | async-done | bytes 1605664 | tf_op jit(solution)/shard_map/all_to_all | solution.py:272
  49.3 0.4 shard_map.80
  49.7 0.1 collective-permute-start.4
  49.8 1.2 %collective-permute-done.4.refs_0_ = f32[32,128]{1,0:T(8,128)S(1)} collective-permute-done((f32[32,128]{1,0:T(8,128)S(1)}, f32[32,128]{1,0:T(8,128)S(1)}, u32[]{:S(2)}, u32[]{:S(2)}) %collective-permute-start.4) | collective-permute-done | bytes 16416 | tf_op jit(solution)/shard_map/ppermute | solution.py:306
  50.9 1.3 %collective-permute-start.5 = (f32[18,4,256]{2,1,0:T(4,128)S(1)}, f32[18,4,256]{2,1,0:T(4,128)S(1)}, u32[]{:S(2)}, u32[]{:S(2)}) collective-permute-start(f32[18,4,256]{2,1,0:T(4,128)S(1)} %get-tuple-element.20), channel_id=1, source_target_pairs={{2,0},{4,2},{6,4},{8,6},{10,8},{12,10},{14,12},{16,14},{18,16},{20... | collective-permute-start | bytes 221192 | tf_op jit(solution)/shard_map/ppermute | solution.py:312
  52.2 4.5 %collective-permute-start.6 = (f32[18,4,256]{2,1,0:T(4,128)S(1)}, f32[18,4,256]{2,1,0:T(4,128)S(1)}, u32[]{:S(2)}, u32[]{:S(2)}) collective-permute-start(f32[18,4,256]{2,1,0:T(4,128)S(1)} %get-tuple-element.21), channel_id=1, source_target_pairs={{0,2},{2,4},{4,6},{6,8},{8,10},{10,12},{12,14},{14,16},{16,18},{18... | collective-permute-start | bytes 221192 | tf_op jit(solution)/shard_map/ppermute | solution.py:311
  56.8 0.0 collective-permute-done.north_ref
  56.8 0.0 collective-permute-done.1.south_ref
  56.8 0.3 shard_map.77
  57.2 1.5 %collective-permute-start.2 = (f32[40,128]{1,0:T(8,128)S(1)}, f32[40,128]{1,0:T(8,128)S(1)}, u32[]{:S(2)}, u32[]{:S(2)}) collective-permute-start(f32[40,128]{1,0:T(8,128)S(1)} %get-tuple-element.14), channel_id=1, source_target_pairs={{0,1},{2,3},{4,5},{6,7},{8,9},{10,11},{12,13},{14,15},{16,17},{18,... | collective-permute-start | bytes 61448 | tf_op jit(solution)/shard_map/ppermute | solution.py:289
  58.7 1.3 %collective-permute-start.3 = (f32[40,128]{1,0:T(8,128)S(1)}, f32[40,128]{1,0:T(8,128)S(1)}, u32[]{:S(2)}, u32[]{:S(2)}) collective-permute-start(f32[40,128]{1,0:T(8,128)S(1)} %get-tuple-element.15), channel_id=1, source_target_pairs={{1,0},{3,2},{5,4},{7,6},{9,8},{11,10},{13,12},{15,14},{17,16},{19,... | collective-permute-start | bytes 61448 | tf_op jit(solution)/shard_map/ppermute | solution.py:290
  60.0 0.0 collective-permute-done.2.west_ref
  60.0 1.8 %collective-permute-done.3.east_ref = f32[40,128]{1,0:T(8,128)S(1)} collective-permute-done((f32[40,128]{1,0:T(8,128)S(1)}, f32[40,128]{1,0:T(8,128)S(1)}, u32[]{:S(2)}, u32[]{:S(2)}) %collective-permute-start.3) | collective-permute-done | bytes 20512 | tf_op jit(solution)/shard_map/ppermute | solution.py:290
  61.8 1.4 %shard_map.78 = (f32[24,40,384]{2,1,0:T(8,128)S(1)}, f32[40,384]{1,0:T(8,128)S(1)}) custom-call(f32[25,40,256]{2,1,0:T(8,128)S(1)} %get-tuple-element.13.ext_ref, f32[40,128]{1,0:T(8,128)S(1)} %collective-permute-done.2.west_ref, f32[40,128]{1,0:T(8,128)S(1)} %collective-permute-done.3.east_ref), custom_call_target="tpu_custom_call" | custom-call | flops 7372800 | bytes 2949120 | tf_op jit(solution)/shard_map/pallas_call | solution.py:291
  63.1 0.0 collective-permute-done.5.north_ref
  63.1 0.0 collective-permute-done.6.south_ref
  63.1 3.3 %shard_map.82 = (f32[24,32,256]{2,1,0:T(8,128)}, f32[32,128]{1,0:T(8,128)}) custom-call(f32[24,40,384]{2,1,0:T(8,128)S(1)} %get-tuple-element.16.first_ref, f32[40,384]{1,0:T(8,128)S(1)} %get-tuple-element.17.mask_ref, f32[24,32,256]{2,1,0:T(8,128)S(1)} %get-tuple-element.18.force_ref, f32[32,128]{1,0:T(8,128)S(1)} %get-tuple-element.19.edge_ref, ...), custom_call_target="tpu_custom_call" | custom-call | flops 22118400 | bytes 2949120 | tf_op jit(solution)/shard_map/pallas_call | solution.py:313
  66.4 8.5 %all-to-all-start.1 = ((f32[32,1,128]{2,1,0:T(1,128)}), f32[32,1,128]{2,1,0:T(1,128)S(1)}, u32[]{:S(2)}, u32[]{:S(2)}) async-start(f32[32,1,128]{2,1,0:T(1,128)} %bitcast.10), calls=%async_computation.1 | async-start | bytes 32768 | tf_op jit(solution)/shard_map/all_to_all | solution.py:324
  75.0 7.1 %all-to-all-done.1 = f32[32,1,128]{2,1,0:T(1,128)S(1)} async-done(((f32[32,1,128]{2,1,0:T(1,128)}), f32[32,1,128]{2,1,0:T(1,128)S(1)}, u32[]{:S(2)}, u32[]{:S(2)}) %all-to-all-start.1) | async-done | bytes 16416 | tf_op jit(solution)/shard_map/all_to_all | solution.py:324
  82.1 0.8 shard_map.83
  (6 shorter events, 0.1 us)
Async XLA Ops:
  0.6 1.1 %copy-start.2 = (bf16[64,24,256]{2,1,0:T(8,128)(2,1)S(1)}, bf16[64,24,256]{2,1,0:T(8,128)(2,1)}, u32[]{:S(2)}) copy-start(bf16[64,24,256]{2,1,0:T(8,128)(2,1)} %rows_ref.1) | copy-start | bytes 2359300
  1.8 0.7 copy-start.3
  2.4 0.7 copy-start.4
  3.1 0.7 copy-start.5
  6.1 8.5 %copy-start.1 = (s32[32,256]{1,0:T(8,128)S(1)}, s32[32,256]{1,0:T(8,128)}, u32[]{:S(2)}) copy-start(s32[32,256]{1,0:T(8,128)} %wet_ref.1) | copy-start | bytes 98308
  6.1 8.5 %copy-start = (f32[3,8,32,256]{3,2,1,0:T(8,128)S(1)}, f32[3,8,32,256]{3,2,1,0:T(8,128)}, u32[]{:S(2)}) copy-start(f32[3,8,32,256]{3,2,1,0:T(8,128)} %param.6) | copy-start | bytes 2359300
  6.1 43.2 %all-to-all-start = ((bf16[16,8,6272]{2,1,0:T(8,128)(2,1)}), bf16[16,8,6272]{2,1,0:T(8,128)(2,1)S(1)}, u32[]{:S(2)}, u32[]{:S(2)}) async-start(bf16[16,8,6272]{2,1,0:T(8,128)(2,1)} %bitcast.5), calls=%async_computation | async-start | bytes 3211264 | tf_op jit(solution)/shard_map/all_to_all | solution.py:272
  14.7 42.2 %collective-permute-start = (f32[25,4,256]{2,1,0:T(4,128)S(1)}, f32[25,4,256]{2,1,0:T(4,128)S(1)}, u32[]{:S(2)}, u32[]{:S(2)}) collective-permute-start(f32[25,4,256]{2,1,0:T(4,128)S(1)} %pad_maximum_fusion), channel_id=1, source_target_pairs={{2,0},{4,2},{6,4},{8,6},{10,8},{12,10},{14,12},{16,14},{18,16},{20... | collective-permute-start | bytes 307208 | tf_op jit(solution)/shard_map/ppermute | solution.py:279
  16.0 40.8 %collective-permute-start.1 = (f32[25,4,256]{2,1,0:T(4,128)S(1)}, f32[25,4,256]{2,1,0:T(4,128)S(1)}, u32[]{:S(2)}, u32[]{:S(2)}) collective-permute-start(f32[25,4,256]{2,1,0:T(4,128)S(1)} %pad_maximum_fusion.1), channel_id=1, source_target_pairs={{0,2},{2,4},{4,6},{6,8},{8,10},{10,12},{12,14},{14,16},{16,18},{18... | collective-permute-start | bytes 307208 | tf_op jit(solution)/shard_map/ppermute | solution.py:278
  49.7 1.2 %collective-permute-start.4 = (f32[32,128]{1,0:T(8,128)S(1)}, f32[32,128]{1,0:T(8,128)S(1)}, u32[]{:S(2)}, u32[]{:S(2)}) collective-permute-start(f32[32,128]{1,0:T(8,128)S(1)} %get-tuple-element.19.edge_ref), channel_id=1, source_target_pairs={{0,1},{1,0},{2,3},{3,2},{4,5},{5,4},{6,7},{7,6},{8,9},{9,8},{10,11... | collective-permute-start | bytes 49160 | tf_op jit(solution)/shard_map/ppermute | solution.py:306
  50.9 12.2 %collective-permute-start.5 = (f32[18,4,256]{2,1,0:T(4,128)S(1)}, f32[18,4,256]{2,1,0:T(4,128)S(1)}, u32[]{:S(2)}, u32[]{:S(2)}) collective-permute-start(f32[18,4,256]{2,1,0:T(4,128)S(1)} %get-tuple-element.20), channel_id=1, source_target_pairs={{2,0},{4,2},{6,4},{8,6},{10,8},{12,10},{14,12},{16,14},{18,16},{20... | collective-permute-start | bytes 221192 | tf_op jit(solution)/shard_map/ppermute | solution.py:312
  52.2 10.9 %collective-permute-start.6 = (f32[18,4,256]{2,1,0:T(4,128)S(1)}, f32[18,4,256]{2,1,0:T(4,128)S(1)}, u32[]{:S(2)}, u32[]{:S(2)}) collective-permute-start(f32[18,4,256]{2,1,0:T(4,128)S(1)} %get-tuple-element.21), channel_id=1, source_target_pairs={{0,2},{2,4},{4,6},{6,8},{8,10},{10,12},{12,14},{14,16},{16,18},{18... | collective-permute-start | bytes 221192 | tf_op jit(solution)/shard_map/ppermute | solution.py:311
  57.2 2.8 %collective-permute-start.2 = (f32[40,128]{1,0:T(8,128)S(1)}, f32[40,128]{1,0:T(8,128)S(1)}, u32[]{:S(2)}, u32[]{:S(2)}) collective-permute-start(f32[40,128]{1,0:T(8,128)S(1)} %get-tuple-element.14), channel_id=1, source_target_pairs={{0,1},{2,3},{4,5},{6,7},{8,9},{10,11},{12,13},{14,15},{16,17},{18,... | collective-permute-start | bytes 61448 | tf_op jit(solution)/shard_map/ppermute | solution.py:289
  58.7 3.1 %collective-permute-start.3 = (f32[40,128]{1,0:T(8,128)S(1)}, f32[40,128]{1,0:T(8,128)S(1)}, u32[]{:S(2)}, u32[]{:S(2)}) collective-permute-start(f32[40,128]{1,0:T(8,128)S(1)} %get-tuple-element.15), channel_id=1, source_target_pairs={{1,0},{3,2},{5,4},{7,6},{9,8},{11,10},{13,12},{15,14},{17,16},{19,... | collective-permute-start | bytes 61448 | tf_op jit(solution)/shard_map/ppermute | solution.py:290
  66.4 15.7 %all-to-all-start.1 = ((f32[32,1,128]{2,1,0:T(1,128)}), f32[32,1,128]{2,1,0:T(1,128)S(1)}, u32[]{:S(2)}, u32[]{:S(2)}) async-start(f32[32,1,128]{2,1,0:T(1,128)} %bitcast.10), calls=%async_computation.1 | async-start | bytes 32768 | tf_op jit(solution)/shard_map/all_to_all | solution.py:324

commit v2 on v1

v2 whole, which is shorter than its diff:
```python
import functools

import jax
import jax.numpy as jnp
from jax import lax
from jax.experimental import pallas as pl
from jax.experimental.pallas import tpu as pltpu
from jax.sharding import PartitionSpec as P

SEND = 64
STEPS = 3

KH = 0.2
KZ = 0.05
ADV = 0.25
PG = 0.5
GAMMA = 0.5
DISPERSE = 2.0

EDGE = 3
RIM = 4
LANES = 128
STATE_SCALE = 8192.0
FORCE_SCALE = 64.0
VMEM_LIMIT = 16 * 1024 * 1024
VMEM_MOST = 60 * 1024 * 1024


def call(body, out_shape, flops=0, moved=0, limit=VMEM_LIMIT, **more):
    return pl.pallas_call(
        body,
        out_shape=out_shape,
        compiler_params=pltpu.CompilerParams(vmem_limit_bytes=limit),
        cost_estimate=pl.CostEstimate(flops=flops, bytes_accessed=moved, transcendentals=0),
        **more,
    )


def iota(shape, dim):
    return lax.broadcasted_iota(jnp.int32, shape, dim)


def gather_body(capacity, slots, *refs):
    sources, out_ref, targets, held_ref, copied, sent = refs[:4], refs[4], refs[5:9], refs[9], refs[10], refs[11]
    copies = [
        pltpu.make_async_copy(source, target, copied.at[k]) for k, (source, target) in enumerate(zip(sources, targets))
    ]
    for copy in copies:
        copy.start()
    dest_ref, pick_ref, offset_ref, rows_ref = targets
    send, planes, cols = rows_ref.shape
    for copy in copies[:3]:
        copy.wait()
    dest = dest_ref[...]
    eye = iota((send, send), 0) == iota((send, send), 1)
    dest_column = jnp.sum(jnp.where(eye, dest, 0), axis=1, keepdims=True)
    earlier = (dest_column == dest) & (iota((send, send), 0) < iota((send, send), 1))
    rank = jnp.sum(earlier.astype(jnp.int32), axis=0, keepdims=True)
    slot_of = dest * capacity + rank
    taken = iota((slots, send), 0) == slot_of
    source = jnp.sum(jnp.where(taken, pick_ref[...] + 1, 0), axis=1, keepdims=True) - 1
    label = jnp.sum(jnp.where(taken, offset_ref[...] + 1, 0), axis=1, keepdims=True)
    group = 8
    lane = iota((slots, send * group), 1)
    select = jnp.concatenate(
        [(lane == source * group + j).astype(jnp.float32).astype(jnp.bfloat16) for j in range(group)], axis=0
    )
    width = planes * cols
    held_ref[:, width:] = jnp.broadcast_to(label, (slots, LANES)).astype(jnp.float32).astype(jnp.bfloat16)
    copies[3].wait()
    parts = []

    def send_columns(start, size):
        part = pltpu.make_async_copy(
            held_ref.at[:, pl.ds(start, size)], out_ref.at[:, pl.ds(start, size)], sent.at[len(parts)]
        )
        part.start()
        parts.append(part)

    send_columns(width, LANES)
    for g in range(planes // group):
        block = rows_ref[:, g * group : (g + 1) * group, :].reshape(send * group, cols)
        got = jnp.dot(select, block, preferred_element_type=jnp.float32).astype(jnp.bfloat16)
        for j in range(group):
            at = (g * group + j) * cols
            held_ref[:, at : at + cols] = got[j * slots : (j + 1) * slots]
        send_columns(g * group * cols, group * cols)
    for part in parts:
        part.wait()


def landing_body(planes, cols, token_ref, arrived_ref, force_ref, edge_ref):
    slots = arrived_ref.shape[0]
    rows = force_ref.shape[1]
    width = planes * cols
    label = arrived_ref[:, width:].astype(jnp.float32)
    landing = (label == (iota((slots, LANES), 1) + 1).astype(jnp.float32)).astype(jnp.float32)
    landing = landing.T[:rows].astype(jnp.bfloat16)
    count = jnp.dot(landing, jnp.ones((slots, LANES), jnp.bfloat16), preferred_element_type=jnp.float32)
    moving = 2 * planes // 3
    edge = count
    for j in range(planes):
        force = jnp.dot(landing, arrived_ref[:, j * cols : (j + 1) * cols], preferred_element_type=jnp.float32)
        force_ref[j] = force
        if j < moving:
            edge = packed(edge, force[:, :LANES], 0, EDGE * j)
            edge = packed(edge, force[:, cols - LANES :], LANES - EDGE, EDGE * (moving + j))
    edge_ref[...] = edge


def packed(into, tile, start, at):
    lane = iota(tile.shape, 1)
    shifted = pltpu.roll(tile, (at - start) % LANES, 1)
    return jnp.where((lane >= at) & (lane < at + EDGE), shifted, into)


def sides_body(state_ref, wet_ref, first_ref, last_ref):
    planes, rows, cols = state_ref.shape
    first = jnp.zeros((rows, LANES), jnp.float32)
    last = jnp.zeros((rows, LANES), jnp.float32)
    for j in range(planes + 1):
        own = state_ref[j] if j < planes else wet_ref[...].astype(jnp.float32)
        first = packed(first, own[:, :LANES], 0, EDGE * j)
        last = packed(last, own[:, cols - LANES :], LANES - EDGE, EDGE * j)
    first_ref[...] = first
    last_ref[...] = last


def side_tile(west, west_at, east, east_at):
    lane = iota(west.shape, 1)
    right = pltpu.roll(east, (LANES - east_at) % LANES, 1)
    left = pltpu.roll(west, (2 * LANES - EDGE - west_at) % LANES, 1)
    return jnp.where(lane < EDGE, right, jnp.where(lane >= LANES - EDGE, left, 0.0))


def around(field):
    rows, cols = field.shape
    return (
        pltpu.roll(field, cols - 1, 1),
        pltpu.roll(field, 1, 1),
        pltpu.roll(field, rows - 1, 0),
        pltpu.roll(field, 1, 0),
    )


def around_between(field, north_row, south_row):
    east, west, north, south = around(field)
    row = iota(field.shape, 0)
    return east, west, jnp.where(row == field.shape[0] - 1, north_row, north), jnp.where(row == 0, south_row, south)


def moved(load, near, levels, z):
    upper, lower = min(z + 1, levels - 1), max(z - 1, 0)
    results = []
    fields = [load(f * levels + z) for f in range(3)]
    tracer, across, along = fields
    around_tracer = near(z, tracer)
    east, west, north, south = around_tracer
    ddx, ddy = 0.5 * (east - west), 0.5 * (north - south)
    extra = (ADV * (across * ddx + along * ddy), PG * ddx, PG * ddy)
    for f, centre in enumerate(fields):
        sides = around_tracer if f == 0 else near(f * levels + z, centre)
        lap = (sides[0] + sides[1]) + (sides[2] + sides[3]) - 4.0 * centre
        lapz = load(f * levels + upper) + load(f * levels + lower) - 2.0 * centre
        results.append(centre + KH * lap + KZ * lapz - extra[f])
    return results


def added(sign, along, tracer, across_near, along_near):
    return [
        (KH - sign * 0.5 * ADV * along) * tracer,
        KH * across_near,
        KH * along_near - sign * 0.5 * PG * tracer,
    ]


def begin_body(state_ref, wet_ref, west_ref, east_ref, full_ref, mask_ref, begun_ref, token_ref):
    planes, rows, cols = state_ref.shape
    levels = planes // 3
    west, east = west_ref[...], east_ref[...]
    for j in range(planes):
        full_ref[j, :, :cols] = state_ref[j]
        full_ref[j, :, cols:] = side_tile(west, EDGE * j, east, EDGE * j)
    mask_ref[:, :cols] = wet_ref[...].astype(jnp.float32)
    mask_ref[:, cols:] = side_tile(west, EDGE * planes, east, EDGE * planes)
    for z in range(levels):
        values = moved(lambda j: full_ref[j], lambda j, field: around_between(field, 0.0, 0.0), levels, z)
        for f, value in enumerate(values):
            begun_ref[f * levels + z] = value
    token_ref[...] = jnp.zeros_like(token_ref)


def outer_body(force_ref, edge_ref, state_ref, wet_ref, west_ref, east_ref, *refs):
    sides, (up_ref, down_ref) = refs[:-2], refs[-2:]
    planes, rows, cols = state_ref.shape
    moving = 2 * planes // 3
    ends = ((up_ref, slice(rows - RIM, rows)), (down_ref, slice(0, RIM)))
    for out_ref, at in ends:
        out_ref[:moving] = force_ref[:moving, at] * FORCE_SCALE
        out_ref[moving : moving + planes] = state_ref[:, at] * STATE_SCALE
        out_ref[moving + planes] = wet_ref[at].astype(jnp.float32) * STATE_SCALE
        parts = [west_ref[at], east_ref[at], edge_ref[at]] + [side[at] for side in sides]
        for k, part in enumerate(parts):
            lane = (k % 2) * LANES
            out_ref[moving + planes + 1 + k // 2, :, lane : lane + LANES] = part * (STATE_SCALE if k < 2 else FORCE_SCALE)


def steps_body(sides, devices, full_ref, mask_ref, begun_ref, force_ref, edge_ref, north_ref, south_ref, *refs):
    side_refs = refs[:sides]
    state_ref, parts_ref, push_ref, halo_ref, one_ref, two_ref = refs[sides:]
    planes, rows, wide = full_ref.shape
    levels = planes // 3
    cols = wide - LANES
    total = rows + 2 * RIM
    moving = 2 * levels
    last = rows - 2 * RIM

    def joined(index):
        both = jnp.concatenate([north_ref[index], south_ref[index]], axis=0)
        if index > moving + planes:
            return both
        return both * (1.0 / (FORCE_SCALE if index < moving else STATE_SCALE))

    pairs = [joined(moving + planes + 1 + k) for k in range((sides + 4) // 2)]
    outer = [
        pairs[k // 2][:, (k % 2) * LANES : (k % 2 + 1) * LANES] * (1.0 / (STATE_SCALE if k < 2 else FORCE_SCALE))
        for k in range(3 + sides)
    ]
    edges = [jnp.concatenate([side[...], outer[3 + k]], axis=0) for k, side in enumerate(side_refs)]
    west, east = edges[0], edges[-1]
    own = jnp.concatenate([edge_ref[...], outer[2]], axis=0)

    def counts(edge):
        return jnp.broadcast_to(edge[:, LANES - 1 :], (total, LANES))

    lane = iota((total, LANES), 1)
    count_side = jnp.where(lane < LANES // 2, counts(east), counts(west))
    count = jnp.concatenate([counts(own)] * (cols // LANES) + [count_side], axis=1)

    def halo(index, at):
        return jnp.concatenate([joined(index), side_tile(outer[0], at, outer[1], at)], axis=1)

    mask = jnp.concatenate([mask_ref[...], halo(moving + planes, EDGE * planes)], axis=0)
    relax = mask / (1.0 + GAMMA * count)
    half = GAMMA * relax

    for j in range(moving):
        tile = side_tile(west, EDGE * (moving + j), east, EDGE * j)
        whole = jnp.concatenate([force_ref[j], joined(j)], axis=0)
        push_ref[j, :, :cols] = whole * half[:, :cols]
        push_ref[j, :, cols:] = tile * half[:, cols:]
    for j in range(planes):
        halo_ref[j] = halo(moving + j, EDGE * j)

    def finish(values, z, at=(slice(None),)):
        tracer, across, along = values
        rated = relax[at]
        return (tracer * rated + push_ref[(z, *at)], across * rated, along * rated + push_ref[(levels + z, *at)])

    row = iota((2 * RIM, wide), 0)
    head, tail = slice(0, 2 * RIM), slice(last, rows)

    def near(j, field):
        return around_between(field, full_ref[j, :1], full_ref[j, rows - 1 :])

    for z in range(levels):
        index = [f * levels + z for f in range(3)]
        beyond = [halo_ref[j] for j in index]
        north = [jnp.where(row == 2 * RIM - 1, value[:1], 0.0) for value in beyond]
        south = [jnp.where(row == 0, value[2 * RIM - 1 :], 0.0) for value in beyond]
        first = added(-1.0, full_ref[index[2], head], *south)
        final = added(1.0, full_ref[index[2], tail], *north)
        blocks = (
            (head, [begun_ref[j, head] + extra for j, extra in zip(index, first)]),
            (slice(2 * RIM, last), [begun_ref[j, 2 * RIM : last] for j in index]),
            (tail, [begun_ref[j, tail] + extra for j, extra in zip(index, final)]),
            (slice(rows, total), moved(lambda j: halo_ref[j], near, levels, z)),
        )
        for at, values in blocks:
            for j, value in zip(index, finish(values, z, (at,))):
                one_ref[j, at] = value

    for z in range(levels):
        for f, value in enumerate(finish(moved(lambda j: one_ref[j], lambda j, field: around(field), levels, z), z)):
            two_ref[f * levels + z] = value
    share = 1.0 / (1.0 + count[:rows, :1])
    sums = [jnp.zeros((rows, cols), jnp.float32) for _ in range(3)]
    own_cols = (slice(None), slice(0, cols))
    for z in range(levels):
        values = moved(
            lambda j: two_ref[j, :, :cols],
            lambda j, field: tuple(side[:, :cols] for side in around(two_ref[j])),
            levels,
            z,
        )
        values = finish(values, z, own_cols)
        for f, value in enumerate(values):
            state_ref[f * levels + z] = value[:rows]
        tracer = values[0]
        inner = tracer[:rows]
        ddy = pltpu.roll(tracer, total - 1, 0)[:rows] - pltpu.roll(tracer, 1, 0)[:rows]
        sums[0] = sums[0] + values[2][:rows] * inner
        sums[1] = sums[1] + force_ref[moving + z] * inner
        sums[2] = sums[2] + ddy
    raw = [jnp.sum(value, axis=1, keepdims=True) for value in sums]
    raw = [raw[0], raw[1] * share, raw[2] * (-0.5 * DISPERSE)]
    row, lane = iota((rows, LANES), 0), iota((rows, LANES), 1)
    part = jnp.zeros((rows, LANES), jnp.float32)
    for q in range(3):
        part = part + jnp.where(lane == q * rows + row, raw[q], 0.0)
    part = jnp.sum(part, axis=0, keepdims=True)
    parts_ref[...] = jnp.broadcast_to(part, (devices, LANES))


def profile_body(across, along, me_ref, parts_ref, out_ref):
    rows = out_ref.shape[1]
    parts = parts_ref[...]
    devices = parts.shape[0]
    total = parts
    for k in range(1, across):
        total = total + pltpu.roll(parts, devices - k, 0)
    row = iota(parts.shape, 0)
    squares = jnp.sum(jnp.where(row % across == 0, total * total, 0.0), keepdims=True)
    scale = jnp.sqrt(squares / (3 * rows * along) + 1e-06)
    mine = jnp.sum(jnp.where(row == me_ref[0] * across, total, 0.0), axis=0, keepdims=True) / scale
    for q in range(3):
        out_ref[q : q + 1, :] = mine[:, q * rows : (q + 1) * rows]


def per_device(state, parent_rows, dest, pick, offset, wet):
    fields, levels, rows, cols = state.shape
    planes = fields * levels
    moving = 2 * levels
    along, across = lax.axis_size("gy"), lax.axis_size("gx")
    capacity = 2 * SEND // along
    slots = along * capacity
    total, wide = rows + 2 * RIM, cols + LANES
    f32 = jnp.float32
    even_pairs = [(i, i ^ 1) for i in range(along)]
    odd_pairs = [(i, ((i + 1) ^ 1) - 1) for i in range(1, along - 1)]
    eastward = [(i, i + 1) for i in range(across - 1)]
    westward = [(i + 1, i) for i in range(across - 1)]

    payload = call(
        functools.partial(gather_body, capacity, slots),
        jax.ShapeDtypeStruct((slots, planes * cols + LANES), jnp.bfloat16),
        flops=2 * 8 * slots * SEND * planes * cols,
        moved=2 * (SEND + slots) * planes * cols,
        limit=VMEM_MOST,
        in_specs=[pl.BlockSpec(memory_space=pl.ANY)] * 4,
        out_specs=pl.BlockSpec(memory_space=pl.ANY),
        scratch_shapes=[pltpu.VMEM((1, SEND), jnp.int32)] * 3
        + [
            pltpu.VMEM(parent_rows.shape, jnp.bfloat16),
            pltpu.VMEM((slots, planes * cols + LANES), jnp.bfloat16),
            pltpu.SemaphoreType.DMA((4,)),
            pltpu.SemaphoreType.DMA((4,)),
        ],
    )(dest.reshape(1, SEND), pick.reshape(1, SEND), offset.reshape(1, SEND), parent_rows)
    arrived = lax.all_to_all(payload, "gy", split_axis=0, concat_axis=0, tiled=True)

    cells = state.reshape(planes, rows, cols)
    packed_side = jax.ShapeDtypeStruct((rows, LANES), f32)
    first, last = call(sides_body, (packed_side, packed_side), moved=4 * planes * rows * cols)(cells, wet)
    from_west = lax.ppermute(last, "gx", eastward)
    from_east = lax.ppermute(first, "gx", westward)
    own_wide = jax.ShapeDtypeStruct((planes, rows, wide), f32)
    full, mask, begun, token = call(
        begin_body,
        (own_wide, jax.ShapeDtypeStruct((rows, wide), f32), own_wide, jax.ShapeDtypeStruct((8, LANES), f32)),
        flops=20 * planes * rows * wide,
        moved=12 * planes * rows * wide,
    )(cells, wet, from_west, from_east)

    force, edge = call(
        functools.partial(landing_body, planes, cols),
        (jax.ShapeDtypeStruct((planes, rows, cols), f32), packed_side),
        flops=2 * rows * slots * planes * cols,
        moved=2 * slots * planes * cols + 4 * rows * planes * cols,
    )(token, arrived)
    if across == 2:
        sides = [lax.ppermute(edge, "gx", [(0, 1), (1, 0)])]
    else:
        sides = [lax.ppermute(edge, "gx", eastward), lax.ppermute(edge, "gx", westward)]
    outer = jax.ShapeDtypeStruct((moving + planes + 1 + (len(sides) + 4) // 2, RIM, cols), f32)
    up, down = call(outer_body, (outer, outer), moved=16 * (moving + planes) * RIM * cols)(
        force, edge, cells, wet, from_west, from_east, *sides
    )
    even = lax.axis_index("gy") % 2 == 0
    far = lax.ppermute(jnp.where(even, down, up).astype(jnp.float16), "gy", odd_pairs).astype(f32)
    near = lax.ppermute(jnp.where(even, up, down).astype(jnp.float16), "gy", even_pairs).astype(f32)
    above, below = jnp.where(even, near, far), jnp.where(even, far, near)
    new_state, parts = call(
        functools.partial(steps_body, len(sides), along * across),
        (jax.ShapeDtypeStruct((planes, rows, cols), f32), jax.ShapeDtypeStruct((along * across, LANES), f32)),
        flops=60 * planes * total * wide,
        moved=8 * planes * total * wide,
        scratch_shapes=[
            pltpu.VMEM((moving, total, wide), f32),
            pltpu.VMEM((planes, 2 * RIM, wide), f32),
            pltpu.VMEM((planes, total, wide), f32),
            pltpu.VMEM((planes, total, wide), f32),
        ],
    )(full, mask, begun, force, edge, above, below, *sides)
    every = lax.all_to_all(parts, ("gy", "gx"), split_axis=0, concat_axis=0, tiled=True)
    me = lax.axis_index("gy").astype(jnp.int32).reshape(1)
    profile = call(
        functools.partial(profile_body, across, along),
        jax.ShapeDtypeStruct((3, rows), f32),
        in_specs=[pl.BlockSpec(memory_space=pltpu.SMEM), pl.BlockSpec(memory_space=pltpu.VMEM)],
    )(me, every)
    return new_state.reshape(state.shape), profile


def solution(mesh):
    in_specs = (
        P(None, None, "gy", "gx"),
        P(("gy", "gx"), None, None),
        P(("gy", "gx"), None),
        P(("gy", "gx")),
        P(("gy", "gx")),
        P("gy", "gx"),
    )
    out_specs = (P(None, None, "gy", "gx"), P(None, "gy"))
    return jax.shard_map(
        per_device, mesh=mesh, in_specs=in_specs, out_specs=out_specs, check_vma=False
    )
```

time: 83.3 us -> 76.8 us (0.922)
  starting transfers between devices: 31.5 us -> 13 us
  blocking collectives: 0 us -> 18.3 us
  waiting for transfers between devices: 38.8 us -> 32.7 us
  local copies, waits for them, and re-layouts: 3.14 us -> 2.06 us
  Pallas kernels: 8.54 us -> 9.6 us
    all_to_all x0 -> x1, blocking collectives: none -> 18.3 us  [per_device(): lax.all_to_all(parts, ('gy', 'gx'), split_axis=0, concat_axis=0, tiled=True)]
    ppermute x4 -> x2, starting transfers between devices: 11.7 us -> 1.66 us  [the longest x1 1 us: per_device(): lax.ppermute(jnp.where(even, up, down).astype(jnp.float16), 'gy', even_pa...]
    all_to_all x1 -> x0, starting transfers between devices: 8.5 us -> none  [per_device(): lax.all_to_all(parts, ('gy', 'gx'), split_axis=0, concat_axis=0, tiled=True)]
    all_to_all x1 -> x0, waiting for transfers between devices: 7.14 us -> none  [per_device(): lax.all_to_all(parts, ('gy', 'gx'), split_axis=0, concat_axis=0, tiled=True)]
    ppermute x4 -> x2, waiting for transfers between devices: 0.01 us -> 3.05 us  [the longest x1 3.05 us: per_device(): lax.ppermute(jnp.where(even, up, down).astype(jnp.float16), 'gy', even_pa...]
    all_to_all x1, waiting for transfers between devices: 28.7 us -> 26.7 us  [per_device(): lax.all_to_all(payload, 'gy', split_axis=0, concat_axis=0, tiled=True)]
    unnamed x12, local copies, waits for them, and re-layouts: 3.1 us -> 2.06 us
    pallas_call x1, Pallas kernels: 2.34 us -> 3.23 us  [per_device(): call(functools.partial(gather_body, capacity, slots), jax.ShapeDtypeStruc...]
  transfers between devices with their start and end apart: 9 -> 6, of which waited for: 4 -> 4; matrix products, arithmetic and copies ran while one was open for 0% -> 0% of each run, Pallas kernels for 3% -> 2%
where the time goes in v2:
time: 76.8 us; the launch traced here: 76.5 us
  waiting for transfers between devices  32.7 us (43%)
  blocking collectives  18.3 us (24%)
  starting transfers between devices  13 us (17%)
  Pallas kernels  9.6 us (12%)
  local copies, waits for them, and re-layouts  2.06 us (3%)
  between operations  0.81 us (1%)
    all_to_all x1, waiting for transfers between devices, per_device(): lax.all_to_all(payload, 'gy', split_axis=0, concat_axis=0, tiled=True)  26.7 us
    all_to_all x1, blocking collectives, per_device(): lax.all_to_all(parts, ('gy', 'gx'), split_axis=0, concat_axis=0, tiled=True)  18.3 us
    all_to_all x1, starting transfers between devices, per_device(): lax.all_to_all(payload, 'gy', split_axis=0, concat_axis=0, tiled=True)  8.46 us
    pallas_call x1, Pallas kernels, per_device(): call(functools.partial(steps_body, len(sides), along * across), (jax.Shap...  3.74 us
    pallas_call x1, Pallas kernels, per_device(): call(functools.partial(gather_body, capacity, slots), jax.ShapeDtypeStruc...  3.23 us
    ppermute x1, waiting for transfers between devices, per_device(): lax.ppermute(jnp.where(even, up, down).astype(jnp.float16), 'gy', even_pa...  3.05 us
    unnamed x12, local copies, waits for them, and re-layouts  2.06 us
    ppermute x1, waiting for transfers between devices, per_device(): from_east = lax.ppermute(first, 'gx', westward)  1.77 us
  transfers between devices with their start and end apart: 6, of which 4 were waited for; matrix products, arithmetic and copies ran while one was open for 0% of the time, Pallas kernels for 2%

profile of v2, /device:TPU:0, one launch (start us, length us, event | category | flops | bytes accessed | tf_op | source)
XLA Modules:
  0.0 76.5 jit_solution(11197626462122605337)
XLA Ops:
  0.6 3.2 %shard_map.79 = bf16[128,6272]{1,0:T(8,128)(2,1)} custom-call(s32[1,64]{1,0:T(1,128)} %bitcast.20, s32[1,64]{1,0:T(1,128)} %bitcast.21, s32[1,64]{1,0:T(1,128)} %bitcast.22, bf16[64,24,256]{2,1,0:T(8,128)(2,1)} %refs_3_.1), custom_call_target="tpu_custom_call" | custom-call | flops 805306368 | bytes 2359296 | tf_op jit(solution)/shard_map/pallas_call | solution.py:344
  3.9 0.0 copy-start
  3.9 0.0 copy-start.5
  3.9 8.5 %all-to-all-start = ((bf16[16,8,6272]{2,1,0:T(8,128)(2,1)}), bf16[16,8,6272]{2,1,0:T(8,128)(2,1)S(1)}, u32[]{:S(2)}, u32[]{:S(2)}) async-start(bf16[16,8,6272]{2,1,0:T(8,128)(2,1)} %bitcast.18), calls=%async_computation | async-start | bytes 3211264 | tf_op jit(solution)/shard_map/all_to_all | solution.py:360
  12.4 0.0 copy-done
  12.4 0.0 copy-done.5
  12.4 0.3 shard_map.77
  12.7 1.5 %collective-permute-start = (f32[32,128]{1,0:T(8,128)S(1)}, f32[32,128]{1,0:T(8,128)S(1)}, u32[]{:S(2)}, u32[]{:S(2)}) collective-permute-start(f32[32,128]{1,0:T(8,128)S(1)} %get-tuple-element.14), channel_id=1, source_target_pairs={{0,1},{2,3},{4,5},{6,7},{8,9},{10,11},{12,13},{14,15},{16,17},{18,... | collective-permute-start | bytes 49160 | tf_op jit(solution)/shard_map/ppermute | solution.py:365
  14.1 1.3 %collective-permute-start.1 = (f32[32,128]{1,0:T(8,128)S(1)}, f32[32,128]{1,0:T(8,128)S(1)}, u32[]{:S(2)}, u32[]{:S(2)}) collective-permute-start(f32[32,128]{1,0:T(8,128)S(1)} %get-tuple-element.15), channel_id=1, source_target_pairs={{1,0},{3,2},{5,4},{7,6},{9,8},{11,10},{13,12},{15,14},{17,16},{19,... | collective-permute-start | bytes 49160 | tf_op jit(solution)/shard_map/ppermute | solution.py:366
  15.4 0.0 collective-permute-done.west_ref
  15.5 1.8 %collective-permute-done.1.east_ref = f32[32,128]{1,0:T(8,128)S(1)} collective-permute-done((f32[32,128]{1,0:T(8,128)S(1)}, f32[32,128]{1,0:T(8,128)S(1)}, u32[]{:S(2)}, u32[]{:S(2)}) %collective-permute-start.1) | collective-permute-done | bytes 16416 | tf_op jit(solution)/shard_map/ppermute | solution.py:366
  17.2 1.1 %shard_map.78 = (f32[24,32,384]{2,1,0:T(8,128)S(1)}, f32[32,384]{1,0:T(8,128)S(1)}, f32[24,32,384]{2,1,0:T(8,128)S(1)}, f32[8,128]{1,0:T(8,128)S(1)}) custom-call(f32[24,32,256]{2,1,0:T(8,128)S(1)} %bitcast.13, s32[32,256]{1,0:T(8,128)S(1)} %copy-done.5, f32[32,128]{1,0:T(8,128)S(1)} %collective-permute-done.west_ref, ...), custom_call_target="tpu_custom_call" | custom-call | flops 5898240 | bytes 3538944 | tf_op jit(solution)/shard_map/pallas_call | solution.py:368
  18.3 0.0 copy-start.1
  18.3 1.0 %copy-done.1 = f32[24,32,384]{2,1,0:T(8,128)} copy-done((f32[24,32,384]{2,1,0:T(8,128)}, f32[24,32,384]{2,1,0:T(8,128)S(1)}, u32[]{:S(2)}) %copy-start.1) | copy-done | bytes 1179672
  19.4 0.0 copy-start.3
  19.4 1.0 %copy-done.3 = f32[24,32,384]{2,1,0:T(8,128)} copy-done((f32[24,32,384]{2,1,0:T(8,128)}, f32[24,32,384]{2,1,0:T(8,128)S(1)}, u32[]{:S(2)}) %copy-start.3) | copy-done | bytes 1179672
  20.4 26.7 %all-to-all-done = bf16[16,8,6272]{2,1,0:T(8,128)(2,1)S(1)} async-done(((bf16[16,8,6272]{2,1,0:T(8,128)(2,1)}), bf16[16,8,6272]{2,1,0:T(8,128)(2,1)S(1)}, u32[]{:S(2)}, u32[]{:S(2)}) %all-to-all-start) | async-done | bytes 1605664 | tf_op jit(solution)/shard_map/all_to_all | solution.py:360
  47.1 0.4 shard_map.80
  47.5 0.0 copy-start.2
  47.5 0.1 collective-permute-start.2
  47.6 0.0 copy-start.4
  47.6 1.1 %collective-permute-done.2.refs_0_ = f32[32,128]{1,0:T(8,128)S(1)} collective-permute-done((f32[32,128]{1,0:T(8,128)S(1)}, f32[32,128]{1,0:T(8,128)S(1)}, u32[]{:S(2)}, u32[]{:S(2)}) %collective-permute-start.2) | collective-permute-done | bytes 16416 | tf_op jit(solution)/shard_map/ppermute | solution.py:382
  48.8 0.1 shard_map.81
  48.9 0.1 select_convert_fusion.1
  48.9 1.0 %collective-permute-start.3 = (f16[43,4,256]{2,1,0:T(4,128)(2,1)S(1)}, f16[43,4,256]{2,1,0:T(4,128)(2,1)S(1)}, u32[]{:S(2)}, u32[]{:S(2)}) collective-permute-start(f16[43,4,256]{2,1,0:T(4,128)(2,1)S(1)} %get-tuple-element.26), channel_id=1, source_target_pairs={{0,2},{2,0},{4,6},{6,4},{8,10},{10,8},{12,14},{14,12},{16,18},{18,... | collective-permute-start | bytes 264200 | tf_op jit(solution)/shard_map/ppermute | solution.py:391
  49.9 0.7 collective-permute-start.4
  50.6 3.0 %collective-permute-done.3 = f16[43,4,256]{2,1,0:T(4,128)(2,1)S(1)} collective-permute-done((f16[43,4,256]{2,1,0:T(4,128)(2,1)S(1)}, f16[43,4,256]{2,1,0:T(4,128)(2,1)S(1)}, u32[]{:S(2)}, u32[]{:S(2)}) %collective-permute-start.3) | collective-permute-done | bytes 88096 | tf_op jit(solution)/shard_map/ppermute | solution.py:391
  53.6 0.0 collective-permute-done.4
  53.6 0.1 convert_select_fusion
  53.7 0.0 copy-done.2
  53.7 0.0 copy-done.4
  53.7 3.7 %shard_map.82 = (f32[24,32,256]{2,1,0:T(8,128)}, f32[32,128]{1,0:T(8,128)S(1)}) custom-call(f32[24,32,384]{2,1,0:T(8,128)S(1)} %copy-done.2, f32[32,384]{1,0:T(8,128)S(1)} %get-tuple-element.17.mask_ref, f32[24,32,384]{2,1,0:T(8,128)S(1)} %copy-done.4, f32[24,32,256]{2,1,0:T(8,128)S(1)} %get-tuple-element.20.force_ref, ...), custom_call_target="tpu_custom_call" | custom-call | flops 22118400 | bytes 2949120 | tf_op jit(solution)/shard_map/pallas_call | solution.py:393
  57.5 18.3 %all_to_all.22 = f32[32,1,128]{2,1,0:T(1,128)S(1)} all-to-all(f32[32,1,128]{2,1,0:T(1,128)S(1)} %bitcast.17), channel_id=1, replica_groups=mesh['gy'=16,'gx'=2] {'gy','gx'}, dimensions={0} | all-to-all | bytes 32768 | tf_op jit(solution)/shard_map/all_to_all | solution.py:405
  75.8 0.8 %shard_map.83 = f32[3,32]{1,0:T(4,128)} custom-call(s32[1]{0:T(128)} %bitcast.7.me_ref, f32[32,128]{1,0:T(8,128)S(1)} %bitcast.16), custom_call_target="tpu_custom_call" | custom-call | tf_op jit(solution)/shard_map/pallas_call | solution.py:407
Async XLA Ops:
  3.9 8.5 %copy-start = (f32[3,8,32,256]{3,2,1,0:T(8,128)S(1)}, f32[3,8,32,256]{3,2,1,0:T(8,128)}, u32[]{:S(2)}) copy-start(f32[3,8,32,256]{3,2,1,0:T(8,128)} %param.6) | copy-start | bytes 2359300
  3.9 8.5 %copy-start.5 = (s32[32,256]{1,0:T(8,128)S(1)}, s32[32,256]{1,0:T(8,128)}, u32[]{:S(2)}) copy-start(s32[32,256]{1,0:T(8,128)} %wet_ref.5) | copy-start | bytes 98308
  3.9 43.2 %all-to-all-start = ((bf16[16,8,6272]{2,1,0:T(8,128)(2,1)}), bf16[16,8,6272]{2,1,0:T(8,128)(2,1)S(1)}, u32[]{:S(2)}, u32[]{:S(2)}) async-start(bf16[16,8,6272]{2,1,0:T(8,128)(2,1)} %bitcast.18), calls=%async_computation | async-start | bytes 3211264 | tf_op jit(solution)/shard_map/all_to_all | solution.py:360
  12.7 2.8 %collective-permute-start = (f32[32,128]{1,0:T(8,128)S(1)}, f32[32,128]{1,0:T(8,128)S(1)}, u32[]{:S(2)}, u32[]{:S(2)}) collective-permute-start(f32[32,128]{1,0:T(8,128)S(1)} %get-tuple-element.14), channel_id=1, source_target_pairs={{0,1},{2,3},{4,5},{6,7},{8,9},{10,11},{12,13},{14,15},{16,17},{18,... | collective-permute-start | bytes 49160 | tf_op jit(solution)/shard_map/ppermute | solution.py:365
  14.1 3.1 %collective-permute-start.1 = (f32[32,128]{1,0:T(8,128)S(1)}, f32[32,128]{1,0:T(8,128)S(1)}, u32[]{:S(2)}, u32[]{:S(2)}) collective-permute-start(f32[32,128]{1,0:T(8,128)S(1)} %get-tuple-element.15), channel_id=1, source_target_pairs={{1,0},{3,2},{5,4},{7,6},{9,8},{11,10},{13,12},{15,14},{17,16},{19,... | collective-permute-start | bytes 49160 | tf_op jit(solution)/shard_map/ppermute | solution.py:366
  18.3 1.0 %copy-start.1 = (f32[24,32,384]{2,1,0:T(8,128)}, f32[24,32,384]{2,1,0:T(8,128)S(1)}, u32[]{:S(2)}) copy-start(f32[24,32,384]{2,1,0:T(8,128)S(1)} %get-tuple-element.16.full_ref) | copy-start | bytes 3538948
  19.4 1.0 %copy-start.3 = (f32[24,32,384]{2,1,0:T(8,128)}, f32[24,32,384]{2,1,0:T(8,128)S(1)}, u32[]{:S(2)}) copy-start(f32[24,32,384]{2,1,0:T(8,128)S(1)} %get-tuple-element.18.begun_ref) | copy-start | bytes 3538948
  47.5 6.2 %copy-start.2 = (f32[24,32,384]{2,1,0:T(8,128)S(1)}, f32[24,32,384]{2,1,0:T(8,128)}, u32[]{:S(2)}) copy-start(f32[24,32,384]{2,1,0:T(8,128)} %copy-done.1) | copy-start | bytes 3538948
  47.5 1.2 %collective-permute-start.2 = (f32[32,128]{1,0:T(8,128)S(1)}, f32[32,128]{1,0:T(8,128)S(1)}, u32[]{:S(2)}, u32[]{:S(2)}) collective-permute-start(f32[32,128]{1,0:T(8,128)S(1)} %get-tuple-element.21.edge_ref), channel_id=1, source_target_pairs={{0,1},{1,0},{2,3},{3,2},{4,5},{5,4},{6,7},{7,6},{8,9},{9,8},{10,11... | collective-permute-start | bytes 49160 | tf_op jit(solution)/shard_map/ppermute | solution.py:382
  47.6 6.1 %copy-start.4 = (f32[24,32,384]{2,1,0:T(8,128)S(1)}, f32[24,32,384]{2,1,0:T(8,128)}, u32[]{:S(2)}) copy-start(f32[24,32,384]{2,1,0:T(8,128)} %copy-done.3) | copy-start | bytes 3538948
  48.9 4.7 %collective-permute-start.3 = (f16[43,4,256]{2,1,0:T(4,128)(2,1)S(1)}, f16[43,4,256]{2,1,0:T(4,128)(2,1)S(1)}, u32[]{:S(2)}, u32[]{:S(2)}) collective-permute-start(f16[43,4,256]{2,1,0:T(4,128)(2,1)S(1)} %get-tuple-element.26), channel_id=1, source_target_pairs={{0,2},{2,0},{4,6},{6,4},{8,10},{10,8},{12,14},{14,12},{16,18},{18,... | collective-permute-start | bytes 264200 | tf_op jit(solution)/shard_map/ppermute | solution.py:391
  49.9 3.7 %collective-permute-start.4 = (f16[43,4,256]{2,1,0:T(4,128)(2,1)S(1)}, f16[43,4,256]{2,1,0:T(4,128)(2,1)S(1)}, u32[]{:S(2)}, u32[]{:S(2)}) collective-permute-start(f16[43,4,256]{2,1,0:T(4,128)(2,1)S(1)} %get-tuple-element.27), channel_id=1, source_target_pairs={{2,4},{4,2},{6,8},{8,6},{10,12},{12,10},{14,16},{16,14},{18,20},{2... | collective-permute-start | bytes 264200 | tf_op jit(solution)/shard_map/ppermute | solution.py:390

commit v3 on v2

--- a/solution.py
+++ b/solution.py
@@ -205,87 +205,36 @@
             out_ref[moving + planes + 1 + k // 2, :, lane : lane + LANES] = part * (STATE_SCALE if k < 2 else FORCE_SCALE)
 
 
-def steps_body(sides, devices, full_ref, mask_ref, begun_ref, force_ref, edge_ref, north_ref, south_ref, *refs):
-    side_refs = refs[:sides]
-    state_ref, parts_ref, push_ref, halo_ref, one_ref, two_ref = refs[sides:]
-    planes, rows, wide = full_ref.shape
-    levels = planes // 3
+def factors(mask, own, west, east, force_rows, push_ref):
+    moving, total, wide = push_ref.shape
     cols = wide - LANES
-    total = rows + 2 * RIM
-    moving = 2 * levels
-    last = rows - 2 * RIM
-
-    def joined(index):
-        both = jnp.concatenate([north_ref[index], south_ref[index]], axis=0)
-        if index > moving + planes:
-            return both
-        return both * (1.0 / (FORCE_SCALE if index < moving else STATE_SCALE))
-
-    pairs = [joined(moving + planes + 1 + k) for k in range((sides + 4) // 2)]
-    outer = [
-        pairs[k // 2][:, (k % 2) * LANES : (k % 2 + 1) * LANES] * (1.0 / (STATE_SCALE if k < 2 else FORCE_SCALE))
-        for k in range(3 + sides)
-    ]
-    edges = [jnp.concatenate([side[...], outer[3 + k]], axis=0) for k, side in enumerate(side_refs)]
-    west, east = edges[0], edges[-1]
-    own = jnp.concatenate([edge_ref[...], outer[2]], axis=0)
 
     def counts(edge):
         return jnp.broadcast_to(edge[:, LANES - 1 :], (total, LANES))
 
     lane = iota((total, LANES), 1)
     count_side = jnp.where(lane < LANES // 2, counts(east), counts(west))
-    count = jnp.concatenate([counts(own)] * (cols // LANES) + [count_side], axis=1)
-
-    def halo(index, at):
-        return jnp.concatenate([joined(index), side_tile(outer[0], at, outer[1], at)], axis=1)
-
-    mask = jnp.concatenate([mask_ref[...], halo(moving + planes, EDGE * planes)], axis=0)
-    relax = mask / (1.0 + GAMMA * count)
+    relax = mask / (1.0 + GAMMA * jnp.concatenate([counts(own)] * (cols // LANES) + [count_side], axis=1))
     half = GAMMA * relax
-
     for j in range(moving):
-        tile = side_tile(west, EDGE * (moving + j), east, EDGE * j)
-        whole = jnp.concatenate([force_ref[j], joined(j)], axis=0)
-        push_ref[j, :, :cols] = whole * half[:, :cols]
-        push_ref[j, :, cols:] = tile * half[:, cols:]
-    for j in range(planes):
-        halo_ref[j] = halo(moving + j, EDGE * j)
-
-    def finish(values, z, at=(slice(None),)):
-        tracer, across, along = values
-        rated = relax[at]
-        return (tracer * rated + push_ref[(z, *at)], across * rated, along * rated + push_ref[(levels + z, *at)])
-
-    row = iota((2 * RIM, wide), 0)
-    head, tail = slice(0, 2 * RIM), slice(last, rows)
-
-    def near(j, field):
-        return around_between(field, full_ref[j, :1], full_ref[j, rows - 1 :])
-
+        push_ref[j, :, :cols] = force_rows(j) * half[:, :cols]
+        push_ref[j, :, cols:] = side_tile(west, EDGE * (moving + j), east, EDGE * j) * half[:, cols:]
+    return relax
+
+
+def finish(relax, push_ref, levels, values, z, at=(slice(None),)):
+    tracer, across, along = values
+    rated = relax[at]
+    return (tracer * rated + push_ref[(z, *at)], across * rated, along * rated + push_ref[(levels + z, *at)])
+
+
+def two_more(relax, push_ref, one_ref, two_ref, last):
+    levels = one_ref.shape[0] // 3
+    cols = one_ref.shape[2] - LANES
     for z in range(levels):
-        index = [f * levels + z for f in range(3)]
-        beyond = [halo_ref[j] for j in index]
-        north = [jnp.where(row == 2 * RIM - 1, value[:1], 0.0) for value in beyond]
-        south = [jnp.where(row == 0, value[2 * RIM - 1 :], 0.0) for value in beyond]
-        first = added(-1.0, full_ref[index[2], head], *south)
-        final = added(1.0, full_ref[index[2], tail], *north)
-        blocks = (
-            (head, [begun_ref[j, head] + extra for j, extra in zip(index, first)]),
-            (slice(2 * RIM, last), [begun_ref[j, 2 * RIM : last] for j in index]),
-            (tail, [begun_ref[j, tail] + extra for j, extra in zip(index, final)]),
-            (slice(rows, total), moved(lambda j: halo_ref[j], near, levels, z)),
-        )
-        for at, values in blocks:
-            for j, value in zip(index, finish(values, z, (at,))):
-                one_ref[j, at] = value
-
-    for z in range(levels):
-        for f, value in enumerate(finish(moved(lambda j: one_ref[j], lambda j, field: around(field), levels, z), z)):
+        values = moved(lambda j: one_ref[j], lambda j, field: around(field), levels, z)
+        for f, value in enumerate(finish(relax, push_ref, levels, values, z)):
             two_ref[f * levels + z] = value
-    share = 1.0 / (1.0 + count[:rows, :1])
-    sums = [jnp.zeros((rows, cols), jnp.float32) for _ in range(3)]
-    own_cols = (slice(None), slice(0, cols))
     for z in range(levels):
         values = moved(
             lambda j: two_ref[j, :, :cols],
@@ -293,23 +242,154 @@
             levels,
             z,
         )
-        values = finish(values, z, own_cols)
+        last(z, finish(relax, push_ref, levels, values, z, (slice(None), slice(0, cols))))
+
+
+def terms(values, stokes):
+    rows, total = stokes.shape[0], values[0].shape[0]
+    tracer = values[0]
+    ddy = pltpu.roll(tracer, total - 1, 0)[:rows] - pltpu.roll(tracer, 1, 0)[:rows]
+    return [values[2][:rows] * tracer[:rows], stokes * tracer[:rows], ddy]
+
+
+def transports(sums, count, child, all_rows):
+    raw = [jnp.sum(value, axis=1, keepdims=True) for value in sums]
+    raw = [raw[0], raw[1] / (1.0 + count), raw[2] * (-0.5 * DISPERSE)]
+    lane = iota(child.shape, 1)
+    part = jnp.zeros(child.shape, jnp.float32)
+    for q in range(3):
+        part = part + jnp.where((child >= 0) & (lane == q * all_rows + child), raw[q], 0.0)
+    return jnp.sum(part, axis=0, keepdims=True)
+
+
+def inner_body(mask_ref, begun_ref, force_ref, edge_ref, *refs):
+    side_refs, (middle_ref, ends_ref, part_ref, push_ref, one_ref, two_ref) = refs[:-6], refs[-6:]
+    planes, rows, wide = begun_ref.shape
+    levels = planes // 3
+    cols = wide - LANES
+    moving = 2 * levels
+    tile = 2 * RIM
+    relax = factors(
+        mask_ref[...], edge_ref[...], side_refs[0][...], side_refs[-1][...], lambda j: force_ref[j], push_ref
+    )
+    for z in range(levels):
+        index = [f * levels + z for f in range(3)]
+        for j, value in zip(index, finish(relax, push_ref, levels, [begun_ref[j] for j in index], z)):
+            one_ref[j] = value
+    sums = [jnp.zeros((rows, cols), jnp.float32) for _ in range(3)]
+
+    def last(z, values):
         for f, value in enumerate(values):
-            state_ref[f * levels + z] = value[:rows]
-        tracer = values[0]
-        inner = tracer[:rows]
-        ddy = pltpu.roll(tracer, total - 1, 0)[:rows] - pltpu.roll(tracer, 1, 0)[:rows]
-        sums[0] = sums[0] + values[2][:rows] * inner
-        sums[1] = sums[1] + force_ref[moving + z] * inner
-        sums[2] = sums[2] + ddy
-    raw = [jnp.sum(value, axis=1, keepdims=True) for value in sums]
-    raw = [raw[0], raw[1] * share, raw[2] * (-0.5 * DISPERSE)]
-    row, lane = iota((rows, LANES), 0), iota((rows, LANES), 1)
-    part = jnp.zeros((rows, LANES), jnp.float32)
-    for q in range(3):
-        part = part + jnp.where(lane == q * rows + row, raw[q], 0.0)
-    part = jnp.sum(part, axis=0, keepdims=True)
-    parts_ref[...] = jnp.broadcast_to(part, (devices, LANES))
+            middle_ref[f, z] = value[tile : rows - tile]
+            ends_ref[f, z, :tile] = value[:tile]
+            ends_ref[f, z, tile:] = value[rows - tile :]
+        for q, term in enumerate(terms(values, force_ref[moving + z])):
+            sums[q] = sums[q] + term
+
+    two_more(relax, push_ref, one_ref, two_ref, last)
+    row = iota((rows, LANES), 0)
+    child = jnp.where((row >= RIM) & (row < rows - RIM), row, -1)
+    part_ref[...] = transports(sums, edge_ref[:, LANES - 1 :], child, rows)
+
+
+def steps_body(
+    sides, full_ref, mask_ref, begun_ref, force_ref, edge_ref, north_ref, south_ref, middle_ref, ends_ref, part_ref, *refs
+):
+    side_refs = refs[:sides]
+    state_ref, parts_ref, push_ref, halo_ref, one_ref, two_ref, held_ref, sent = refs[sides:]
+    planes, rows, wide = full_ref.shape
+    levels = planes // 3
+    cols = wide - LANES
+    moving = 2 * levels
+    tile = 2 * RIM
+    own_rows, total = 2 * tile, 3 * tile
+    tail = slice(rows - tile, rows)
+    copies = [pltpu.make_async_copy(middle_ref, state_ref.at[:, :, pl.ds(tile, rows - 2 * tile)], sent.at[0])]
+    copies[0].start()
+
+    def slab(ref, *index):
+        return [ref[(*index, slice(0, tile))], ref[(*index, tail)]]
+
+    def joined(index):
+        both = jnp.concatenate([north_ref[index], south_ref[index]], axis=0)
+        if index > moving + planes:
+            return both
+        return both * (1.0 / (FORCE_SCALE if index < moving else STATE_SCALE))
+
+    pairs = [joined(moving + planes + 1 + k) for k in range((sides + 4) // 2)]
+    outer = [
+        pairs[k // 2][:, (k % 2) * LANES : (k % 2 + 1) * LANES] * (1.0 / (STATE_SCALE if k < 2 else FORCE_SCALE))
+        for k in range(3 + sides)
+    ]
+    edges = [jnp.concatenate([*slab(side), outer[3 + k]], axis=0) for k, side in enumerate(side_refs)]
+    own = jnp.concatenate([*slab(edge_ref), outer[2]], axis=0)
+
+    def halo(index, at):
+        return jnp.concatenate([joined(index), side_tile(outer[0], at, outer[1], at)], axis=1)
+
+    mask = jnp.concatenate([*slab(mask_ref), halo(moving + planes, EDGE * planes)], axis=0)
+    relax = factors(
+        mask,
+        own,
+        edges[0],
+        edges[-1],
+        lambda j: jnp.concatenate([*slab(force_ref, j), joined(j)], axis=0),
+        push_ref,
+    )
+    for j in range(planes):
+        halo_ref[j] = halo(moving + j, EDGE * j)
+    row = iota((tile, wide), 0)
+
+    def near(j, field):
+        return around_between(field, full_ref[j, :1], full_ref[j, rows - 1 :])
+
+    for z in range(levels):
+        index = [f * levels + z for f in range(3)]
+        beyond = [halo_ref[j] for j in index]
+        north = [jnp.where(row == tile - 1, value[:1], 0.0) for value in beyond]
+        south = [jnp.where(row == 0, value[tile - 1 :], 0.0) for value in beyond]
+        first = added(-1.0, full_ref[index[2], :tile], *south)
+        final = added(1.0, full_ref[index[2], tail], *north)
+        blocks = (
+            [begun_ref[j, :tile] + extra for j, extra in zip(index, first)],
+            [begun_ref[j, tail] + extra for j, extra in zip(index, final)],
+            moved(lambda j: halo_ref[j], near, levels, z),
+        )
+        for k, values in enumerate(blocks):
+            at = slice(k * tile, (k + 1) * tile)
+            for j, value in zip(index, finish(relax, push_ref, levels, values, z, (at,))):
+                one_ref[j, at] = value
+
+    sums = [jnp.zeros((own_rows, cols), jnp.float32) for _ in range(3)]
+    row = iota((tile, cols), 0)
+    batch = levels // 2
+
+    def last(z, values):
+        for f, value in enumerate(values):
+            held_ref[f, z, :tile] = jnp.where(row < RIM, value[:tile], ends_ref[f, z, :tile])
+            held_ref[f, z, tile:] = jnp.where(row < RIM, ends_ref[f, z, tile:], value[tile:own_rows])
+        stokes = jnp.concatenate(slab(force_ref, moving + z), axis=0)
+        for q, term in enumerate(terms(values, stokes)):
+            sums[q] = sums[q] + term
+        if z % batch == batch - 1:
+            at = pl.ds(z + 1 - batch, batch)
+            for k, start in enumerate((0, rows - tile)):
+                copies.append(
+                    pltpu.make_async_copy(
+                        held_ref.at[:, at, pl.ds(k * tile, tile)],
+                        state_ref.at[:, at, pl.ds(start, tile)],
+                        sent.at[len(copies)],
+                    )
+                )
+                copies[-1].start()
+
+    two_more(relax, push_ref, one_ref, two_ref, last)
+    row = iota((own_rows, LANES), 0)
+    child = jnp.where(row < RIM, row, jnp.where(row >= own_rows - RIM, row + rows - own_rows, -1))
+    part = transports(sums, own[:own_rows, LANES - 1 :], child, rows) + part_ref[...]
+    parts_ref[...] = jnp.broadcast_to(part, parts_ref.shape)
+    for copy in copies:
+        copy.wait()
 
 
 def profile_body(across, along, me_ref, parts_ref, out_ref):
@@ -334,7 +414,7 @@
     along, across = lax.axis_size("gy"), lax.axis_size("gx")
     capacity = 2 * SEND // along
     slots = along * capacity
-    total, wide = rows + 2 * RIM, cols + LANES
+    wide = cols + LANES
     f32 = jnp.float32
     even_pairs = [(i, i ^ 1) for i in range(along)]
     odd_pairs = [(i, ((i + 1) ^ 1) - 1) for i in range(1, along - 1)]
@@ -390,18 +470,39 @@
     far = lax.ppermute(jnp.where(even, down, up).astype(jnp.float16), "gy", odd_pairs).astype(f32)
     near = lax.ppermute(jnp.where(even, up, down).astype(jnp.float16), "gy", even_pairs).astype(f32)
     above, below = jnp.where(even, near, far), jnp.where(even, far, near)
+    tile = 2 * RIM
+    middle, ends, part = call(
+        inner_body,
+        (
+            jax.ShapeDtypeStruct((fields, levels, rows - 2 * tile, cols), f32),
+            jax.ShapeDtypeStruct((fields, levels, 2 * tile, cols), f32),
+            jax.ShapeDtypeStruct((1, LANES), f32),
+        ),
+        flops=60 * planes * rows * wide,
+        moved=8 * planes * rows * wide,
+        scratch_shapes=[
+            pltpu.VMEM((moving, rows, wide), f32),
+            pltpu.VMEM((planes, rows, wide), f32),
+            pltpu.VMEM((planes, rows, wide), f32),
+        ],
+    )(mask, begun, force, edge, *sides)
+    whole = pl.BlockSpec(memory_space=pltpu.VMEM)
     new_state, parts = call(
-        functools.partial(steps_body, len(sides), along * across),
-        (jax.ShapeDtypeStruct((planes, rows, cols), f32), jax.ShapeDtypeStruct((along * across, LANES), f32)),
-        flops=60 * planes * total * wide,
-        moved=8 * planes * total * wide,
+        functools.partial(steps_body, len(sides)),
+        (jax.ShapeDtypeStruct(state.shape, f32), jax.ShapeDtypeStruct((along * across, LANES), f32)),
+        flops=60 * planes * 3 * tile * wide,
+        moved=8 * planes * 3 * tile * wide,
+        in_specs=[whole] * (10 + len(sides)),
+        out_specs=[pl.BlockSpec(memory_space=pl.ANY), whole],
         scratch_shapes=[
-            pltpu.VMEM((moving, total, wide), f32),
-            pltpu.VMEM((planes, 2 * RIM, wide), f32),
-            pltpu.VMEM((planes, total, wide), f32),
-            pltpu.VMEM((planes, total, wide), f32),
+            pltpu.VMEM((moving, 3 * tile, wide), f32),
+            pltpu.VMEM((planes, tile, wide), f32),
+            pltpu.VMEM((planes, 3 * tile, wide), f32),
+            pltpu.VMEM((planes, 3 * tile, wide), f32),
+            pltpu.VMEM((fields, levels, 2 * tile, cols), f32),
+            pltpu.SemaphoreType.DMA((5,)),
         ],
-    )(full, mask, begun, force, edge, above, below, *sides)
+    )(full, mask, begun, force, edge, above, below, middle, ends, part, *sides)
     every = lax.all_to_all(parts, ("gy", "gx"), split_axis=0, concat_axis=0, tiled=True)
     me = lax.axis_index("gy").astype(jnp.int32).reshape(1)
     profile = call(
@@ -409,7 +510,7 @@
         jax.ShapeDtypeStruct((3, rows), f32),
         in_specs=[pl.BlockSpec(memory_space=pltpu.SMEM), pl.BlockSpec(memory_space=pltpu.VMEM)],
     )(me, every)
-    return new_state.reshape(state.shape), profile
+    return new_state, profile
 
 
 def solution(mesh):

time: 76.8 us -> 75.6 us (0.984)
  waiting for transfers between devices: 32.7 us -> 30.7 us
  Pallas kernels: 9.6 us -> 10.4 us
    ppermute x1, waiting for transfers between devices: 3.05 us -> 1.02 us  [per_device(): lax.ppermute(jnp.where(even, up, down).astype(jnp.float16), 'gy', even_pa...]
    pallas_call x1 -> x2, Pallas kernels: 3.74 us -> 4.54 us  [the longest x1 2.53 us: per_device(): call(functools.partial(steps_body, len(sides)), (jax.ShapeDtypeStruct(sta...]
  transfers between devices with their start and end apart: 6 -> 6, of which waited for: 4 -> 4; matrix products, arithmetic and copies ran while one was open for 0% -> 0% of each run, Pallas kernels for 2% -> 4%
where the time goes in v3:
time: 75.6 us; the launch traced here: 75.3 us
  waiting for transfers between devices  30.7 us (41%)
  blocking collectives  18.3 us (24%)
  starting transfers between devices  13 us (17%)
  Pallas kernels  10.4 us (14%)
  local copies, waits for them, and re-layouts  2.07 us (3%)
  between operations  0.82 us (1%)
    all_to_all x1, waiting for transfers between devices, per_device(): lax.all_to_all(payload, 'gy', split_axis=0, concat_axis=0, tiled=True)  26.7 us
    all_to_all x1, blocking collectives, per_device(): lax.all_to_all(parts, ('gy', 'gx'), split_axis=0, concat_axis=0, tiled=True)  18.3 us
    all_to_all x1, starting transfers between devices, per_device(): lax.all_to_all(payload, 'gy', split_axis=0, concat_axis=0, tiled=True)  8.46 us
    pallas_call x1, Pallas kernels, per_device(): call(functools.partial(gather_body, capacity, slots), jax.ShapeDtypeStruc...  3.19 us
    pallas_call x1, Pallas kernels, per_device(): call(functools.partial(steps_body, len(sides)), (jax.ShapeDtypeStruct(sta...  2.53 us
    unnamed x12, local copies, waits for them, and re-layouts  2.07 us
    pallas_call x1, Pallas kernels, per_device(): call(inner_body, (jax.ShapeDtypeStruct((fields, levels, rows - 2 * tile,...  2.01 us
    ppermute x1, waiting for transfers between devices, per_device(): from_east = lax.ppermute(first, 'gx', westward)  1.77 us
  transfers between devices with their start and end apart: 6, of which 4 were waited for; matrix products, arithmetic and copies ran while one was open for 0% of the time, Pallas kernels for 4%

profile of v3, /device:TPU:0, one launch (start us, length us, event | category | flops | bytes accessed | tf_op | source)
XLA Modules:
  0.0 75.3 jit_solution(3027789615555944216)
XLA Ops:
  0.6 3.2 %shard_map.79 = bf16[128,6272]{1,0:T(8,128)(2,1)} custom-call(s32[1,64]{1,0:T(1,128)} %bitcast.18, s32[1,64]{1,0:T(1,128)} %bitcast.19, s32[1,64]{1,0:T(1,128)} %bitcast.20, bf16[64,24,256]{2,1,0:T(8,128)(2,1)} %refs_3_.1), custom_call_target="tpu_custom_call" | custom-call | flops 805306368 | bytes 2359296 | tf_op jit(solution)/shard_map/pallas_call | solution.py:424
  3.8 0.0 copy-start
  3.8 0.0 copy-start.5
  3.9 8.5 %all-to-all-start = ((bf16[16,8,6272]{2,1,0:T(8,128)(2,1)}), bf16[16,8,6272]{2,1,0:T(8,128)(2,1)S(1)}, u32[]{:S(2)}, u32[]{:S(2)}) async-start(bf16[16,8,6272]{2,1,0:T(8,128)(2,1)} %bitcast.17), calls=%async_computation | async-start | bytes 3211264 | tf_op jit(solution)/shard_map/all_to_all | solution.py:440
  12.3 0.0 copy-done
  12.3 0.0 copy-done.5
  12.3 0.3 shard_map.77
  12.6 1.5 %collective-permute-start = (f32[32,128]{1,0:T(8,128)S(1)}, f32[32,128]{1,0:T(8,128)S(1)}, u32[]{:S(2)}, u32[]{:S(2)}) collective-permute-start(f32[32,128]{1,0:T(8,128)S(1)} %get-tuple-element.17), channel_id=1, source_target_pairs={{0,1},{2,3},{4,5},{6,7},{8,9},{10,11},{12,13},{14,15},{16,17},{18,... | collective-permute-start | bytes 49160 | tf_op jit(solution)/shard_map/ppermute | solution.py:445
  14.1 1.3 %collective-permute-start.1 = (f32[32,128]{1,0:T(8,128)S(1)}, f32[32,128]{1,0:T(8,128)S(1)}, u32[]{:S(2)}, u32[]{:S(2)}) collective-permute-start(f32[32,128]{1,0:T(8,128)S(1)} %get-tuple-element.18), channel_id=1, source_target_pairs={{1,0},{3,2},{5,4},{7,6},{9,8},{11,10},{13,12},{15,14},{17,16},{19,... | collective-permute-start | bytes 49160 | tf_op jit(solution)/shard_map/ppermute | solution.py:446
  15.4 0.0 collective-permute-done.west_ref
  15.4 1.8 %collective-permute-done.1.east_ref = f32[32,128]{1,0:T(8,128)S(1)} collective-permute-done((f32[32,128]{1,0:T(8,128)S(1)}, f32[32,128]{1,0:T(8,128)S(1)}, u32[]{:S(2)}, u32[]{:S(2)}) %collective-permute-start.1) | collective-permute-done | bytes 16416 | tf_op jit(solution)/shard_map/ppermute | solution.py:446
  17.2 1.1 %shard_map.78 = (f32[24,32,384]{2,1,0:T(8,128)S(1)}, f32[32,384]{1,0:T(8,128)S(1)}, f32[24,32,384]{2,1,0:T(8,128)S(1)}, f32[8,128]{1,0:T(8,128)S(1)}) custom-call(f32[24,32,256]{2,1,0:T(8,128)S(1)} %bitcast.12, s32[32,256]{1,0:T(8,128)S(1)} %copy-done.5, f32[32,128]{1,0:T(8,128)S(1)} %collective-permute-done.west_ref, ...), custom_call_target="tpu_custom_call" | custom-call | flops 5898240 | bytes 3538944 | tf_op jit(solution)/shard_map/pallas_call | solution.py:448
  18.3 0.0 copy-start.1
  18.3 1.0 %copy-done.1 = f32[24,32,384]{2,1,0:T(8,128)} copy-done((f32[24,32,384]{2,1,0:T(8,128)}, f32[24,32,384]{2,1,0:T(8,128)S(1)}, u32[]{:S(2)}) %copy-start.1) | copy-done | bytes 1179672
  19.3 0.0 copy-start.3
  19.3 1.0 %copy-done.3 = f32[24,32,384]{2,1,0:T(8,128)} copy-done((f32[24,32,384]{2,1,0:T(8,128)}, f32[24,32,384]{2,1,0:T(8,128)S(1)}, u32[]{:S(2)}) %copy-start.3) | copy-done | bytes 1179672
  20.3 26.7 %all-to-all-done = bf16[16,8,6272]{2,1,0:T(8,128)(2,1)S(1)} async-done(((bf16[16,8,6272]{2,1,0:T(8,128)(2,1)}), bf16[16,8,6272]{2,1,0:T(8,128)(2,1)S(1)}, u32[]{:S(2)}, u32[]{:S(2)}) %all-to-all-start) | async-done | bytes 1605664 | tf_op jit(solution)/shard_map/all_to_all | solution.py:440
  47.1 0.4 shard_map.80
  47.5 0.0 copy-start.2
  47.5 0.1 collective-permute-start.2
  47.6 1.2 %collective-permute-done.2.refs_0_ = f32[32,128]{1,0:T(8,128)S(1)} collective-permute-done((f32[32,128]{1,0:T(8,128)S(1)}, f32[32,128]{1,0:T(8,128)S(1)}, u32[]{:S(2)}, u32[]{:S(2)}) %collective-permute-start.2) | collective-permute-done | bytes 16416 | tf_op jit(solution)/shard_map/ppermute | solution.py:462
  48.8 0.1 shard_map.81
  48.8 0.0 copy-start.4
  48.8 0.1 select_convert_fusion.1
  48.9 1.0 %collective-permute-start.3 = (f16[43,4,256]{2,1,0:T(4,128)(2,1)S(1)}, f16[43,4,256]{2,1,0:T(4,128)(2,1)S(1)}, u32[]{:S(2)}, u32[]{:S(2)}) collective-permute-start(f16[43,4,256]{2,1,0:T(4,128)(2,1)S(1)} %get-tuple-element.32), channel_id=1, source_target_pairs={{0,2},{2,0},{4,6},{6,4},{8,10},{10,8},{12,14},{14,12},{16,18},{18,... | collective-permute-start | bytes 264200 | tf_op jit(solution)/shard_map/ppermute | solution.py:471
  49.9 0.7 collective-permute-start.4
  50.6 0.0 copy-done.2
  50.6 2.0 %shard_map.82 = (f32[3,8,16,256]{3,2,1,0:T(8,128)S(1)}, f32[3,8,16,256]{3,2,1,0:T(8,128)S(1)}, f32[1,128]{1,0:T(1,128)S(1)}) custom-call(f32[32,384]{1,0:T(8,128)S(1)} %get-tuple-element.20.mask_ref, f32[24,32,384]{2,1,0:T(8,128)S(1)} %copy-done.2, f32[24,32,256]{2,1,0:T(8,128)S(1)} %get-tuple-element.23.force_ref, ...), custom_call_target="tpu_custom_call" | custom-call | flops 17694720 | bytes 2359296 | tf_op jit(solution)/shard_map/pallas_call | solution.py:474
  52.6 1.0 %collective-permute-done.3 = f16[43,4,256]{2,1,0:T(4,128)(2,1)S(1)} collective-permute-done((f16[43,4,256]{2,1,0:T(4,128)(2,1)S(1)}, f16[43,4,256]{2,1,0:T(4,128)(2,1)S(1)}, u32[]{:S(2)}, u32[]{:S(2)}) %collective-permute-start.3) | collective-permute-done | bytes 88096 | tf_op jit(solution)/shard_map/ppermute | solution.py:471
  53.6 0.0 collective-permute-done.4
  53.6 0.1 convert_select_fusion
  53.7 0.0 copy-done.4
  53.7 2.5 %shard_map.83 = (f32[3,8,32,256]{3,2,1,0:T(8,128)}, f32[32,128]{1,0:T(8,128)S(1)}) custom-call(f32[24,32,384]{2,1,0:T(8,128)S(1)} %copy-done.4, f32[32,384]{1,0:T(8,128)S(1)} %get-tuple-element.20.mask_ref, f32[24,32,384]{2,1,0:T(8,128)S(1)} %copy-done.2, f32[24,32,256]{2,1,0:T(8,128)S(1)} %get-tuple-element.23.force_ref, ...), custom_call_target="tpu_custom_call" | custom-call | flops 13271040 | bytes 1769472 | tf_op jit(solution)/shard_map/pallas_call | solution.py:490
  56.2 18.3 %all_to_all.22 = f32[32,1,128]{2,1,0:T(1,128)S(1)} all-to-all(f32[32,1,128]{2,1,0:T(1,128)S(1)} %bitcast.16), channel_id=1, replica_groups=mesh['gy'=16,'gx'=2] {'gy','gx'}, dimensions={0} | all-to-all | bytes 32768 | tf_op jit(solution)/shard_map/all_to_all | solution.py:506
  74.5 0.8 %shard_map.84 = f32[3,32]{1,0:T(4,128)} custom-call(s32[1]{0:T(128)} %bitcast.6.me_ref, f32[32,128]{1,0:T(8,128)S(1)} %bitcast.15), custom_call_target="tpu_custom_call" | custom-call | tf_op jit(solution)/shard_map/pallas_call | solution.py:508
Async XLA Ops:
  3.8 8.5 %copy-start = (f32[3,8,32,256]{3,2,1,0:T(8,128)S(1)}, f32[3,8,32,256]{3,2,1,0:T(8,128)}, u32[]{:S(2)}) copy-start(f32[3,8,32,256]{3,2,1,0:T(8,128)} %param.6) | copy-start | bytes 2359300
  3.8 8.5 %copy-start.5 = (s32[32,256]{1,0:T(8,128)S(1)}, s32[32,256]{1,0:T(8,128)}, u32[]{:S(2)}) copy-start(s32[32,256]{1,0:T(8,128)} %wet_ref.5) | copy-start | bytes 98308
  3.9 43.2 %all-to-all-start = ((bf16[16,8,6272]{2,1,0:T(8,128)(2,1)}), bf16[16,8,6272]{2,1,0:T(8,128)(2,1)S(1)}, u32[]{:S(2)}, u32[]{:S(2)}) async-start(bf16[16,8,6272]{2,1,0:T(8,128)(2,1)} %bitcast.17), calls=%async_computation | async-start | bytes 3211264 | tf_op jit(solution)/shard_map/all_to_all | solution.py:440
  12.6 2.8 %collective-permute-start = (f32[32,128]{1,0:T(8,128)S(1)}, f32[32,128]{1,0:T(8,128)S(1)}, u32[]{:S(2)}, u32[]{:S(2)}) collective-permute-start(f32[32,128]{1,0:T(8,128)S(1)} %get-tuple-element.17), channel_id=1, source_target_pairs={{0,1},{2,3},{4,5},{6,7},{8,9},{10,11},{12,13},{14,15},{16,17},{18,... | collective-permute-start | bytes 49160 | tf_op jit(solution)/shard_map/ppermute | solution.py:445
  14.1 3.1 %collective-permute-start.1 = (f32[32,128]{1,0:T(8,128)S(1)}, f32[32,128]{1,0:T(8,128)S(1)}, u32[]{:S(2)}, u32[]{:S(2)}) collective-permute-start(f32[32,128]{1,0:T(8,128)S(1)} %get-tuple-element.18), channel_id=1, source_target_pairs={{1,0},{3,2},{5,4},{7,6},{9,8},{11,10},{13,12},{15,14},{17,16},{19,... | collective-permute-start | bytes 49160 | tf_op jit(solution)/shard_map/ppermute | solution.py:446
  18.3 1.0 %copy-start.1 = (f32[24,32,384]{2,1,0:T(8,128)}, f32[24,32,384]{2,1,0:T(8,128)S(1)}, u32[]{:S(2)}) copy-start(f32[24,32,384]{2,1,0:T(8,128)S(1)} %get-tuple-element.21.begun_ref) | copy-start | bytes 3538948
  19.3 1.0 %copy-start.3 = (f32[24,32,384]{2,1,0:T(8,128)}, f32[24,32,384]{2,1,0:T(8,128)S(1)}, u32[]{:S(2)}) copy-start(f32[24,32,384]{2,1,0:T(8,128)S(1)} %get-tuple-element.19.full_ref) | copy-start | bytes 3538948
  47.5 3.1 %copy-start.2 = (f32[24,32,384]{2,1,0:T(8,128)S(1)}, f32[24,32,384]{2,1,0:T(8,128)}, u32[]{:S(2)}) copy-start(f32[24,32,384]{2,1,0:T(8,128)} %copy-done.1) | copy-start | bytes 3538948
  47.5 1.2 %collective-permute-start.2 = (f32[32,128]{1,0:T(8,128)S(1)}, f32[32,128]{1,0:T(8,128)S(1)}, u32[]{:S(2)}, u32[]{:S(2)}) collective-permute-start(f32[32,128]{1,0:T(8,128)S(1)} %get-tuple-element.24.edge_ref), channel_id=1, source_target_pairs={{0,1},{1,0},{2,3},{3,2},{4,5},{5,4},{6,7},{7,6},{8,9},{9,8},{10,11... | collective-permute-start | bytes 49160 | tf_op jit(solution)/shard_map/ppermute | solution.py:462
  48.8 4.9 %copy-start.4 = (f32[24,32,384]{2,1,0:T(8,128)S(1)}, f32[24,32,384]{2,1,0:T(8,128)}, u32[]{:S(2)}) copy-start(f32[24,32,384]{2,1,0:T(8,128)} %copy-done.3) | copy-start | bytes 3538948
  48.9 4.7 %collective-permute-start.3 = (f16[43,4,256]{2,1,0:T(4,128)(2,1)S(1)}, f16[43,4,256]{2,1,0:T(4,128)(2,1)S(1)}, u32[]{:S(2)}, u32[]{:S(2)}) collective-permute-start(f16[43,4,256]{2,1,0:T(4,128)(2,1)S(1)} %get-tuple-element.32), channel_id=1, source_target_pairs={{0,2},{2,0},{4,6},{6,4},{8,10},{10,8},{12,14},{14,12},{16,18},{18,... | collective-permute-start | bytes 264200 | tf_op jit(solution)/shard_map/ppermute | solution.py:471
  49.9 3.7 %collective-permute-start.4 = (f16[43,4,256]{2,1,0:T(4,128)(2,1)S(1)}, f16[43,4,256]{2,1,0:T(4,128)(2,1)S(1)}, u32[]{:S(2)}, u32[]{:S(2)}) collective-permute-start(f16[43,4,256]{2,1,0:T(4,128)(2,1)S(1)} %get-tuple-element.33), channel_id=1, source_target_pairs={{2,4},{4,2},{6,8},{8,6},{10,12},{12,10},{14,16},{16,14},{18,20},{2... | collective-permute-start | bytes 264200 | tf_op jit(solution)/shard_map/ppermute | solution.py:470

commit v4 on v3

--- a/solution.py
+++ b/solution.py
@@ -22,6 +22,7 @@
 LANES = 128
 STATE_SCALE = 8192.0
 FORCE_SCALE = 64.0
+SUM_SCALE = 128.0
 VMEM_LIMIT = 16 * 1024 * 1024
 VMEM_MOST = 60 * 1024 * 1024
 
@@ -40,7 +41,7 @@
     return lax.broadcasted_iota(jnp.int32, shape, dim)
 
 
-def gather_body(capacity, slots, *refs):
+def gather_body(capacity, slots, far, *refs):
     sources, out_ref, targets, held_ref, copied, sent = refs[:4], refs[4], refs[5:9], refs[9], refs[10], refs[11]
     copies = [
         pltpu.make_async_copy(source, target, copied.at[k]) for k, (source, target) in enumerate(zip(sources, targets))
@@ -56,7 +57,10 @@
     dest_column = jnp.sum(jnp.where(eye, dest, 0), axis=1, keepdims=True)
     earlier = (dest_column == dest) & (iota((send, send), 0) < iota((send, send), 1))
     rank = jnp.sum(earlier.astype(jnp.int32), axis=0, keepdims=True)
-    slot_of = dest * capacity + rank
+    half = slots // capacity
+    mine = lax.axis_index("gy") >= half
+    there = (dest >= half) != mine if far else (dest >= half) == mine
+    slot_of = jnp.where(there, jnp.where(dest >= half, dest - half, dest) * capacity + rank, -1)
     taken = iota((slots, send), 0) == slot_of
     source = jnp.sum(jnp.where(taken, pick_ref[...] + 1, 0), axis=1, keepdims=True) - 1
     label = jnp.sum(jnp.where(taken, offset_ref[...] + 1, 0), axis=1, keepdims=True)
@@ -89,18 +93,42 @@
         part.wait()
 
 
-def landing_body(planes, cols, token_ref, arrived_ref, force_ref, edge_ref):
+def landing_of(arrived_ref, rows):
+    slots, width = arrived_ref.shape
+    label = arrived_ref[:, width - LANES :].astype(jnp.float32)
+    landing = (label == (iota((slots, LANES), 1) + 1).astype(jnp.float32)).astype(jnp.float32)
+    return landing.T[:rows].astype(jnp.bfloat16)
+
+
+def landed(landing, values):
+    return jnp.dot(landing, values, preferred_element_type=jnp.float32)
+
+
+def far_body(token_ref, arrived_ref, sums_ref):
+    rows = sums_ref.shape[0]
+    slots, width = arrived_ref.shape
+    landing = landing_of(arrived_ref, rows)
+    step = 2 * LANES
+    for at in range(0, width - LANES, step):
+        sums_ref[:, at : at + step] = landed(landing, arrived_ref[:, at : at + step]) * SUM_SCALE
+    sums_ref[:, width - LANES :] = landed(landing, jnp.full((slots, LANES), SUM_SCALE, jnp.bfloat16))
+
+
+def come_body(sums_ref, token_ref):
+    token_ref[...] = jnp.zeros_like(token_ref)
+
+
+def landing_body(planes, cols, token_ref, arrived_ref, sums_ref, force_ref, edge_ref):
     slots = arrived_ref.shape[0]
     rows = force_ref.shape[1]
-    width = planes * cols
-    label = arrived_ref[:, width:].astype(jnp.float32)
-    landing = (label == (iota((slots, LANES), 1) + 1).astype(jnp.float32)).astype(jnp.float32)
-    landing = landing.T[:rows].astype(jnp.bfloat16)
-    count = jnp.dot(landing, jnp.ones((slots, LANES), jnp.bfloat16), preferred_element_type=jnp.float32)
+    landing = landing_of(arrived_ref, rows)
+    far = 1.0 / SUM_SCALE
+    count = landed(landing, jnp.ones((slots, LANES), jnp.bfloat16)) + sums_ref[:, planes * cols :] * far
     moving = 2 * planes // 3
     edge = count
     for j in range(planes):
-        force = jnp.dot(landing, arrived_ref[:, j * cols : (j + 1) * cols], preferred_element_type=jnp.float32)
+        at = slice(j * cols, (j + 1) * cols)
+        force = landed(landing, arrived_ref[:, at]) + sums_ref[:, at] * far
         force_ref[j] = force
         if j < moving:
             edge = packed(edge, force[:, :LANES], 0, EDGE * j)
@@ -174,13 +202,16 @@
     ]
 
 
-def begin_body(state_ref, wet_ref, west_ref, east_ref, full_ref, mask_ref, begun_ref, token_ref):
+def begin_body(state_ref, wet_ref, west_ref, east_ref, tips_ref, mask_ref, begun_ref, token_ref, full_ref):
     planes, rows, cols = state_ref.shape
     levels = planes // 3
+    tile = 2 * RIM
     west, east = west_ref[...], east_ref[...]
     for j in range(planes):
         full_ref[j, :, :cols] = state_ref[j]
         full_ref[j, :, cols:] = side_tile(west, EDGE * j, east, EDGE * j)
+        tips_ref[j, :tile] = full_ref[j, :tile]
+        tips_ref[j, tile:] = full_ref[j, rows - tile :]
     mask_ref[:, :cols] = wet_ref[...].astype(jnp.float32)
     mask_ref[:, cols:] = side_tile(west, EDGE * planes, east, EDGE * planes)
     for z in range(levels):
@@ -190,15 +221,15 @@
     token_ref[...] = jnp.zeros_like(token_ref)
 
 
-def outer_body(force_ref, edge_ref, state_ref, wet_ref, west_ref, east_ref, *refs):
+def outer_body(force_ref, edge_ref, tips_ref, mask_ref, west_ref, east_ref, *refs):
     sides, (up_ref, down_ref) = refs[:-2], refs[-2:]
-    planes, rows, cols = state_ref.shape
+    planes, rows, cols = force_ref.shape
     moving = 2 * planes // 3
-    ends = ((up_ref, slice(rows - RIM, rows)), (down_ref, slice(0, RIM)))
-    for out_ref, at in ends:
+    ends = ((up_ref, slice(rows - RIM, rows), slice(3 * RIM, 4 * RIM)), (down_ref, slice(0, RIM), slice(0, RIM)))
+    for out_ref, at, tip in ends:
         out_ref[:moving] = force_ref[:moving, at] * FORCE_SCALE
-        out_ref[moving : moving + planes] = state_ref[:, at] * STATE_SCALE
-        out_ref[moving + planes] = wet_ref[at].astype(jnp.float32) * STATE_SCALE
+        out_ref[moving : moving + planes] = tips_ref[:, tip, :cols] * STATE_SCALE
+        out_ref[moving + planes] = mask_ref[at, :cols] * STATE_SCALE
         parts = [west_ref[at], east_ref[at], edge_ref[at]] + [side[at] for side in sides]
         for k, part in enumerate(parts):
             lane = (k % 2) * LANES
@@ -293,11 +324,11 @@
 
 
 def steps_body(
-    sides, full_ref, mask_ref, begun_ref, force_ref, edge_ref, north_ref, south_ref, middle_ref, ends_ref, part_ref, *refs
+    sides, tips_ref, mask_ref, begun_ref, force_ref, edge_ref, north_ref, south_ref, middle_ref, ends_ref, part_ref, *refs
 ):
     side_refs = refs[:sides]
     state_ref, parts_ref, push_ref, halo_ref, one_ref, two_ref, held_ref, sent = refs[sides:]
-    planes, rows, wide = full_ref.shape
+    planes, rows, wide = begun_ref.shape
     levels = planes // 3
     cols = wide - LANES
     moving = 2 * levels
@@ -341,15 +372,15 @@
     row = iota((tile, wide), 0)
 
     def near(j, field):
-        return around_between(field, full_ref[j, :1], full_ref[j, rows - 1 :])
+        return around_between(field, tips_ref[j, :1], tips_ref[j, own_rows - 1 :])
 
     for z in range(levels):
         index = [f * levels + z for f in range(3)]
         beyond = [halo_ref[j] for j in index]
         north = [jnp.where(row == tile - 1, value[:1], 0.0) for value in beyond]
         south = [jnp.where(row == 0, value[tile - 1 :], 0.0) for value in beyond]
-        first = added(-1.0, full_ref[index[2], :tile], *south)
-        final = added(1.0, full_ref[index[2], tail], *north)
+        first = added(-1.0, tips_ref[index[2], :tile], *south)
+        final = added(1.0, tips_ref[index[2], tile:], *north)
         blocks = (
             [begun_ref[j, :tile] + extra for j, extra in zip(index, first)],
             [begun_ref[j, tail] + extra for j, extra in zip(index, final)],
@@ -413,7 +444,6 @@
     moving = 2 * levels
     along, across = lax.axis_size("gy"), lax.axis_size("gx")
     capacity = 2 * SEND // along
-    slots = along * capacity
     wide = cols + LANES
     f32 = jnp.float32
     even_pairs = [(i, i ^ 1) for i in range(along)]
@@ -421,23 +451,33 @@
     eastward = [(i, i + 1) for i in range(across - 1)]
     westward = [(i + 1, i) for i in range(across - 1)]
 
-    payload = call(
-        functools.partial(gather_body, capacity, slots),
-        jax.ShapeDtypeStruct((slots, planes * cols + LANES), jnp.bfloat16),
-        flops=2 * 8 * slots * SEND * planes * cols,
-        moved=2 * (SEND + slots) * planes * cols,
-        limit=VMEM_MOST,
-        in_specs=[pl.BlockSpec(memory_space=pl.ANY)] * 4,
-        out_specs=pl.BlockSpec(memory_space=pl.ANY),
-        scratch_shapes=[pltpu.VMEM((1, SEND), jnp.int32)] * 3
-        + [
-            pltpu.VMEM(parent_rows.shape, jnp.bfloat16),
-            pltpu.VMEM((slots, planes * cols + LANES), jnp.bfloat16),
-            pltpu.SemaphoreType.DMA((4,)),
-            pltpu.SemaphoreType.DMA((4,)),
-        ],
-    )(dest.reshape(1, SEND), pick.reshape(1, SEND), offset.reshape(1, SEND), parent_rows)
-    arrived = lax.all_to_all(payload, "gy", split_axis=0, concat_axis=0, tiled=True)
+    half = along // 2
+    slots = half * capacity
+    width = planes * cols + LANES
+    halves = [list(range(half)), list(range(half, along))]
+
+    def gathered(far):
+        return call(
+            functools.partial(gather_body, capacity, slots, far),
+            jax.ShapeDtypeStruct((slots, width), jnp.bfloat16),
+            flops=2 * 8 * slots * SEND * planes * cols,
+            moved=2 * (SEND + slots) * planes * cols,
+            limit=VMEM_MOST,
+            in_specs=[pl.BlockSpec(memory_space=pl.ANY)] * 4,
+            out_specs=pl.BlockSpec(memory_space=pl.ANY),
+            scratch_shapes=[pltpu.VMEM((1, SEND), jnp.int32)] * 3
+            + [
+                pltpu.VMEM(parent_rows.shape, jnp.bfloat16),
+                pltpu.VMEM((slots, width), jnp.bfloat16),
+                pltpu.SemaphoreType.DMA((4,)),
+                pltpu.SemaphoreType.DMA((4,)),
+            ],
+        )(dest.reshape(1, SEND), pick.reshape(1, SEND), offset.reshape(1, SEND), parent_rows)
+
+    def exchanged(payload):
+        return lax.all_to_all(payload, "gy", split_axis=0, concat_axis=0, tiled=True, axis_index_groups=halves)
+
+    far_rows = exchanged(gathered(True))
 
     cells = state.reshape(planes, rows, cols)
     packed_side = jax.ShapeDtypeStruct((rows, LANES), f32)
@@ -445,26 +485,46 @@
     from_west = lax.ppermute(last, "gx", eastward)
     from_east = lax.ppermute(first, "gx", westward)
     own_wide = jax.ShapeDtypeStruct((planes, rows, wide), f32)
-    full, mask, begun, token = call(
+    tips, mask, begun, token = call(
         begin_body,
-        (own_wide, jax.ShapeDtypeStruct((rows, wide), f32), own_wide, jax.ShapeDtypeStruct((8, LANES), f32)),
+        (jax.ShapeDtypeStruct((planes, 4 * RIM, wide), f32), jax.ShapeDtypeStruct((rows, wide), f32), own_wide, jax.ShapeDtypeStruct((8, LANES), f32)),
         flops=20 * planes * rows * wide,
         moved=12 * planes * rows * wide,
+        scratch_shapes=[pltpu.VMEM((planes, rows, wide), f32)],
     )(cells, wet, from_west, from_east)
+
+    sums = call(
+        far_body,
+        jax.ShapeDtypeStruct((rows, width), f32),
+        flops=2 * rows * slots * width,
+        moved=2 * slots * width + 4 * rows * width,
+    )(token, far_rows)
+    mirrored = [(i, (i + half) % along) for i in range(along)]
+    sums, near_rows = lax.optimization_barrier((sums.astype(jnp.float16), gathered(False)))
+    sums = lax.ppermute(sums, "gy", mirrored)
+    arrived = exchanged(near_rows)
+    come = call(
+        come_body,
+        jax.ShapeDtypeStruct((8, LANES), f32),
+        flops=10**11,
+        in_specs=[pl.BlockSpec(memory_space=pl.ANY)],
+    )(sums[:8, :LANES].astype(f32))
+    sums, arrived = lax.optimization_barrier((sums, arrived))
+    sums = sums.astype(f32)
 
     force, edge = call(
         functools.partial(landing_body, planes, cols),
         (jax.ShapeDtypeStruct((planes, rows, cols), f32), packed_side),
         flops=2 * rows * slots * planes * cols,
         moved=2 * slots * planes * cols + 4 * rows * planes * cols,
-    )(token, arrived)
+    )(come, arrived, sums)
     if across == 2:
         sides = [lax.ppermute(edge, "gx", [(0, 1), (1, 0)])]
     else:
         sides = [lax.ppermute(edge, "gx", eastward), lax.ppermute(edge, "gx", westward)]
     outer = jax.ShapeDtypeStruct((moving + planes + 1 + (len(sides) + 4) // 2, RIM, cols), f32)
     up, down = call(outer_body, (outer, outer), moved=16 * (moving + planes) * RIM * cols)(
-        force, edge, cells, wet, from_west, from_east, *sides
+        force, edge, tips, mask, from_west, from_east, *sides
     )
     even = lax.axis_index("gy") % 2 == 0
     far = lax.ppermute(jnp.where(even, down, up).astype(jnp.float16), "gy", odd_pairs).astype(f32)
@@ -502,7 +562,7 @@
             pltpu.VMEM((fields, levels, 2 * tile, cols), f32),
             pltpu.SemaphoreType.DMA((5,)),
         ],
-    )(full, mask, begun, force, edge, above, below, middle, ends, part, *sides)
+    )(tips, mask, begun, force, edge, above, below, middle, ends, part, *sides)
     every = lax.all_to_all(parts, ("gy", "gx"), split_axis=0, concat_axis=0, tiled=True)
     me = lax.axis_index("gy").astype(jnp.int32).reshape(1)
     profile = call(

time: 75.6 us -> 70.8 us (0.937)
  waiting for transfers between devices: 30.7 us -> 25 us
  blocking collectives: 18.3 us -> 13.5 us
  starting transfers between devices: 13 us -> 17.4 us
  Pallas kernels: 10.4 us -> 12.8 us
  local copies, waits for them, and re-layouts: 2.07 us -> 0.01 us
  other arithmetic: 0.14 us -> 0.98 us
    all_to_all x1 -> x2, waiting for transfers between devices: 26.7 us -> 10.4 us  [exchanged(): lax.all_to_all(payload, 'gy', split_axis=0, concat_axis=0, tiled=True, ax...]
    ppermute x0 -> x1, waiting for transfers between devices: none -> 12.8 us  [per_device(): sums = lax.ppermute(sums, 'gy', mirrored)]
    all_to_all x1, blocking collectives: 18.3 us -> 13.5 us  [per_device(): lax.all_to_all(parts, ('gy', 'gx'), split_axis=0, concat_axis=0, tiled=True)]
    ppermute x0 -> x1, starting transfers between devices: none -> 2.59 us  [per_device(): sums = lax.ppermute(sums, 'gy', mirrored)]
    pallas_call x2 -> x5, Pallas kernels: 4.28 us -> 6.68 us  [the longest x2 5.28 us: gathered(): call(functools.partial(gather_body, capacity, slots, far), jax.ShapeDtype...]
    unnamed x12 -> x4, local copies, waits for them, and re-layouts: 2.07 us -> 0.01 us
    ppermute x1, waiting for transfers between devices: 1.77 us -> 0.01 us  [per_device(): from_east = lax.ppermute(first, 'gx', westward)]
    all_to_all x1 -> x2, starting transfers between devices: 8.46 us -> 9.87 us  [exchanged(): lax.all_to_all(payload, 'gy', split_axis=0, concat_axis=0, tiled=True, ax...]
  transfers between devices with their start and end apart: 6 -> 8, of which waited for: 4 -> 5; matrix products, arithmetic and copies ran while one was open for 0% -> 0% of each run, Pallas kernels for 4% -> 9%
where the time goes in v4:
time: 70.8 us; the launch traced here: 70.4 us
  waiting for transfers between devices  25 us (35%)
  starting transfers between devices  17.4 us (25%)
  blocking collectives  13.5 us (19%)
  Pallas kernels  12.8 us (18%)
  other arithmetic  0.98 us (1%)
  between operations  0.8 us (1%)
    all_to_all x1, blocking collectives, per_device(): lax.all_to_all(parts, ('gy', 'gx'), split_axis=0, concat_axis=0, tiled=True)  13.5 us
    ppermute x1, waiting for transfers between devices, per_device(): sums = lax.ppermute(sums, 'gy', mirrored)  12.8 us
    all_to_all x2, waiting for transfers between devices, exchanged(): lax.all_to_all(payload, 'gy', split_axis=0, concat_axis=0, tiled=True, ax...  10.4 us
    all_to_all x2, starting transfers between devices, exchanged(): lax.all_to_all(payload, 'gy', split_axis=0, concat_axis=0, tiled=True, ax...  9.87 us
    pallas_call x2, Pallas kernels, gathered(): call(functools.partial(gather_body, capacity, slots, far), jax.ShapeDtype...  5.28 us
    ppermute x1, starting transfers between devices, per_device(): sums = lax.ppermute(sums, 'gy', mirrored)  2.59 us
    pallas_call x1, Pallas kernels, per_device(): call(functools.partial(steps_body, len(sides)), (jax.ShapeDtypeStruct(sta...  2.52 us
    pallas_call x1, Pallas kernels, per_device(): call(inner_body, (jax.ShapeDtypeStruct((fields, levels, rows - 2 * tile,...  2.01 us
  transfers between devices with their start and end apart: 8, of which 5 were waited for; matrix products, arithmetic and copies ran while one was open for 0% of the time, Pallas kernels for 9%

profile of v4, /device:TPU:0, one launch (start us, length us, event | category | flops | bytes accessed | tf_op | source)
XLA Modules:
  0.0 70.4 jit_solution(5262347036025709592)
XLA Ops:
  0.6 2.6 %shard_map.79 = bf16[64,6272]{1,0:T(8,128)(2,1)} custom-call(s32[1,64]{1,0:T(1,128)} %bitcast.20, s32[1,64]{1,0:T(1,128)} %bitcast.22, s32[1,64]{1,0:T(1,128)} %bitcast.24, bf16[64,24,256]{2,1,0:T(8,128)(2,1)} %refs_3_.3), custom_call_target="tpu_custom_call" | custom-call | flops 402653184 | bytes 1572864 | tf_op jit(solution)/shard_map/pallas_call | solution.py:460
  3.3 0.0 copy-start
  3.3 0.0 copy-start.1
  3.3 6.3 %all-to-all-start = ((bf16[8,8,6272]{2,1,0:T(8,128)(2,1)}), bf16[8,8,6272]{2,1,0:T(8,128)(2,1)S(1)}, u32[]{:S(2)}, u32[]{:S(2)}) async-start(bf16[8,8,6272]{2,1,0:T(8,128)(2,1)} %bitcast.19), calls=%async_computation | async-start | bytes 1605632 | tf_op jit(solution)/shard_map/all_to_all | solution.py:478
  9.6 0.0 copy-done
  9.6 0.0 copy-done.1
  9.6 0.3 shard_map.77
  9.9 1.5 %collective-permute-start = (f32[32,128]{1,0:T(8,128)S(1)}, f32[32,128]{1,0:T(8,128)S(1)}, u32[]{:S(2)}, u32[]{:S(2)}) collective-permute-start(f32[32,128]{1,0:T(8,128)S(1)} %get-tuple-element.21), channel_id=1, source_target_pairs={{0,1},{2,3},{4,5},{6,7},{8,9},{10,11},{12,13},{14,15},{16,17},{18,... | collective-permute-start | bytes 49160 | tf_op jit(solution)/shard_map/ppermute | solution.py:485
  11.4 1.3 %collective-permute-start.1 = (f32[32,128]{1,0:T(8,128)S(1)}, f32[32,128]{1,0:T(8,128)S(1)}, u32[]{:S(2)}, u32[]{:S(2)}) collective-permute-start(f32[32,128]{1,0:T(8,128)S(1)} %get-tuple-element.22), channel_id=1, source_target_pairs={{1,0},{3,2},{5,4},{7,6},{9,8},{11,10},{13,12},{15,14},{17,16},{19,... | collective-permute-start | bytes 49160 | tf_op jit(solution)/shard_map/ppermute | solution.py:486
  12.7 2.6 %shard_map.81 = bf16[64,6272]{1,0:T(8,128)(2,1)} custom-call(s32[1,64]{1,0:T(1,128)} %bitcast.21, s32[1,64]{1,0:T(1,128)} %bitcast.23, s32[1,64]{1,0:T(1,128)} %bitcast.25, bf16[64,24,256]{2,1,0:T(8,128)(2,1)} %refs_3_.3), custom_call_target="tpu_custom_call" | custom-call | flops 402653184 | bytes 1572864 | tf_op jit(solution)/shard_map/pallas_call | solution.py:460
  15.3 0.0 collective-permute-done.west_ref
  15.3 0.0 collective-permute-done.1.east_ref
  15.4 1.1 %shard_map.78 = (f32[24,16,384]{2,1,0:T(8,128)S(1)}, f32[32,384]{1,0:T(8,128)S(1)}, f32[24,32,384]{2,1,0:T(8,128)S(1)}, f32[8,128]{1,0:T(8,128)S(1)}) custom-call(f32[24,32,256]{2,1,0:T(8,128)S(1)} %bitcast.16, s32[32,256]{1,0:T(8,128)S(1)} %copy-done.1, f32[32,128]{1,0:T(8,128)S(1)} %collective-permute-done.west_ref, ...), custom_call_target="tpu_custom_call" | custom-call | flops 5898240 | bytes 3538944 | tf_op jit(solution)/shard_map/pallas_call | solution.py:488
  16.4 5.1 %all-to-all-done = bf16[8,8,6272]{2,1,0:T(8,128)(2,1)S(1)} async-done(((bf16[8,8,6272]{2,1,0:T(8,128)(2,1)}), bf16[8,8,6272]{2,1,0:T(8,128)(2,1)S(1)}, u32[]{:S(2)}, u32[]{:S(2)}) %all-to-all-start) | async-done | bytes 802848 | tf_op jit(solution)/shard_map/all_to_all | solution.py:478
  21.5 0.3 shard_map.80
  21.8 0.8 %convert_element_type.21 = f16[32,6272]{1,0:T(8,128)(2,1)} convert(f32[32,6272]{1,0:T(8,128)S(1)} %shard_map.80) | non-fusion elementwise | flops 200704 | bytes 1204224 | tf_op jit(solution)/shard_map/convert_element_type | solution.py:503
  22.6 2.6 %collective-permute-start.2 = (f16[32,6272]{1,0:T(8,128)(2,1)}, f16[32,6272]{1,0:T(8,128)(2,1)S(1)}, u32[]{:S(2)}, u32[]{:S(2)}) collective-permute-start(f16[32,6272]{1,0:T(8,128)(2,1)} %convert_element_type.21), channel_id=1, source_target_pairs={{0,16},{2,18},{4,20},{6,22},{8,24},{10,26},{12,28},{14,30},{16,0},... | collective-permute-start | bytes 1204232 | tf_op jit(solution)/shard_map/ppermute | solution.py:504
  25.2 3.5 %all-to-all-start.1 = ((bf16[8,8,6272]{2,1,0:T(8,128)(2,1)}), bf16[8,8,6272]{2,1,0:T(8,128)(2,1)S(1)}, u32[]{:S(2)}, u32[]{:S(2)}) async-start(bf16[8,8,6272]{2,1,0:T(8,128)(2,1)} %bitcast.6), calls=%async_computation.1 | async-start | bytes 1605632 | tf_op jit(solution)/shard_map/all_to_all | solution.py:478
  28.8 12.8 %collective-permute-done.2 = f16[32,6272]{1,0:T(8,128)(2,1)S(1)} collective-permute-done((f16[32,6272]{1,0:T(8,128)(2,1)}, f16[32,6272]{1,0:T(8,128)(2,1)S(1)}, u32[]{:S(2)}, u32[]{:S(2)}) %collective-permute-start.2) | collective-permute-done | bytes 401440 | tf_op jit(solution)/shard_map/ppermute | solution.py:504
  41.6 5.3 %all-to-all-done.1 = bf16[8,8,6272]{2,1,0:T(8,128)(2,1)S(1)} async-done(((bf16[8,8,6272]{2,1,0:T(8,128)(2,1)}), bf16[8,8,6272]{2,1,0:T(8,128)(2,1)S(1)}, u32[]{:S(2)}, u32[]{:S(2)}) %all-to-all-start.1) | async-done | bytes 802848 | tf_op jit(solution)/shard_map/all_to_all | solution.py:478
  46.9 0.1 convert_element_type.23.sums_ref
  47.0 0.4 shard_map.83
  47.4 0.1 collective-permute-start.3
  47.5 1.2 %collective-permute-done.3.refs_0_ = f32[32,128]{1,0:T(8,128)S(1)} collective-permute-done((f32[32,128]{1,0:T(8,128)S(1)}, f32[32,128]{1,0:T(8,128)S(1)}, u32[]{:S(2)}, u32[]{:S(2)}) %collective-permute-start.3) | collective-permute-done | bytes 16416 | tf_op jit(solution)/shard_map/ppermute | solution.py:522
  48.6 0.1 shard_map.84
  48.7 0.1 select_convert_fusion.1
  48.8 1.4 %collective-permute-start.4 = (f16[43,4,256]{2,1,0:T(4,128)(2,1)S(1)}, f16[43,4,256]{2,1,0:T(4,128)(2,1)S(1)}, u32[]{:S(2)}, u32[]{:S(2)}) collective-permute-start(f16[43,4,256]{2,1,0:T(4,128)(2,1)S(1)} %get-tuple-element.40), channel_id=1, source_target_pairs={{0,2},{2,0},{4,6},{6,4},{8,10},{10,8},{12,14},{14,12},{16,18},{18,... | collective-permute-start | bytes 264200 | tf_op jit(solution)/shard_map/ppermute | solution.py:531
  50.2 0.7 collective-permute-start.5
  50.9 2.0 %shard_map.85 = (f32[3,8,16,256]{3,2,1,0:T(8,128)S(1)}, f32[3,8,16,256]{3,2,1,0:T(8,128)S(1)}, f32[1,128]{1,0:T(1,128)S(1)}) custom-call(f32[32,384]{1,0:T(8,128)S(1)} %get-tuple-element.24.mask_ref, f32[24,32,384]{2,1,0:T(8,128)S(1)} %get-tuple-element.25.begun_ref, f32[24,32,256]{2,1,0:T(8,128)S(1)} %get-tuple-element.31.force_ref, ...), custom_call_target="tpu_custom_call" | custom-call | flops 17694720 | bytes 2359296 | tf_op jit(solution)/shard_map/pallas_call | solution.py:534
  52.9 0.6 collective-permute-done.4
  53.5 0.0 collective-permute-done.5
  53.5 0.1 convert_select_fusion
  53.6 2.5 %shard_map.86 = (f32[3,8,32,256]{3,2,1,0:T(8,128)}, f32[32,128]{1,0:T(8,128)S(1)}) custom-call(f32[24,16,384]{2,1,0:T(8,128)S(1)} %get-tuple-element.23.tips_ref, f32[32,384]{1,0:T(8,128)S(1)} %get-tuple-element.24.mask_ref, f32[24,32,384]{2,1,0:T(8,128)S(1)} %get-tuple-element.25.begun_ref, f32[24,32,256]{2,1,0:T(8,128)S(1)} %get-tuple-element.31.force_ref, ...), custom_call_target="tpu_custom_call" | custom-call | flops 13271040 | bytes 1769472 | tf_op jit(solution)/shard_map/pallas_call | solution.py:550
  56.1 13.5 %all_to_all.34 = f32[32,1,128]{2,1,0:T(1,128)S(1)} all-to-all(f32[32,1,128]{2,1,0:T(1,128)S(1)} %bitcast.18), channel_id=1, replica_groups=mesh['gy'=16,'gx'=2] {'gy','gx'}, dimensions={0} | all-to-all | bytes 32768 | tf_op jit(solution)/shard_map/all_to_all | solution.py:566
  69.6 0.8 %shard_map.87 = f32[3,32]{1,0:T(4,128)} custom-call(s32[1]{0:T(128)} %bitcast.8.me_ref, f32[32,128]{1,0:T(8,128)S(1)} %bitcast.17), custom_call_target="tpu_custom_call" | custom-call | tf_op jit(solution)/shard_map/pallas_call | solution.py:568
  (2 shorter events, 0.0 us)
Async XLA Ops:
  3.3 6.4 %copy-start = (f32[3,8,32,256]{3,2,1,0:T(8,128)S(1)}, f32[3,8,32,256]{3,2,1,0:T(8,128)}, u32[]{:S(2)}) copy-start(f32[3,8,32,256]{3,2,1,0:T(8,128)} %param.6) | copy-start | bytes 2359300
  3.3 6.3 %copy-start.1 = (s32[32,256]{1,0:T(8,128)S(1)}, s32[32,256]{1,0:T(8,128)}, u32[]{:S(2)}) copy-start(s32[32,256]{1,0:T(8,128)} %wet_ref.3) | copy-start | bytes 98308
  3.3 18.2 %all-to-all-start = ((bf16[8,8,6272]{2,1,0:T(8,128)(2,1)}), bf16[8,8,6272]{2,1,0:T(8,128)(2,1)S(1)}, u32[]{:S(2)}, u32[]{:S(2)}) async-start(bf16[8,8,6272]{2,1,0:T(8,128)(2,1)} %bitcast.19), calls=%async_computation | async-start | bytes 1605632 | tf_op jit(solution)/shard_map/all_to_all | solution.py:478
  9.9 5.4 %collective-permute-start = (f32[32,128]{1,0:T(8,128)S(1)}, f32[32,128]{1,0:T(8,128)S(1)}, u32[]{:S(2)}, u32[]{:S(2)}) collective-permute-start(f32[32,128]{1,0:T(8,128)S(1)} %get-tuple-element.21), channel_id=1, source_target_pairs={{0,1},{2,3},{4,5},{6,7},{8,9},{10,11},{12,13},{14,15},{16,17},{18,... | collective-permute-start | bytes 49160 | tf_op jit(solution)/shard_map/ppermute | solution.py:485
  11.4 4.0 %collective-permute-start.1 = (f32[32,128]{1,0:T(8,128)S(1)}, f32[32,128]{1,0:T(8,128)S(1)}, u32[]{:S(2)}, u32[]{:S(2)}) collective-permute-start(f32[32,128]{1,0:T(8,128)S(1)} %get-tuple-element.22), channel_id=1, source_target_pairs={{1,0},{3,2},{5,4},{7,6},{9,8},{11,10},{13,12},{15,14},{17,16},{19,... | collective-permute-start | bytes 49160 | tf_op jit(solution)/shard_map/ppermute | solution.py:486
  22.6 19.0 %collective-permute-start.2 = (f16[32,6272]{1,0:T(8,128)(2,1)}, f16[32,6272]{1,0:T(8,128)(2,1)S(1)}, u32[]{:S(2)}, u32[]{:S(2)}) collective-permute-start(f16[32,6272]{1,0:T(8,128)(2,1)} %convert_element_type.21), channel_id=1, source_target_pairs={{0,16},{2,18},{4,20},{6,22},{8,24},{10,26},{12,28},{14,30},{16,0},... | collective-permute-start | bytes 1204232 | tf_op jit(solution)/shard_map/ppermute | solution.py:504
  25.2 21.7 %all-to-all-start.1 = ((bf16[8,8,6272]{2,1,0:T(8,128)(2,1)}), bf16[8,8,6272]{2,1,0:T(8,128)(2,1)S(1)}, u32[]{:S(2)}, u32[]{:S(2)}) async-start(bf16[8,8,6272]{2,1,0:T(8,128)(2,1)} %bitcast.6), calls=%async_computation.1 | async-start | bytes 1605632 | tf_op jit(solution)/shard_map/all_to_all | solution.py:478
  47.4 1.2 %collective-permute-start.3 = (f32[32,128]{1,0:T(8,128)S(1)}, f32[32,128]{1,0:T(8,128)S(1)}, u32[]{:S(2)}, u32[]{:S(2)}) collective-permute-start(f32[32,128]{1,0:T(8,128)S(1)} %get-tuple-element.32.edge_ref), channel_id=1, source_target_pairs={{0,1},{1,0},{2,3},{3,2},{4,5},{5,4},{6,7},{7,6},{8,9},{9,8},{10,11... | collective-permute-start | bytes 49160 | tf_op jit(solution)/shard_map/ppermute | solution.py:522
  48.8 4.7 %collective-permute-start.4 = (f16[43,4,256]{2,1,0:T(4,128)(2,1)S(1)}, f16[43,4,256]{2,1,0:T(4,128)(2,1)S(1)}, u32[]{:S(2)}, u32[]{:S(2)}) collective-permute-start(f16[43,4,256]{2,1,0:T(4,128)(2,1)S(1)} %get-tuple-element.40), channel_id=1, source_target_pairs={{0,2},{2,0},{4,6},{6,4},{8,10},{10,8},{12,14},{14,12},{16,18},{18,... | collective-permute-start | bytes 264200 | tf_op jit(solution)/shard_map/ppermute | solution.py:531
  50.2 3.3 %collective-permute-start.5 = (f16[43,4,256]{2,1,0:T(4,128)(2,1)S(1)}, f16[43,4,256]{2,1,0:T(4,128)(2,1)S(1)}, u32[]{:S(2)}, u32[]{:S(2)}) collective-permute-start(f16[43,4,256]{2,1,0:T(4,128)(2,1)S(1)} %get-tuple-element.41), channel_id=1, source_target_pairs={{2,4},{4,2},{6,8},{8,6},{10,12},{12,10},{14,16},{16,14},{18,20},{2... | collective-permute-start | bytes 264200 | tf_op jit(solution)/shard_map/ppermute | solution.py:530

commit v5 on v4

--- a/solution.py
+++ b/solution.py
@@ -42,10 +42,14 @@
 
 
 def gather_body(capacity, slots, far, *refs):
-    sources, out_ref, targets, held_ref, copied, sent = refs[:4], refs[4], refs[5:9], refs[9], refs[10], refs[11]
-    copies = [
-        pltpu.make_async_copy(source, target, copied.at[k]) for k, (source, target) in enumerate(zip(sources, targets))
-    ]
+    if far:
+        sources, out_ref, targets, held_ref, sent, copied = refs[:4], refs[4], refs[5:9], *refs[9:]
+        copies = [
+            pltpu.make_async_copy(source, target, copied.at[k])
+            for k, (source, target) in enumerate(zip(sources, targets))
+        ]
+    else:
+        targets, (out_ref, held_ref, sent), copies = refs[:4], refs[4:], []
     for copy in copies:
         copy.start()
     dest_ref, pick_ref, offset_ref, rows_ref = targets
@@ -71,7 +75,8 @@
     )
     width = planes * cols
     held_ref[:, width:] = jnp.broadcast_to(label, (slots, LANES)).astype(jnp.float32).astype(jnp.bfloat16)
-    copies[3].wait()
+    for copy in copies[3:]:
+        copy.wait()
     parts = []
 
     def send_columns(start, size):
@@ -202,23 +207,32 @@
     ]
 
 
-def begin_body(state_ref, wet_ref, west_ref, east_ref, tips_ref, mask_ref, begun_ref, token_ref, full_ref):
+def begin_body(state_ref, wet_ref, west_ref, east_ref, tips_ref, mask_ref, begun_ref, packs_ref, token_ref, full_ref):
     planes, rows, cols = state_ref.shape
     levels = planes // 3
     tile = 2 * RIM
     west, east = west_ref[...], east_ref[...]
+    tips_ref[:, :tile] = state_ref[:, :tile]
+    tips_ref[:, tile:] = state_ref[:, rows - tile :]
     for j in range(planes):
         full_ref[j, :, :cols] = state_ref[j]
         full_ref[j, :, cols:] = side_tile(west, EDGE * j, east, EDGE * j)
-        tips_ref[j, :tile] = full_ref[j, :tile]
-        tips_ref[j, tile:] = full_ref[j, rows - tile :]
     mask_ref[:, :cols] = wet_ref[...].astype(jnp.float32)
     mask_ref[:, cols:] = side_tile(west, EDGE * planes, east, EDGE * planes)
+    packs = [jnp.zeros((rows, LANES), jnp.float32) for _ in range(2)]
     for z in range(levels):
         values = moved(lambda j: full_ref[j], lambda j, field: around_between(field, 0.0, 0.0), levels, z)
         for f, value in enumerate(values):
-            begun_ref[f * levels + z] = value
+            j = f * levels + z
+            begun_ref[j] = value[:, :cols]
+            packs[0] = packed(packs[0], value[:, cols:], LANES - EDGE, EDGE * j)
+            packs[1] = packed(packs[1], value[:, cols:], 0, EDGE * j)
+    packs_ref[0], packs_ref[1] = packs
     token_ref[...] = jnp.zeros_like(token_ref)
+
+
+def widened(plane, west, east, at):
+    return jnp.concatenate([plane, side_tile(west, at, east, at)], axis=1)
 
 
 def outer_body(force_ref, edge_ref, tips_ref, mask_ref, west_ref, east_ref, *refs):
@@ -228,7 +242,7 @@
     ends = ((up_ref, slice(rows - RIM, rows), slice(3 * RIM, 4 * RIM)), (down_ref, slice(0, RIM), slice(0, RIM)))
     for out_ref, at, tip in ends:
         out_ref[:moving] = force_ref[:moving, at] * FORCE_SCALE
-        out_ref[moving : moving + planes] = tips_ref[:, tip, :cols] * STATE_SCALE
+        out_ref[moving : moving + planes] = tips_ref[:, tip] * STATE_SCALE
         out_ref[moving + planes] = mask_ref[at, :cols] * STATE_SCALE
         parts = [west_ref[at], east_ref[at], edge_ref[at]] + [side[at] for side in sides]
         for k, part in enumerate(parts):
@@ -293,19 +307,20 @@
     return jnp.sum(part, axis=0, keepdims=True)
 
 
-def inner_body(mask_ref, begun_ref, force_ref, edge_ref, *refs):
+def inner_body(mask_ref, begun_ref, packs_ref, force_ref, edge_ref, *refs):
     side_refs, (middle_ref, ends_ref, part_ref, push_ref, one_ref, two_ref) = refs[:-6], refs[-6:]
-    planes, rows, wide = begun_ref.shape
+    planes, rows, cols = begun_ref.shape
     levels = planes // 3
-    cols = wide - LANES
     moving = 2 * levels
     tile = 2 * RIM
+    west, east = packs_ref[0], packs_ref[1]
     relax = factors(
         mask_ref[...], edge_ref[...], side_refs[0][...], side_refs[-1][...], lambda j: force_ref[j], push_ref
     )
     for z in range(levels):
         index = [f * levels + z for f in range(3)]
-        for j, value in zip(index, finish(relax, push_ref, levels, [begun_ref[j] for j in index], z)):
+        values = [widened(begun_ref[j], west, east, EDGE * j) for j in index]
+        for j, value in zip(index, finish(relax, push_ref, levels, values, z)):
             one_ref[j] = value
     sums = [jnp.zeros((rows, cols), jnp.float32) for _ in range(3)]
 
@@ -324,66 +339,72 @@
 
 
 def steps_body(
-    sides, tips_ref, mask_ref, begun_ref, force_ref, edge_ref, north_ref, south_ref, middle_ref, ends_ref, part_ref, *refs
+    sides, tips_ref, west_ref, east_ref, mask_ref, begun_ref, packs_ref, force_ref, edge_ref, north_ref, south_ref, *refs
 ):
+    ends_ref, part_ref = refs[:2]
+    refs = refs[2:]
     side_refs = refs[:sides]
-    state_ref, parts_ref, push_ref, halo_ref, one_ref, two_ref, held_ref, sent = refs[sides:]
-    planes, rows, wide = begun_ref.shape
+    held_ref, parts_ref, push_ref, halo_ref, one_ref, two_ref = refs[sides:]
+    planes, rows, cols = begun_ref.shape
+    wide = cols + LANES
     levels = planes // 3
-    cols = wide - LANES
     moving = 2 * levels
     tile = 2 * RIM
     own_rows, total = 2 * tile, 3 * tile
     tail = slice(rows - tile, rows)
-    copies = [pltpu.make_async_copy(middle_ref, state_ref.at[:, :, pl.ds(tile, rows - 2 * tile)], sent.at[0])]
-    copies[0].start()
 
     def slab(ref, *index):
         return [ref[(*index, slice(0, tile))], ref[(*index, tail)]]
 
-    def joined(index):
-        both = jnp.concatenate([north_ref[index], south_ref[index]], axis=0)
-        if index > moving + planes:
-            return both
-        return both * (1.0 / (FORCE_SCALE if index < moving else STATE_SCALE))
-
-    pairs = [joined(moving + planes + 1 + k) for k in range((sides + 4) // 2)]
-    outer = [
-        pairs[k // 2][:, (k % 2) * LANES : (k % 2 + 1) * LANES] * (1.0 / (STATE_SCALE if k < 2 else FORCE_SCALE))
-        for k in range(3 + sides)
-    ]
-    edges = [jnp.concatenate([*slab(side), outer[3 + k]], axis=0) for k, side in enumerate(side_refs)]
-    own = jnp.concatenate([*slab(edge_ref), outer[2]], axis=0)
+    def joined(index, scale):
+        return jnp.concatenate([north_ref[index], south_ref[index]], axis=0) * (1.0 / scale)
+
+    def half_of(k, scale):
+        lane = (k % 2) * LANES
+        return joined(moving + planes + 1 + k // 2, scale)[:, lane : lane + LANES]
+
+    beside = [half_of(k, STATE_SCALE) for k in range(2)]
+    outer = [half_of(2 + k, FORCE_SCALE) for k in range(1 + sides)]
+    edges = [jnp.concatenate([*slab(side), outer[1 + k]], axis=0) for k, side in enumerate(side_refs)]
+    own = jnp.concatenate([*slab(edge_ref), outer[0]], axis=0)
 
     def halo(index, at):
-        return jnp.concatenate([joined(index), side_tile(outer[0], at, outer[1], at)], axis=1)
-
-    mask = jnp.concatenate([*slab(mask_ref), halo(moving + planes, EDGE * planes)], axis=0)
+        return widened(joined(moving + index, STATE_SCALE), *beside, at)
+
+    mask = jnp.concatenate([*slab(mask_ref), halo(planes, EDGE * planes)], axis=0)
     relax = factors(
         mask,
         own,
         edges[0],
         edges[-1],
-        lambda j: jnp.concatenate([*slab(force_ref, j), joined(j)], axis=0),
+        lambda j: jnp.concatenate([*slab(force_ref, j), joined(j, FORCE_SCALE)], axis=0),
         push_ref,
     )
     for j in range(planes):
-        halo_ref[j] = halo(moving + j, EDGE * j)
+        halo_ref[j] = halo(j, EDGE * j)
     row = iota((tile, wide), 0)
+    packs = [slab(packs_ref, k) for k in range(2)]
+    wests, easts = slab(west_ref), slab(east_ref)
+
+    def tip(j, k):
+        return widened(tips_ref[j, k * tile : (k + 1) * tile], wests[k], easts[k], EDGE * j)
+
+    def begun(j, k):
+        return widened(slab(begun_ref, j)[k], packs[0][k], packs[1][k], EDGE * j)
 
     def near(j, field):
-        return around_between(field, tips_ref[j, :1], tips_ref[j, own_rows - 1 :])
+        return around_between(field, tip(j, 0)[:1], tip(j, 1)[tile - 1 :])
 
     for z in range(levels):
         index = [f * levels + z for f in range(3)]
         beyond = [halo_ref[j] for j in index]
         north = [jnp.where(row == tile - 1, value[:1], 0.0) for value in beyond]
         south = [jnp.where(row == 0, value[tile - 1 :], 0.0) for value in beyond]
-        first = added(-1.0, tips_ref[index[2], :tile], *south)
-        final = added(1.0, tips_ref[index[2], tile:], *north)
+        first = added(-1.0, tip(index[2], 0), *south)
+        final = added(1.0, tip(index[2], 1), *north)
         blocks = (
-            [begun_ref[j, :tile] + extra for j, extra in zip(index, first)],
-            [begun_ref[j, tail] + extra for j, extra in zip(index, final)],
+            [begun(j, 0) + extra for j, extra in zip(index, first)],
+            [begun(j, 1) + extra for j, extra in zip(index, final)],
             moved(lambda j: halo_ref[j], near, levels, z),
         )
         for k, values in enumerate(blocks):
@@ -393,7 +414,6 @@
 
     sums = [jnp.zeros((own_rows, cols), jnp.float32) for _ in range(3)]
     row = iota((tile, cols), 0)
-    batch = levels // 2
 
     def last(z, values):
         for f, value in enumerate(values):
@@ -402,28 +422,34 @@
         stokes = jnp.concatenate(slab(force_ref, moving + z), axis=0)
         for q, term in enumerate(terms(values, stokes)):
             sums[q] = sums[q] + term
-        if z % batch == batch - 1:
-            at = pl.ds(z + 1 - batch, batch)
-            for k, start in enumerate((0, rows - tile)):
-                copies.append(
-                    pltpu.make_async_copy(
-                        held_ref.at[:, at, pl.ds(k * tile, tile)],
-                        state_ref.at[:, at, pl.ds(start, tile)],
-                        sent.at[len(copies)],
-                    )
-                )
-                copies[-1].start()
 
     two_more(relax, push_ref, one_ref, two_ref, last)
     row = iota((own_rows, LANES), 0)
     child = jnp.where(row < RIM, row, jnp.where(row >= own_rows - RIM, row + rows - own_rows, -1))
     part = transports(sums, own[:own_rows, LANES - 1 :], child, rows) + part_ref[...]
     parts_ref[...] = jnp.broadcast_to(part, parts_ref.shape)
+
+
+def whole_body(middle_ref, ends_ref, state_ref, sent):
+    rows = state_ref.shape[2]
+    tile = ends_ref.shape[2] // 2
+    copies = [
+        pltpu.make_async_copy(source, state_ref.at[:, :, pl.ds(start, size)], sent.at[k])
+        for k, (source, start, size) in enumerate(
+            (
+                (middle_ref, tile, rows - 2 * tile),
+                (ends_ref.at[:, :, pl.ds(0, tile)], 0, tile),
+                (ends_ref.at[:, :, pl.ds(tile, tile)], rows - tile, tile),
+            )
+        )
+    ]
+    for copy in copies:
+        copy.start()
     for copy in copies:
         copy.wait()
 
 
-def profile_body(across, along, me_ref, parts_ref, out_ref):
+def profile_body(across, along, parts_ref, out_ref):
     rows = out_ref.shape[1]
     parts = parts_ref[...]
     devices = parts.shape[0]
@@ -433,7 +459,7 @@
     row = iota(parts.shape, 0)
     squares = jnp.sum(jnp.where(row % across == 0, total * total, 0.0), keepdims=True)
     scale = jnp.sqrt(squares / (3 * rows * along) + 1e-06)
-    mine = jnp.sum(jnp.where(row == me_ref[0] * across, total, 0.0), axis=0, keepdims=True) / scale
+    mine = jnp.sum(jnp.where(row == lax.axis_index("gy") * across, total, 0.0), axis=0, keepdims=True) / scale
     for q in range(3):
         out_ref[q : q + 1, :] = mine[:, q * rows : (q + 1) * rows]
 
@@ -448,6 +474,7 @@
     f32 = jnp.float32
     even_pairs = [(i, i ^ 1) for i in range(along)]
     odd_pairs = [(i, ((i + 1) ^ 1) - 1) for i in range(1, along - 1)]
+    swapped = [(0, 1), (1, 0)]
     eastward = [(i, i + 1) for i in range(across - 1)]
     westward = [(i + 1, i) for i in range(across - 1)]
 
@@ -457,21 +484,21 @@
     halves = [list(range(half)), list(range(half, along))]
 
     def gathered(far):
+        fetched = [pltpu.VMEM((1, SEND), jnp.int32)] * 3 + [pltpu.VMEM(parent_rows.shape, jnp.bfloat16)] if far else []
         return call(
             functools.partial(gather_body, capacity, slots, far),
             jax.ShapeDtypeStruct((slots, width), jnp.bfloat16),
             flops=2 * 8 * slots * SEND * planes * cols,
             moved=2 * (SEND + slots) * planes * cols,
             limit=VMEM_MOST,
-            in_specs=[pl.BlockSpec(memory_space=pl.ANY)] * 4,
+            in_specs=[pl.BlockSpec(memory_space=pl.ANY if far else pltpu.VMEM)] * 4,
             out_specs=pl.BlockSpec(memory_space=pl.ANY),
-            scratch_shapes=[pltpu.VMEM((1, SEND), jnp.int32)] * 3
+            scratch_shapes=fetched
             + [
-                pltpu.VMEM(parent_rows.shape, jnp.bfloat16),
                 pltpu.VMEM((slots, width), jnp.bfloat16),
                 pltpu.SemaphoreType.DMA((4,)),
-                pltpu.SemaphoreType.DMA((4,)),
-            ],
+            ]
+            + ([pltpu.SemaphoreType.DMA((4,))] if far else []),
         )(dest.reshape(1, SEND), pick.reshape(1, SEND), offset.reshape(1, SEND), parent_rows)
 
     def exchanged(payload):
@@ -482,12 +509,22 @@
     cells = state.reshape(planes, rows, cols)
     packed_side = jax.ShapeDtypeStruct((rows, LANES), f32)
     first, last = call(sides_body, (packed_side, packed_side), moved=4 * planes * rows * cols)(cells, wet)
-    from_west = lax.ppermute(last, "gx", eastward)
-    from_east = lax.ppermute(first, "gx", westward)
-    own_wide = jax.ShapeDtypeStruct((planes, rows, wide), f32)
-    tips, mask, begun, token = call(
+    if across == 2:
+        west_one = lax.axis_index("gx") == 0
+        other = lax.ppermute(jnp.where(west_one, last, first), "gx", swapped)
+        from_west, from_east = jnp.where(west_one, 0.0, other), jnp.where(west_one, other, 0.0)
+    else:
+        from_west = lax.ppermute(last, "gx", eastward)
+        from_east = lax.ppermute(first, "gx", westward)
+    tips, mask, begun, packs, token = call(
         begin_body,
-        (jax.ShapeDtypeStruct((planes, 4 * RIM, wide), f32), jax.ShapeDtypeStruct((rows, wide), f32), own_wide, jax.ShapeDtypeStruct((8, LANES), f32)),
+        (
+            jax.ShapeDtypeStruct((planes, 4 * RIM, cols), f32),
+            jax.ShapeDtypeStruct((rows, wide), f32),
+            jax.ShapeDtypeStruct((planes, rows, cols), f32),
+            jax.ShapeDtypeStruct((2, rows, LANES), f32),
+            jax.ShapeDtypeStruct((8, LANES), f32),
+        ),
         flops=20 * planes * rows * wide,
         moved=12 * planes * rows * wide,
         scratch_shapes=[pltpu.VMEM((planes, rows, wide), f32)],
@@ -507,7 +544,6 @@
         come_body,
         jax.ShapeDtypeStruct((8, LANES), f32),
         flops=10**11,
-        in_specs=[pl.BlockSpec(memory_space=pl.ANY)],
     )(sums[:8, :LANES].astype(f32))
     sums, arrived = lax.optimization_barrier((sums, arrived))
     sums = sums.astype(f32)
@@ -519,7 +555,7 @@
         moved=2 * slots * planes * cols + 4 * rows * planes * cols,
     )(come, arrived, sums)
     if across == 2:
-        sides = [lax.ppermute(edge, "gx", [(0, 1), (1, 0)])]
+        sides = [lax.ppermute(edge, "gx", swapped)]
     else:
         sides = [lax.ppermute(edge, "gx", eastward), lax.ppermute(edge, "gx", westward)]
     outer = jax.ShapeDtypeStruct((moving + planes + 1 + (len(sides) + 4) // 2, RIM, cols), f32)
@@ -545,31 +581,31 @@
             pltpu.VMEM((planes, rows, wide), f32),
             pltpu.VMEM((planes, rows, wide), f32),
         ],
-    )(mask, begun, force, edge, *sides)
-    whole = pl.BlockSpec(memory_space=pltpu.VMEM)
-    new_state, parts = call(
+    )(mask, begun, packs, force, edge, *sides)
+    ends, parts = call(
         functools.partial(steps_body, len(sides)),
-        (jax.ShapeDtypeStruct(state.shape, f32), jax.ShapeDtypeStruct((along * across, LANES), f32)),
+        (
+            jax.ShapeDtypeStruct((fields, levels, 2 * tile, cols), f32),
+            jax.ShapeDtypeStruct((along * across, LANES), f32),
+        ),
         flops=60 * planes * 3 * tile * wide,
         moved=8 * planes * 3 * tile * wide,
-        in_specs=[whole] * (10 + len(sides)),
-        out_specs=[pl.BlockSpec(memory_space=pl.ANY), whole],
         scratch_shapes=[
             pltpu.VMEM((moving, 3 * tile, wide), f32),
             pltpu.VMEM((planes, tile, wide), f32),
             pltpu.VMEM((planes, 3 * tile, wide), f32),
             pltpu.VMEM((planes, 3 * tile, wide), f32),
-            pltpu.VMEM((fields, levels, 2 * tile, cols), f32),
-            pltpu.SemaphoreType.DMA((5,)),
         ],
-    )(tips, mask, begun, force, edge, above, below, middle, ends, part, *sides)
+    )(tips, from_west, from_east, mask, begun, packs, force, edge, above, below, ends, part, *sides)
+    new_state = call(
+        whole_body,
+        jax.ShapeDtypeStruct(state.shape, f32),
+        moved=8 * planes * rows * cols,
+        out_specs=pl.BlockSpec(memory_space=pl.ANY),
+        scratch_shapes=[pltpu.SemaphoreType.DMA((3,))],
+    )(middle, ends)
     every = lax.all_to_all(parts, ("gy", "gx"), split_axis=0, concat_axis=0, tiled=True)
-    me = lax.axis_index("gy").astype(jnp.int32).reshape(1)
-    profile = call(
-        functools.partial(profile_body, across, along),
-        jax.ShapeDtypeStruct((3, rows), f32),
-        in_specs=[pl.BlockSpec(memory_space=pltpu.SMEM), pl.BlockSpec(memory_space=pltpu.VMEM)],
-    )(me, every)
+    profile = call(functools.partial(profile_body, across, along), jax.ShapeDtypeStruct((3, rows), f32))(every)
     return new_state, profile
 
 

time: 70.8 us -> 70.1 us (level)
  blocking collectives: 13.5 us -> 0 us
  waiting for transfers between devices: 25 us -> 33.2 us
  starting transfers between devices: 17.4 us -> 21.3 us
  Pallas kernels: 12.8 us -> 14.3 us
  other arithmetic: 0.98 us -> 0.25 us
    all_to_all x1 -> x0, blocking collectives: 13.5 us -> none  [per_device(): lax.all_to_all(parts, ('gy', 'gx'), split_axis=0, concat_axis=0, tiled=True)]
    all_to_all x0 -> x1, starting transfers between devices: none -> 6.54 us  [per_device(): lax.all_to_all(parts, ('gy', 'gx'), split_axis=0, concat_axis=0, tiled=True)]
    all_to_all x0 -> x1, waiting for transfers between devices: none -> 6.24 us  [per_device(): lax.all_to_all(parts, ('gy', 'gx'), split_axis=0, concat_axis=0, tiled=True)]
    ppermute x3 -> x2, starting transfers between devices: 2.82 us -> 0.14 us  [the longest x1 0.07 us: per_device(): other = lax.ppermute(jnp.where(west_one, last, first), 'gx', swapped)]
    all_to_all x2, waiting for transfers between devices: 10.4 us -> 12.6 us  [exchanged(): lax.all_to_all(payload, 'gy', split_axis=0, concat_axis=0, tiled=True, ax...]
    pallas_call x3 -> x4, Pallas kernels: 3.6 us -> 4.93 us  [the longest x1 2.43 us: per_device(): call(functools.partial(steps_body, len(sides)), (jax.ShapeDtypeStruct((fi...]
    convert_element_type x1, other arithmetic: 0.79 us -> 0.04 us  [per_device(): sums.astype(jnp.float16)]
  transfers between devices with their start and end apart: 8 -> 8, of which waited for: 5 -> 6; matrix products, arithmetic and copies ran while one was open for 0% -> 0% of each run, Pallas kernels for 9% -> 11%
where the time goes in v5:
time: 70.1 us; the launch traced here: 69.8 us
  waiting for transfers between devices  33.2 us (47%)
  starting transfers between devices  21.3 us (30%)
  Pallas kernels  14.3 us (20%)
  between operations  0.82 us (1%)
    ppermute x1, waiting for transfers between devices, per_device(): sums = lax.ppermute(sums, 'gy', mirrored)  12.6 us
    all_to_all x2, waiting for transfers between devices, exchanged(): lax.all_to_all(payload, 'gy', split_axis=0, concat_axis=0, tiled=True, ax...  12.6 us
    all_to_all x2, starting transfers between devices, exchanged(): lax.all_to_all(payload, 'gy', split_axis=0, concat_axis=0, tiled=True, ax...  9.87 us
    all_to_all x1, starting transfers between devices, per_device(): lax.all_to_all(parts, ('gy', 'gx'), split_axis=0, concat_axis=0, tiled=True)  6.54 us
    all_to_all x1, waiting for transfers between devices, per_device(): lax.all_to_all(parts, ('gy', 'gx'), split_axis=0, concat_axis=0, tiled=True)  6.24 us
    pallas_call x2, Pallas kernels, gathered(): call(functools.partial(gather_body, capacity, slots, far), jax.ShapeDtype...  5.44 us
    ppermute x1, starting transfers between devices, per_device(): sums = lax.ppermute(sums, 'gy', mirrored)  2.65 us
    pallas_call x1, Pallas kernels, per_device(): call(functools.partial(steps_body, len(sides)), (jax.ShapeDtypeStruct((fi...  2.43 us
  transfers between devices with their start and end apart: 8, of which 6 were waited for; matrix products, arithmetic and copies ran while one was open for 0% of the time, Pallas kernels for 11%

profile of v5, /device:TPU:0, one launch (start us, length us, event | category | flops | bytes accessed | tf_op | source)
XLA Modules:
  0.0 69.8 jit_solution(716757535839634345)
XLA Ops:
  0.6 2.6 %shard_map.79 = bf16[64,6272]{1,0:T(8,128)(2,1)} custom-call(s32[1,64]{1,0:T(1,128)} %bitcast.18, s32[1,64]{1,0:T(1,128)} %bitcast.20, s32[1,64]{1,0:T(1,128)} %bitcast.22, bf16[64,24,256]{2,1,0:T(8,128)(2,1)} %refs_3_.3), custom_call_target="tpu_custom_call" | custom-call | flops 402653184 | bytes 1572864 | tf_op jit(solution)/shard_map/pallas_call | solution.py:488
  3.3 0.0 copy-start
  3.3 0.0 copy-start.1
  3.3 6.3 %all-to-all-start = ((bf16[8,8,6272]{2,1,0:T(8,128)(2,1)}), bf16[8,8,6272]{2,1,0:T(8,128)(2,1)S(1)}, u32[]{:S(2)}, u32[]{:S(2)}) async-start(bf16[8,8,6272]{2,1,0:T(8,128)(2,1)} %bitcast.17), calls=%async_computation | async-start | bytes 1605632 | tf_op jit(solution)/shard_map/all_to_all | solution.py:505
  9.6 0.0 copy-done
  9.6 0.0 copy-done.1
  9.6 0.3 shard_map.77
  9.9 0.1 collective-permute-start
  10.0 2.8 %shard_map.81 = bf16[64,6272]{1,0:T(8,128)(2,1)} custom-call(s32[1,64]{1,0:T(1,128)} %bitcast.19, s32[1,64]{1,0:T(1,128)} %bitcast.21, s32[1,64]{1,0:T(1,128)} %bitcast.23, bf16[64,24,256]{2,1,0:T(8,128)(2,1)} %refs_3_.3), custom_call_target="tpu_custom_call" | custom-call | flops 402653184 | bytes 1572864 | tf_op jit(solution)/shard_map/pallas_call | solution.py:488
  12.8 0.0 collective-permute-done
  12.8 1.6 %shard_map.78 = (f32[24,16,256]{2,1,0:T(8,128)S(1)}, f32[32,384]{1,0:T(8,128)S(1)}, f32[24,32,256]{2,1,0:T(8,128)S(1)}, f32[2,32,128]{2,1,0:T(8,128)S(1)}, f32[8,128]{1,0:T(8,128)S(1)}) custom-call(f32[24,32,256]{2,1,0:T(8,128)S(1)} %bitcast.15, s32[32,256]{1,0:T(8,128)S(1)} %copy-done.1, f32[32,128]{1,0:T(8,128)S(1)} %get-tuple-element.47.west_ref, ...), custom_call_target="tpu_custom_call" | custom-call | flops 5898240 | bytes 3538944 | tf_op jit(solution)/shard_map/pallas_call | solution.py:519
  14.5 7.0 %all-to-all-done = bf16[8,8,6272]{2,1,0:T(8,128)(2,1)S(1)} async-done(((bf16[8,8,6272]{2,1,0:T(8,128)(2,1)}), bf16[8,8,6272]{2,1,0:T(8,128)(2,1)S(1)}, u32[]{:S(2)}, u32[]{:S(2)}) %all-to-all-start) | async-done | bytes 802848 | tf_op jit(solution)/shard_map/all_to_all | solution.py:505
  21.5 0.3 shard_map.80
  21.9 2.7 %collective-permute-start.1 = (f16[32,6272]{1,0:T(8,128)(2,1)S(1)}, f16[32,6272]{1,0:T(8,128)(2,1)S(1)}, u32[]{:S(2)}, u32[]{:S(2)}) collective-permute-start(f16[32,6272]{1,0:T(8,128)(2,1)S(1)} %convert_element_type.21), channel_id=1, source_target_pairs={{0,16},{2,18},{4,20},{6,22},{8,24},{10,26},{12,28},{14,30},{16,0},... | collective-permute-start | bytes 1204232 | tf_op jit(solution)/shard_map/ppermute | solution.py:541
  24.5 3.5 %all-to-all-start.1 = ((bf16[8,8,6272]{2,1,0:T(8,128)(2,1)}), bf16[8,8,6272]{2,1,0:T(8,128)(2,1)S(1)}, u32[]{:S(2)}, u32[]{:S(2)}) async-start(bf16[8,8,6272]{2,1,0:T(8,128)(2,1)} %bitcast.6), calls=%async_computation.1 | async-start | bytes 1605632 | tf_op jit(solution)/shard_map/all_to_all | solution.py:505
  28.1 12.6 %collective-permute-done.1 = f16[32,6272]{1,0:T(8,128)(2,1)S(1)} collective-permute-done((f16[32,6272]{1,0:T(8,128)(2,1)S(1)}, f16[32,6272]{1,0:T(8,128)(2,1)S(1)}, u32[]{:S(2)}, u32[]{:S(2)}) %collective-permute-start.1) | collective-permute-done | bytes 401440 | tf_op jit(solution)/shard_map/ppermute | solution.py:541
  40.7 5.5 %all-to-all-done.1 = bf16[8,8,6272]{2,1,0:T(8,128)(2,1)S(1)} async-done(((bf16[8,8,6272]{2,1,0:T(8,128)(2,1)}), bf16[8,8,6272]{2,1,0:T(8,128)(2,1)S(1)}, u32[]{:S(2)}, u32[]{:S(2)}) %all-to-all-start.1) | async-done | bytes 802848 | tf_op jit(solution)/shard_map/all_to_all | solution.py:505
  46.2 0.1 convert_element_type.23.sums_ref
  46.3 0.4 shard_map.83
  46.7 0.1 collective-permute-start.2
  46.8 1.2 %collective-permute-done.2.refs_0_.refs_2_ = f32[32,128]{1,0:T(8,128)S(1)} collective-permute-done((f32[32,128]{1,0:T(8,128)S(1)}, f32[32,128]{1,0:T(8,128)S(1)}, u32[]{:S(2)}, u32[]{:S(2)}) %collective-permute-start.2) | collective-permute-done | bytes 16416 | tf_op jit(solution)/shard_map/ppermute | solution.py:558
  48.0 0.1 shard_map.85
  48.0 0.1 select_convert_fusion.1
  48.1 1.4 %collective-permute-start.3 = (f16[43,4,256]{2,1,0:T(4,128)(2,1)S(1)}, f16[43,4,256]{2,1,0:T(4,128)(2,1)S(1)}, u32[]{:S(2)}, u32[]{:S(2)}) collective-permute-start(f16[43,4,256]{2,1,0:T(4,128)(2,1)S(1)} %get-tuple-element.42), channel_id=1, source_target_pairs={{0,2},{2,0},{4,6},{6,4},{8,10},{10,8},{12,14},{14,12},{16,18},{18,... | collective-permute-start | bytes 264200 | tf_op jit(solution)/shard_map/ppermute | solution.py:567
  49.5 0.7 collective-permute-start.4
  50.2 2.0 %shard_map.84 = (f32[3,8,16,256]{3,2,1,0:T(8,128)S(1)}, f32[3,8,16,256]{3,2,1,0:T(8,128)S(1)}, f32[1,128]{1,0:T(1,128)S(1)}) custom-call(f32[32,384]{1,0:T(8,128)S(1)} %get-tuple-element.24.mask_ref, f32[24,32,256]{2,1,0:T(8,128)S(1)} %get-tuple-element.25.begun_ref, f32[2,32,128]{2,1,0:T(8,128)S(1)} %get-tuple-element.26.packs_ref, ...), custom_call_target="tpu_custom_call" | custom-call | flops 17694720 | bytes 2359296 | tf_op jit(solution)/shard_map/pallas_call | solution.py:570
  52.2 0.6 collective-permute-done.3
  52.8 0.0 collective-permute-done.4
  52.8 0.1 convert_select_fusion
  52.9 2.4 %shard_map.86 = (f32[3,8,16,256]{3,2,1,0:T(8,128)S(1)}, f32[32,128]{1,0:T(8,128)}) custom-call(f32[24,16,256]{2,1,0:T(8,128)S(1)} %get-tuple-element.35.tips_ref, f32[32,128]{1,0:T(8,128)S(1)} %get-tuple-element.47.west_ref, f32[32,128]{1,0:T(8,128)S(1)} %get-tuple-element.46.east_ref, f32[32,384]{1,0:T(8,128)S(1)} %get-tuple-element.24.mask_ref, ...), custom_call_target="tpu_custom_call" | custom-call | flops 13271040 | bytes 1769472 | tf_op jit(solution)/shard_map/pallas_call | solution.py:585
  55.3 6.5 %all-to-all-start.2 = ((f32[32,1,128]{2,1,0:T(1,128)}), f32[32,1,128]{2,1,0:T(1,128)S(1)}, u32[]{:S(2)}, u32[]{:S(2)}) async-start(f32[32,1,128]{2,1,0:T(1,128)} %bitcast.9), calls=%async_computation.2 | async-start | bytes 32768 | tf_op jit(solution)/shard_map/all_to_all | solution.py:607
  61.9 0.9 %shard_map.87 = f32[3,8,32,256]{3,2,1,0:T(8,128)} custom-call(f32[3,8,16,256]{3,2,1,0:T(8,128)S(1)} %get-tuple-element.34.middle_ref, f32[3,8,16,256]{3,2,1,0:T(8,128)S(1)} %get-tuple-element.40.ends_ref), custom_call_target="tpu_custom_call" | custom-call | bytes 1572864 | tf_op jit(solution)/shard_map/pallas_call | solution.py:600
  62.8 6.2 %all-to-all-done.2 = f32[32,1,128]{2,1,0:T(1,128)S(1)} async-done(((f32[32,1,128]{2,1,0:T(1,128)}), f32[32,1,128]{2,1,0:T(1,128)S(1)}, u32[]{:S(2)}, u32[]{:S(2)}) %all-to-all-start.2) | async-done | bytes 16416 | tf_op jit(solution)/shard_map/all_to_all | solution.py:607
  69.0 0.8 %shard_map.88 = f32[3,32]{1,0:T(4,128)} custom-call(f32[32,128]{1,0:T(8,128)S(1)} %bitcast.16), custom_call_target="tpu_custom_call" | custom-call | tf_op jit(solution)/shard_map/pallas_call | solution.py:608
  (5 shorter events, 0.1 us)
Async XLA Ops:
  3.3 6.4 %copy-start = (f32[3,8,32,256]{3,2,1,0:T(8,128)S(1)}, f32[3,8,32,256]{3,2,1,0:T(8,128)}, u32[]{:S(2)}) copy-start(f32[3,8,32,256]{3,2,1,0:T(8,128)} %param.6) | copy-start | bytes 2359300
  3.3 6.3 %copy-start.1 = (s32[32,256]{1,0:T(8,128)S(1)}, s32[32,256]{1,0:T(8,128)}, u32[]{:S(2)}) copy-start(s32[32,256]{1,0:T(8,128)} %wet_ref.3) | copy-start | bytes 98308
  3.3 18.2 %all-to-all-start = ((bf16[8,8,6272]{2,1,0:T(8,128)(2,1)}), bf16[8,8,6272]{2,1,0:T(8,128)(2,1)S(1)}, u32[]{:S(2)}, u32[]{:S(2)}) async-start(bf16[8,8,6272]{2,1,0:T(8,128)(2,1)} %bitcast.17), calls=%async_computation | async-start | bytes 1605632 | tf_op jit(solution)/shard_map/all_to_all | solution.py:505
  9.9 2.9 %collective-permute-start = (f32[32,128]{1,0:T(8,128)S(1)}, f32[32,128]{1,0:T(8,128)S(1)}, u32[]{:S(2)}, u32[]{:S(2)}) collective-permute-start(f32[32,128]{1,0:T(8,128)S(1)} %broadcast_select_fusion.2), channel_id=1, source_target_pairs={{0,1},{1,0},{2,3},{3,2},{4,5},{5,4},{6,7},{7,6},{8,9},{9,8},{10,11... | collective-permute-start | bytes 49160 | tf_op jit(solution)/shard_map/ppermute | solution.py:514
  21.9 18.8 %collective-permute-start.1 = (f16[32,6272]{1,0:T(8,128)(2,1)S(1)}, f16[32,6272]{1,0:T(8,128)(2,1)S(1)}, u32[]{:S(2)}, u32[]{:S(2)}) collective-permute-start(f16[32,6272]{1,0:T(8,128)(2,1)S(1)} %convert_element_type.21), channel_id=1, source_target_pairs={{0,16},{2,18},{4,20},{6,22},{8,24},{10,26},{12,28},{14,30},{16,0},... | collective-permute-start | bytes 1204232 | tf_op jit(solution)/shard_map/ppermute | solution.py:541
  24.5 21.7 %all-to-all-start.1 = ((bf16[8,8,6272]{2,1,0:T(8,128)(2,1)}), bf16[8,8,6272]{2,1,0:T(8,128)(2,1)S(1)}, u32[]{:S(2)}, u32[]{:S(2)}) async-start(bf16[8,8,6272]{2,1,0:T(8,128)(2,1)} %bitcast.6), calls=%async_computation.1 | async-start | bytes 1605632 | tf_op jit(solution)/shard_map/all_to_all | solution.py:505
  46.7 1.2 %collective-permute-start.2 = (f32[32,128]{1,0:T(8,128)S(1)}, f32[32,128]{1,0:T(8,128)S(1)}, u32[]{:S(2)}, u32[]{:S(2)}) collective-permute-start(f32[32,128]{1,0:T(8,128)S(1)} %get-tuple-element.33.edge_ref), channel_id=1, source_target_pairs={{0,1},{1,0},{2,3},{3,2},{4,5},{5,4},{6,7},{7,6},{8,9},{9,8},{10,11... | collective-permute-start | bytes 49160 | tf_op jit(solution)/shard_map/ppermute | solution.py:558
  48.1 4.7 %collective-permute-start.3 = (f16[43,4,256]{2,1,0:T(4,128)(2,1)S(1)}, f16[43,4,256]{2,1,0:T(4,128)(2,1)S(1)}, u32[]{:S(2)}, u32[]{:S(2)}) collective-permute-start(f16[43,4,256]{2,1,0:T(4,128)(2,1)S(1)} %get-tuple-element.42), channel_id=1, source_target_pairs={{0,2},{2,0},{4,6},{6,4},{8,10},{10,8},{12,14},{14,12},{16,18},{18,... | collective-permute-start | bytes 264200 | tf_op jit(solution)/shard_map/ppermute | solution.py:567
  49.5 3.3 %collective-permute-start.4 = (f16[43,4,256]{2,1,0:T(4,128)(2,1)S(1)}, f16[43,4,256]{2,1,0:T(4,128)(2,1)S(1)}, u32[]{:S(2)}, u32[]{:S(2)}) collective-permute-start(f16[43,4,256]{2,1,0:T(4,128)(2,1)S(1)} %get-tuple-element.43), channel_id=1, source_target_pairs={{2,4},{4,2},{6,8},{8,6},{10,12},{12,10},{14,16},{16,14},{18,20},{2... | collective-permute-start | bytes 264200 | tf_op jit(solution)/shard_map/ppermute | solution.py:566
  55.3 13.7 %all-to-all-start.2 = ((f32[32,1,128]{2,1,0:T(1,128)}), f32[32,1,128]{2,1,0:T(1,128)S(1)}, u32[]{:S(2)}, u32[]{:S(2)}) async-start(f32[32,1,128]{2,1,0:T(1,128)} %bitcast.9), calls=%async_computation.2 | async-start | bytes 32768 | tf_op jit(solution)/shard_map/all_to_all | solution.py:607

commit v6 on v5

--- a/solution.py
+++ b/solution.py
@@ -109,14 +109,17 @@
     return jnp.dot(landing, values, preferred_element_type=jnp.float32)
 
 
-def far_body(token_ref, arrived_ref, sums_ref):
-    rows = sums_ref.shape[0]
-    slots, width = arrived_ref.shape
+def far_body(token_ref, arrived_ref, sums_ref, stokes_ref):
+    rows, width = sums_ref.shape
+    slots = arrived_ref.shape[0]
     landing = landing_of(arrived_ref, rows)
-    step = 2 * LANES
-    for at in range(0, width - LANES, step):
+    moving, step = width - LANES, 2 * LANES
+    for at in range(0, moving, step):
         sums_ref[:, at : at + step] = landed(landing, arrived_ref[:, at : at + step]) * SUM_SCALE
-    sums_ref[:, width - LANES :] = landed(landing, jnp.full((slots, LANES), SUM_SCALE, jnp.bfloat16))
+    sums_ref[:, moving:] = landed(landing, jnp.full((slots, LANES), SUM_SCALE, jnp.bfloat16))
+    for at in range(0, stokes_ref.shape[1], step):
+        there = slice(moving + at, moving + at + step)
+        stokes_ref[:, at : at + step] = landed(landing, arrived_ref[:, there]) * SUM_SCALE
 
 
 def come_body(sums_ref, token_ref):
@@ -128,12 +131,14 @@
     rows = force_ref.shape[1]
     landing = landing_of(arrived_ref, rows)
     far = 1.0 / SUM_SCALE
-    count = landed(landing, jnp.ones((slots, LANES), jnp.bfloat16)) + sums_ref[:, planes * cols :] * far
     moving = 2 * planes // 3
+    count = landed(landing, jnp.ones((slots, LANES), jnp.bfloat16)) + sums_ref[:, moving * cols :] * far
     edge = count
     for j in range(planes):
         at = slice(j * cols, (j + 1) * cols)
-        force = landed(landing, arrived_ref[:, at]) + sums_ref[:, at] * far
+        force = landed(landing, arrived_ref[:, at])
+        if j < moving:
+            force = force + sums_ref[:, at] * far
         force_ref[j] = force
         if j < moving:
             edge = packed(edge, force[:, :LANES], 0, EDGE * j)
@@ -189,13 +194,13 @@
     tracer, across, along = fields
     around_tracer = near(z, tracer)
     east, west, north, south = around_tracer
-    ddx, ddy = 0.5 * (east - west), 0.5 * (north - south)
-    extra = (ADV * (across * ddx + along * ddy), PG * ddx, PG * ddy)
+    ddx, ddy = east - west, north - south
+    extra = (0.5 * ADV * (across * ddx + along * ddy), 0.5 * PG * ddx, 0.5 * PG * ddy)
     for f, centre in enumerate(fields):
         sides = around_tracer if f == 0 else near(f * levels + z, centre)
-        lap = (sides[0] + sides[1]) + (sides[2] + sides[3]) - 4.0 * centre
-        lapz = load(f * levels + upper) + load(f * levels + lower) - 2.0 * centre
-        results.append(centre + KH * lap + KZ * lapz - extra[f])
+        beside = KH * ((sides[0] + sides[1]) + (sides[2] + sides[3]))
+        beyond = KZ * (load(f * levels + upper) + load(f * levels + lower))
+        results.append((1.0 - 4.0 * KH - 2.0 * KZ) * centre + beside + (beyond - extra[f]))
     return results
 
 
@@ -339,10 +344,10 @@
 
 
 def steps_body(
-    sides, tips_ref, west_ref, east_ref, mask_ref, begun_ref, packs_ref, force_ref, edge_ref, north_ref, south_ref, *refs
+    sides, stokes_ref, tips_ref, west_ref, east_ref, mask_ref, begun_ref, packs_ref, force_ref, edge_ref, north_ref, south_ref, *refs
 ):
-    ends_ref, part_ref = refs[:2]
-    refs = refs[2:]
+    middle_ref, ends_ref, part_ref = refs[:3]
+    refs = refs[3:]
     side_refs = refs[:sides]
     held_ref, parts_ref, push_ref, halo_ref, one_ref, two_ref = refs[sides:]
     planes, rows, cols = begun_ref.shape
@@ -424,9 +429,16 @@
             sums[q] = sums[q] + term
 
     two_more(relax, push_ref, one_ref, two_ref, last)
+    beyond = jnp.zeros((rows, cols), jnp.float32)
+    for z in range(levels):
+        tracer = [held_ref[0, z, :tile], middle_ref[0, z], held_ref[0, z, tile:]]
+        beyond = beyond + stokes_ref[:, z * cols : (z + 1) * cols] * jnp.concatenate(tracer, axis=0)
+    beyond = jnp.sum(beyond, axis=1, keepdims=True) / (SUM_SCALE * (1.0 + edge_ref[:, LANES - 1 :]))
+    row, lane = iota((rows, LANES), 0), iota((rows, LANES), 1)
+    beyond = jnp.sum(jnp.where(lane == rows + row, beyond, 0.0), axis=0, keepdims=True)
     row = iota((own_rows, LANES), 0)
     child = jnp.where(row < RIM, row, jnp.where(row >= own_rows - RIM, row + rows - own_rows, -1))
-    part = transports(sums, own[:own_rows, LANES - 1 :], child, rows) + part_ref[...]
+    part = transports(sums, own[:own_rows, LANES - 1 :], child, rows) + (part_ref[...] + beyond)
     parts_ref[...] = jnp.broadcast_to(part, parts_ref.shape)
 
 
@@ -530,9 +542,12 @@
         scratch_shapes=[pltpu.VMEM((planes, rows, wide), f32)],
     )(cells, wet, from_west, from_east)
 
-    sums = call(
+    sums, stokes = call(
         far_body,
-        jax.ShapeDtypeStruct((rows, width), f32),
+        (
+            jax.ShapeDtypeStruct((rows, moving * cols + LANES), f32),
+            jax.ShapeDtypeStruct((rows, (planes - moving) * cols), f32),
+        ),
         flops=2 * rows * slots * width,
         moved=2 * slots * width + 4 * rows * width,
     )(token, far_rows)
@@ -540,6 +555,7 @@
     sums, near_rows = lax.optimization_barrier((sums.astype(jnp.float16), gathered(False)))
     sums = lax.ppermute(sums, "gy", mirrored)
     arrived = exchanged(near_rows)
+    stokes = lax.ppermute(stokes.astype(jnp.float16), "gy", mirrored)
     come = call(
         come_body,
         jax.ShapeDtypeStruct((8, LANES), f32),
@@ -582,6 +598,8 @@
             pltpu.VMEM((planes, rows, wide), f32),
         ],
     )(mask, begun, packs, force, edge, *sides)
+    stokes, part = lax.optimization_barrier((stokes, part))
+    stokes = stokes.astype(f32)
     ends, parts = call(
         functools.partial(steps_body, len(sides)),
         (
@@ -596,7 +614,7 @@
             pltpu.VMEM((planes, 3 * tile, wide), f32),
             pltpu.VMEM((planes, 3 * tile, wide), f32),
         ],
-    )(tips, from_west, from_east, mask, begun, packs, force, edge, above, below, ends, part, *sides)
+    )(stokes, tips, from_west, from_east, mask, begun, packs, force, edge, above, below, middle, ends, part, *sides)
     new_state = call(
         whole_body,
         jax.ShapeDtypeStruct(state.shape, f32),

time: 70.1 us -> 68.8 us (0.981)
  starting transfers between devices: 21.3 us -> 19.8 us
    ppermute x1, waiting for transfers between devices: 12.6 us -> 6.98 us  [per_device(): sums = lax.ppermute(sums, 'gy', mirrored)]
    ppermute x0 -> x1, waiting for transfers between devices: none -> 3.76 us  [per_device(): stokes = lax.ppermute(stokes.astype(jnp.float16), 'gy', mirrored)]
    all_to_all x2, waiting for transfers between devices: 12.6 us -> 15.3 us  [exchanged(): lax.all_to_all(payload, 'gy', split_axis=0, concat_axis=0, tiled=True, ax...]
    all_to_all x1, starting transfers between devices: 6.54 us -> 5.05 us  [per_device(): lax.all_to_all(parts, ('gy', 'gx'), split_axis=0, concat_axis=0, tiled=True)]
  transfers between devices with their start and end apart: 8 -> 9, of which waited for: 6 -> 6; matrix products, arithmetic and copies ran while one was open for 0% -> 0% of each run, Pallas kernels for 11% -> 11%
where the time goes in v6:
time: 68.8 us; the launch traced here: 68.4 us
  waiting for transfers between devices  33.3 us (48%)
  starting transfers between devices  19.8 us (29%)
  Pallas kernels  14.1 us (20%)
  between operations  0.86 us (1%)
    all_to_all x2, waiting for transfers between devices, exchanged(): lax.all_to_all(payload, 'gy', split_axis=0, concat_axis=0, tiled=True, ax...  15.3 us
    all_to_all x2, starting transfers between devices, exchanged(): lax.all_to_all(payload, 'gy', split_axis=0, concat_axis=0, tiled=True, ax...  9.87 us
    ppermute x1, waiting for transfers between devices, per_device(): sums = lax.ppermute(sums, 'gy', mirrored)  6.98 us
    all_to_all x1, waiting for transfers between devices, per_device(): lax.all_to_all(parts, ('gy', 'gx'), split_axis=0, concat_axis=0, tiled=True)  6.24 us
    pallas_call x2, Pallas kernels, gathered(): call(functools.partial(gather_body, capacity, slots, far), jax.ShapeDtype...  5.41 us
    all_to_all x1, starting transfers between devices, per_device(): lax.all_to_all(parts, ('gy', 'gx'), split_axis=0, concat_axis=0, tiled=True)  5.05 us
    ppermute x1, waiting for transfers between devices, per_device(): stokes = lax.ppermute(stokes.astype(jnp.float16), 'gy', mirrored)  3.76 us
    ppermute x1, starting transfers between devices, per_device(): sums = lax.ppermute(sums, 'gy', mirrored)  2.66 us
  transfers between devices with their start and end apart: 9, of which 6 were waited for; matrix products, arithmetic and copies ran while one was open for 0% of the time, Pallas kernels for 11%

profile of v6, /device:TPU:0, one launch (start us, length us, event | category | flops | bytes accessed | tf_op | source)
XLA Modules:
  0.0 68.4 jit_solution(14535091629888963308)
XLA Ops:
  0.6 2.6 %shard_map.79 = bf16[64,6272]{1,0:T(8,128)(2,1)} custom-call(s32[1,64]{1,0:T(1,128)} %bitcast.18, s32[1,64]{1,0:T(1,128)} %bitcast.20, s32[1,64]{1,0:T(1,128)} %bitcast.22, bf16[64,24,256]{2,1,0:T(8,128)(2,1)} %refs_3_.3), custom_call_target="tpu_custom_call" | custom-call | flops 402653184 | bytes 1572864 | tf_op jit(solution)/shard_map/pallas_call | solution.py:500
  3.3 0.0 copy-start
  3.3 0.0 copy-start.1
  3.3 6.3 %all-to-all-start = ((bf16[8,8,6272]{2,1,0:T(8,128)(2,1)}), bf16[8,8,6272]{2,1,0:T(8,128)(2,1)S(1)}, u32[]{:S(2)}, u32[]{:S(2)}) async-start(bf16[8,8,6272]{2,1,0:T(8,128)(2,1)} %bitcast.17), calls=%async_computation | async-start | bytes 1605632 | tf_op jit(solution)/shard_map/all_to_all | solution.py:517
  9.6 0.0 copy-done
  9.6 0.0 copy-done.1
  9.6 0.3 shard_map.77
  9.9 0.1 collective-permute-start
  10.0 2.8 %shard_map.81 = bf16[64,6272]{1,0:T(8,128)(2,1)} custom-call(s32[1,64]{1,0:T(1,128)} %bitcast.19, s32[1,64]{1,0:T(1,128)} %bitcast.21, s32[1,64]{1,0:T(1,128)} %bitcast.23, bf16[64,24,256]{2,1,0:T(8,128)(2,1)} %refs_3_.3), custom_call_target="tpu_custom_call" | custom-call | flops 402653184 | bytes 1572864 | tf_op jit(solution)/shard_map/pallas_call | solution.py:500
  12.8 0.0 collective-permute-done
  12.8 1.6 %shard_map.78 = (f32[24,16,256]{2,1,0:T(8,128)S(1)}, f32[32,384]{1,0:T(8,128)S(1)}, f32[24,32,256]{2,1,0:T(8,128)S(1)}, f32[2,32,128]{2,1,0:T(8,128)S(1)}, f32[8,128]{1,0:T(8,128)S(1)}) custom-call(f32[24,32,256]{2,1,0:T(8,128)S(1)} %bitcast.15, s32[32,256]{1,0:T(8,128)S(1)} %copy-done.1, f32[32,128]{1,0:T(8,128)S(1)} %get-tuple-element.55.west_ref, ...), custom_call_target="tpu_custom_call" | custom-call | flops 5898240 | bytes 3538944 | tf_op jit(solution)/shard_map/pallas_call | solution.py:531
  14.4 7.1 %all-to-all-done = bf16[8,8,6272]{2,1,0:T(8,128)(2,1)S(1)} async-done(((bf16[8,8,6272]{2,1,0:T(8,128)(2,1)}), bf16[8,8,6272]{2,1,0:T(8,128)(2,1)S(1)}, u32[]{:S(2)}, u32[]{:S(2)}) %all-to-all-start) | async-done | bytes 802848 | tf_op jit(solution)/shard_map/all_to_all | solution.py:517
  21.5 0.3 shard_map.80
  21.9 2.7 %collective-permute-start.1 = (f16[32,4224]{1,0:T(8,128)(2,1)S(1)}, f16[32,4224]{1,0:T(8,128)(2,1)S(1)}, u32[]{:S(2)}, u32[]{:S(2)}) collective-permute-start(f16[32,4224]{1,0:T(8,128)(2,1)S(1)} %convert_element_type.27), channel_id=1, source_target_pairs={{0,16},{2,18},{4,20},{6,22},{8,24},{10,26},{12,28},{14,30},{16,0},... | collective-permute-start | bytes 811016 | tf_op jit(solution)/shard_map/ppermute | solution.py:556
  24.5 3.5 %all-to-all-start.1 = ((bf16[8,8,6272]{2,1,0:T(8,128)(2,1)}), bf16[8,8,6272]{2,1,0:T(8,128)(2,1)S(1)}, u32[]{:S(2)}, u32[]{:S(2)}) async-start(bf16[8,8,6272]{2,1,0:T(8,128)(2,1)} %bitcast.6), calls=%async_computation.1 | async-start | bytes 1605632 | tf_op jit(solution)/shard_map/all_to_all | solution.py:517
  28.1 7.0 %collective-permute-done.1 = f16[32,4224]{1,0:T(8,128)(2,1)S(1)} collective-permute-done((f16[32,4224]{1,0:T(8,128)(2,1)S(1)}, f16[32,4224]{1,0:T(8,128)(2,1)S(1)}, u32[]{:S(2)}, u32[]{:S(2)}) %collective-permute-start.1) | collective-permute-done | bytes 270368 | tf_op jit(solution)/shard_map/ppermute | solution.py:556
  35.1 8.2 %all-to-all-done.1 = bf16[8,8,6272]{2,1,0:T(8,128)(2,1)S(1)} async-done(((bf16[8,8,6272]{2,1,0:T(8,128)(2,1)}), bf16[8,8,6272]{2,1,0:T(8,128)(2,1)S(1)}, u32[]{:S(2)}, u32[]{:S(2)}) %all-to-all-start.1) | async-done | bytes 802848 | tf_op jit(solution)/shard_map/all_to_all | solution.py:517
  43.3 0.4 shard_map.83
  43.7 0.1 collective-permute-start.2
  43.8 0.1 collective-permute-start.3
  43.9 1.1 %collective-permute-done.2.refs_0_.refs_3_ = f32[32,128]{1,0:T(8,128)S(1)} collective-permute-done((f32[32,128]{1,0:T(8,128)S(1)}, f32[32,128]{1,0:T(8,128)S(1)}, u32[]{:S(2)}, u32[]{:S(2)}) %collective-permute-start.2) | collective-permute-done | bytes 16416 | tf_op jit(solution)/shard_map/ppermute | solution.py:574
  45.0 0.1 shard_map.85
  45.0 0.1 select_convert_fusion.1
  45.1 1.4 %collective-permute-start.4 = (f16[43,4,256]{2,1,0:T(4,128)(2,1)S(1)}, f16[43,4,256]{2,1,0:T(4,128)(2,1)S(1)}, u32[]{:S(2)}, u32[]{:S(2)}) collective-permute-start(f16[43,4,256]{2,1,0:T(4,128)(2,1)S(1)} %get-tuple-element.50), channel_id=1, source_target_pairs={{0,2},{2,0},{4,6},{6,4},{8,10},{10,8},{12,14},{14,12},{16,18},{18,... | collective-permute-start | bytes 264200 | tf_op jit(solution)/shard_map/ppermute | solution.py:583
  46.5 0.7 collective-permute-start.5
  47.1 2.0 %shard_map.84 = (f32[3,8,16,256]{3,2,1,0:T(8,128)S(1)}, f32[3,8,16,256]{3,2,1,0:T(8,128)S(1)}, f32[1,128]{1,0:T(1,128)S(1)}) custom-call(f32[32,384]{1,0:T(8,128)S(1)} %get-tuple-element.28.mask_ref, f32[24,32,256]{2,1,0:T(8,128)S(1)} %get-tuple-element.29.begun_ref, f32[2,32,128]{2,1,0:T(8,128)S(1)} %get-tuple-element.30.packs_ref, ...), custom_call_target="tpu_custom_call" | custom-call | flops 17694720 | bytes 2359296 | tf_op jit(solution)/shard_map/pallas_call | solution.py:586
  49.1 3.8 %collective-permute-done.3 = f16[32,2048]{1,0:T(8,128)(2,1)S(1)} collective-permute-done((f16[32,2048]{1,0:T(8,128)(2,1)S(1)}, f16[32,2048]{1,0:T(8,128)(2,1)S(1)}, u32[]{:S(2)}, u32[]{:S(2)}) %collective-permute-start.3) | collective-permute-done | bytes 131104 | tf_op jit(solution)/shard_map/ppermute | solution.py:558
  52.9 0.0 collective-permute-done.4
  52.9 0.0 collective-permute-done.5
  52.9 0.1 convert_select_fusion
  53.0 2.4 %shard_map.86 = (f32[3,8,16,256]{3,2,1,0:T(8,128)S(1)}, f32[32,128]{1,0:T(8,128)}) custom-call(f32[32,2048]{1,0:T(8,128)S(1)} %convert_element_type.31.stokes_ref, f32[24,16,256]{2,1,0:T(8,128)S(1)} %get-tuple-element.43.tips_ref, f32[32,128]{1,0:T(8,128)S(1)} %get-tuple-element.55.west_ref, f32[32,128]{1,0:T(8,128)S(1)} %get-tuple-element.54.east_ref, ...), custom_call_target="tpu_custom_call" | custom-call | flops 13271040 | bytes 1769472 | tf_op jit(solution)/shard_map/pallas_call | solution.py:603
  55.4 5.1 %all-to-all-start.2 = ((f32[32,1,128]{2,1,0:T(1,128)}), f32[32,1,128]{2,1,0:T(1,128)S(1)}, u32[]{:S(2)}, u32[]{:S(2)}) async-start(f32[32,1,128]{2,1,0:T(1,128)} %bitcast.9), calls=%async_computation.2 | async-start | bytes 32768 | tf_op jit(solution)/shard_map/all_to_all | solution.py:625
  60.5 0.9 %shard_map.87 = f32[3,8,32,256]{3,2,1,0:T(8,128)} custom-call(f32[3,8,16,256]{3,2,1,0:T(8,128)S(1)} %get-tuple-element.39.refs_0_.middle_ref, f32[3,8,16,256]{3,2,1,0:T(8,128)S(1)} %get-tuple-element.48.ends_ref), custom_call_target="tpu_custom_call" | custom-call | bytes 1572864 | tf_op jit(solution)/shard_map/pallas_call | solution.py:618
  61.4 6.2 %all-to-all-done.2 = f32[32,1,128]{2,1,0:T(1,128)S(1)} async-done(((f32[32,1,128]{2,1,0:T(1,128)}), f32[32,1,128]{2,1,0:T(1,128)S(1)}, u32[]{:S(2)}, u32[]{:S(2)}) %all-to-all-start.2) | async-done | bytes 16416 | tf_op jit(solution)/shard_map/all_to_all | solution.py:625
  67.6 0.8 %shard_map.88 = f32[3,32]{1,0:T(4,128)} custom-call(f32[32,128]{1,0:T(8,128)S(1)} %bitcast.16), custom_call_target="tpu_custom_call" | custom-call | tf_op jit(solution)/shard_map/pallas_call | solution.py:626
  (8 shorter events, 0.1 us)
Async XLA Ops:
  3.3 6.4 %copy-start = (f32[3,8,32,256]{3,2,1,0:T(8,128)S(1)}, f32[3,8,32,256]{3,2,1,0:T(8,128)}, u32[]{:S(2)}) copy-start(f32[3,8,32,256]{3,2,1,0:T(8,128)} %param.6) | copy-start | bytes 2359300
  3.3 6.3 %copy-start.1 = (s32[32,256]{1,0:T(8,128)S(1)}, s32[32,256]{1,0:T(8,128)}, u32[]{:S(2)}) copy-start(s32[32,256]{1,0:T(8,128)} %wet_ref.3) | copy-start | bytes 98308
  3.3 18.2 %all-to-all-start = ((bf16[8,8,6272]{2,1,0:T(8,128)(2,1)}), bf16[8,8,6272]{2,1,0:T(8,128)(2,1)S(1)}, u32[]{:S(2)}, u32[]{:S(2)}) async-start(bf16[8,8,6272]{2,1,0:T(8,128)(2,1)} %bitcast.17), calls=%async_computation | async-start | bytes 1605632 | tf_op jit(solution)/shard_map/all_to_all | solution.py:517
  9.9 2.9 %collective-permute-start = (f32[32,128]{1,0:T(8,128)S(1)}, f32[32,128]{1,0:T(8,128)S(1)}, u32[]{:S(2)}, u32[]{:S(2)}) collective-permute-start(f32[32,128]{1,0:T(8,128)S(1)} %broadcast_select_fusion.2), channel_id=1, source_target_pairs={{0,1},{1,0},{2,3},{3,2},{4,5},{5,4},{6,7},{7,6},{8,9},{9,8},{10,11... | collective-permute-start | bytes 49160 | tf_op jit(solution)/shard_map/ppermute | solution.py:526
  21.9 13.2 %collective-permute-start.1 = (f16[32,4224]{1,0:T(8,128)(2,1)S(1)}, f16[32,4224]{1,0:T(8,128)(2,1)S(1)}, u32[]{:S(2)}, u32[]{:S(2)}) collective-permute-start(f16[32,4224]{1,0:T(8,128)(2,1)S(1)} %convert_element_type.27), channel_id=1, source_target_pairs={{0,16},{2,18},{4,20},{6,22},{8,24},{10,26},{12,28},{14,30},{16,0},... | collective-permute-start | bytes 811016 | tf_op jit(solution)/shard_map/ppermute | solution.py:556
  24.5 18.7 %all-to-all-start.1 = ((bf16[8,8,6272]{2,1,0:T(8,128)(2,1)}), bf16[8,8,6272]{2,1,0:T(8,128)(2,1)S(1)}, u32[]{:S(2)}, u32[]{:S(2)}) async-start(bf16[8,8,6272]{2,1,0:T(8,128)(2,1)} %bitcast.6), calls=%async_computation.1 | async-start | bytes 1605632 | tf_op jit(solution)/shard_map/all_to_all | solution.py:517
  43.7 1.2 %collective-permute-start.2 = (f32[32,128]{1,0:T(8,128)S(1)}, f32[32,128]{1,0:T(8,128)S(1)}, u32[]{:S(2)}, u32[]{:S(2)}) collective-permute-start(f32[32,128]{1,0:T(8,128)S(1)} %get-tuple-element.38.edge_ref), channel_id=1, source_target_pairs={{0,1},{1,0},{2,3},{3,2},{4,5},{5,4},{6,7},{7,6},{8,9},{9,8},{10,11... | collective-permute-start | bytes 49160 | tf_op jit(solution)/shard_map/ppermute | solution.py:574
  43.8 9.1 %collective-permute-start.3 = (f16[32,2048]{1,0:T(8,128)(2,1)S(1)}, f16[32,2048]{1,0:T(8,128)(2,1)S(1)}, u32[]{:S(2)}, u32[]{:S(2)}) collective-permute-start(f16[32,2048]{1,0:T(8,128)(2,1)S(1)} %convert_element_type.30), channel_id=1, source_target_pairs={{0,16},{2,18},{4,20},{6,22},{8,24},{10,26},{12,28},{14,30},{16,0},... | collective-permute-start | bytes 393224 | tf_op jit(solution)/shard_map/ppermute | solution.py:558
  45.1 7.8 %collective-permute-start.4 = (f16[43,4,256]{2,1,0:T(4,128)(2,1)S(1)}, f16[43,4,256]{2,1,0:T(4,128)(2,1)S(1)}, u32[]{:S(2)}, u32[]{:S(2)}) collective-permute-start(f16[43,4,256]{2,1,0:T(4,128)(2,1)S(1)} %get-tuple-element.50), channel_id=1, source_target_pairs={{0,2},{2,0},{4,6},{6,4},{8,10},{10,8},{12,14},{14,12},{16,18},{18,... | collective-permute-start | bytes 264200 | tf_op jit(solution)/shard_map/ppermute | solution.py:583
  46.5 6.4 %collective-permute-start.5 = (f16[43,4,256]{2,1,0:T(4,128)(2,1)S(1)}, f16[43,4,256]{2,1,0:T(4,128)(2,1)S(1)}, u32[]{:S(2)}, u32[]{:S(2)}) collective-permute-start(f16[43,4,256]{2,1,0:T(4,128)(2,1)S(1)} %get-tuple-element.51), channel_id=1, source_target_pairs={{2,4},{4,2},{6,8},{8,6},{10,12},{12,10},{14,16},{16,14},{18,20},{2... | collective-permute-start | bytes 264200 | tf_op jit(solution)/shard_map/ppermute | solution.py:582
  55.4 12.2 %all-to-all-start.2 = ((f32[32,1,128]{2,1,0:T(1,128)}), f32[32,1,128]{2,1,0:T(1,128)S(1)}, u32[]{:S(2)}, u32[]{:S(2)}) async-start(f32[32,1,128]{2,1,0:T(1,128)} %bitcast.9), calls=%async_computation.2 | async-start | bytes 32768 | tf_op jit(solution)/shard_map/all_to_all | solution.py:625

commit v7 on v6

--- a/solution.py
+++ b/solution.py
@@ -215,10 +215,9 @@
 def begin_body(state_ref, wet_ref, west_ref, east_ref, tips_ref, mask_ref, begun_ref, packs_ref, token_ref, full_ref):
     planes, rows, cols = state_ref.shape
     levels = planes // 3
-    tile = 2 * RIM
     west, east = west_ref[...], east_ref[...]
-    tips_ref[:, :tile] = state_ref[:, :tile]
-    tips_ref[:, tile:] = state_ref[:, rows - tile :]
+    for j in range(planes):
+        tips_ref[j] = outer_rows(state_ref, j)
     for j in range(planes):
         full_ref[j, :, :cols] = state_ref[j]
         full_ref[j, :, cols:] = side_tile(west, EDGE * j, east, EDGE * j)
@@ -236,6 +235,12 @@
     token_ref[...] = jnp.zeros_like(token_ref)
 
 
+def outer_rows(ref, *index):
+    rows, tile = ref.shape[len(index)], 2 * RIM
+    first, last = ref[(*index, slice(0, tile))], ref[(*index, slice(rows - tile, rows))]
+    return jnp.where(iota(first.shape, 0) < RIM, first, last)
+
+
 def widened(plane, west, east, at):
     return jnp.concatenate([plane, side_tile(west, at, east, at)], axis=1)
 
@@ -244,7 +249,7 @@
     sides, (up_ref, down_ref) = refs[:-2], refs[-2:]
     planes, rows, cols = force_ref.shape
     moving = 2 * planes // 3
-    ends = ((up_ref, slice(rows - RIM, rows), slice(3 * RIM, 4 * RIM)), (down_ref, slice(0, RIM), slice(0, RIM)))
+    ends = ((up_ref, slice(rows - RIM, rows), slice(RIM, 2 * RIM)), (down_ref, slice(0, RIM), slice(0, RIM)))
     for out_ref, at, tip in ends:
         out_ref[:moving] = force_ref[:moving, at] * FORCE_SCALE
         out_ref[moving : moving + planes] = tips_ref[:, tip] * STATE_SCALE
@@ -278,13 +283,13 @@
     return (tracer * rated + push_ref[(z, *at)], across * rated, along * rated + push_ref[(levels + z, *at)])
 
 
-def two_more(relax, push_ref, one_ref, two_ref, last):
+def two_more(relax, push_ref, one_ref, two_ref, last, patched=lambda j, value: value):
     levels = one_ref.shape[0] // 3
     cols = one_ref.shape[2] - LANES
     for z in range(levels):
         values = moved(lambda j: one_ref[j], lambda j, field: around(field), levels, z)
         for f, value in enumerate(finish(relax, push_ref, levels, values, z)):
-            two_ref[f * levels + z] = value
+            two_ref[f * levels + z] = patched(f * levels + z, value)
     for z in range(levels):
         values = moved(
             lambda j: two_ref[j, :, :cols],
@@ -313,7 +318,7 @@
 
 
 def inner_body(mask_ref, begun_ref, packs_ref, force_ref, edge_ref, *refs):
-    side_refs, (middle_ref, ends_ref, part_ref, push_ref, one_ref, two_ref) = refs[:-6], refs[-6:]
+    side_refs, (middle_ref, ends_ref, part_ref, twos_ref, push_ref, one_ref, two_ref) = refs[:-7], refs[-7:]
     planes, rows, cols = begun_ref.shape
     levels = planes // 3
     moving = 2 * levels
@@ -338,6 +343,8 @@
             sums[q] = sums[q] + term
 
     two_more(relax, push_ref, one_ref, two_ref, last)
+    for j in range(planes):
+        twos_ref[j] = outer_rows(two_ref, j)
     row = iota((rows, LANES), 0)
     child = jnp.where((row >= RIM) & (row < rows - RIM), row, -1)
     part_ref[...] = transports(sums, edge_ref[:, LANES - 1 :], child, rows)
@@ -346,8 +353,8 @@
 def steps_body(
     sides, stokes_ref, tips_ref, west_ref, east_ref, mask_ref, begun_ref, packs_ref, force_ref, edge_ref, north_ref, south_ref, *refs
 ):
-    middle_ref, ends_ref, part_ref = refs[:3]
-    refs = refs[3:]
+    middle_ref, ends_ref, part_ref, twos_ref = refs[:4]
+    refs = refs[4:]
     side_refs = refs[:sides]
     held_ref, parts_ref, push_ref, halo_ref, one_ref, two_ref = refs[sides:]
     planes, rows, cols = begun_ref.shape
@@ -355,11 +362,7 @@
     levels = planes // 3
     moving = 2 * levels
     tile = 2 * RIM
-    own_rows, total = 2 * tile, 3 * tile
-    tail = slice(rows - tile, rows)
-
-    def slab(ref, *index):
-        return [ref[(*index, slice(0, tile))], ref[(*index, tail)]]
+    total = 2 * tile
 
     def joined(index, scale):
         return jnp.concatenate([north_ref[index], south_ref[index]], axis=0) * (1.0 / scale)
@@ -370,46 +373,46 @@
 
     beside = [half_of(k, STATE_SCALE) for k in range(2)]
     outer = [half_of(2 + k, FORCE_SCALE) for k in range(1 + sides)]
-    edges = [jnp.concatenate([*slab(side), outer[1 + k]], axis=0) for k, side in enumerate(side_refs)]
-    own = jnp.concatenate([*slab(edge_ref), outer[0]], axis=0)
+    edges = [jnp.concatenate([outer_rows(side), outer[1 + k]], axis=0) for k, side in enumerate(side_refs)]
+    own = jnp.concatenate([outer_rows(edge_ref), outer[0]], axis=0)
 
     def halo(index, at):
         return widened(joined(moving + index, STATE_SCALE), *beside, at)
 
-    mask = jnp.concatenate([*slab(mask_ref), halo(planes, EDGE * planes)], axis=0)
+    mask = jnp.concatenate([outer_rows(mask_ref), halo(planes, EDGE * planes)], axis=0)
     relax = factors(
         mask,
         own,
         edges[0],
         edges[-1],
-        lambda j: jnp.concatenate([*slab(force_ref, j), joined(j, FORCE_SCALE)], axis=0),
+        lambda j: jnp.concatenate([outer_rows(force_ref, j), joined(j, FORCE_SCALE)], axis=0),
         push_ref,
     )
     for j in range(planes):
         halo_ref[j] = halo(j, EDGE * j)
     row = iota((tile, wide), 0)
-    packs = [slab(packs_ref, k) for k in range(2)]
-    wests, easts = slab(west_ref), slab(east_ref)
-
-    def tip(j, k):
-        return widened(tips_ref[j, k * tile : (k + 1) * tile], wests[k], easts[k], EDGE * j)
-
-    def begun(j, k):
-        return widened(slab(begun_ref, j)[k], packs[0][k], packs[1][k], EDGE * j)
+    packs = [outer_rows(packs_ref, k) for k in range(2)]
+    wests, easts = outer_rows(west_ref), outer_rows(east_ref)
+
+    def tip(j):
+        return widened(tips_ref[j], wests, easts, EDGE * j)
+
+    def begun(j):
+        return widened(outer_rows(begun_ref, j), *packs, EDGE * j)
 
     def near(j, field):
-        return around_between(field, tip(j, 0)[:1], tip(j, 1)[tile - 1 :])
+        start = tip(j)
+        return around_between(field, start[:1], start[tile - 1 :])
 
     for z in range(levels):
         index = [f * levels + z for f in range(3)]
         beyond = [halo_ref[j] for j in index]
         north = [jnp.where(row == tile - 1, value[:1], 0.0) for value in beyond]
         south = [jnp.where(row == 0, value[tile - 1 :], 0.0) for value in beyond]
-        first = added(-1.0, tip(index[2], 0), *south)
-        final = added(1.0, tip(index[2], 1), *north)
+        along = tip(index[2])
+        extras = zip(added(-1.0, along, *south), added(1.0, along, *north))
         blocks = (
-            [begun(j, 0) + extra for j, extra in zip(index, first)],
-            [begun(j, 1) + extra for j, extra in zip(index, final)],
+            [begun(j) + (first + final) for j, (first, final) in zip(index, extras)],
             moved(lambda j: halo_ref[j], near, levels, z),
         )
         for k, values in enumerate(blocks):
@@ -417,18 +420,32 @@
             for j, value in zip(index, finish(relax, push_ref, levels, values, z, (at,))):
                 one_ref[j, at] = value
 
-    sums = [jnp.zeros((own_rows, cols), jnp.float32) for _ in range(3)]
-    row = iota((tile, cols), 0)
+    meeting = (row == RIM - 1) | (row == RIM)
+
+    def patched(j, value):
+        return jnp.concatenate([jnp.where(meeting, twos_ref[j], value[:tile]), value[tile:]], axis=0)
+
+    sums = [jnp.zeros((tile, cols), jnp.float32) for _ in range(3)]
+    place = iota((tile, cols), 0)
 
     def last(z, values):
+        finals = []
         for f, value in enumerate(values):
-            held_ref[f, z, :tile] = jnp.where(row < RIM, value[:tile], ends_ref[f, z, :tile])
-            held_ref[f, z, tile:] = jnp.where(row < RIM, ends_ref[f, z, tile:], value[tile:own_rows])
-        stokes = jnp.concatenate(slab(force_ref, moving + z), axis=0)
-        for q, term in enumerate(terms(values, stokes)):
+            ends = [ends_ref[f, z, :tile], ends_ref[f, z, tile:]]
+            kept = jnp.where(place < RIM, *ends)
+            final = jnp.where((place == RIM - 1) | (place == RIM), kept, value[:tile])
+            held_ref[f, z, :tile] = jnp.where(place < RIM, final, ends[0])
+            held_ref[f, z, tile:] = jnp.where(place < RIM, ends[1], final)
+            finals.append(final)
+        tracer = jnp.concatenate([finals[0], values[0][tile:]], axis=0)
+        within = jnp.where(place < RIM, ends_ref[0, z, tile:], ends_ref[0, z, :tile])
+        north = jnp.where(place == RIM - 1, pltpu.roll(within, tile - 1, 0), pltpu.roll(tracer, total - 1, 0)[:tile])
+        south = jnp.where(place == RIM, pltpu.roll(within, 1, 0), pltpu.roll(tracer, 1, 0)[:tile])
+        stokes = outer_rows(force_ref, moving + z)
+        for q, term in enumerate((finals[2] * finals[0], stokes * finals[0], north - south)):
             sums[q] = sums[q] + term
 
-    two_more(relax, push_ref, one_ref, two_ref, last)
+    two_more(relax, push_ref, one_ref, two_ref, last, patched)
     beyond = jnp.zeros((rows, cols), jnp.float32)
     for z in range(levels):
         tracer = [held_ref[0, z, :tile], middle_ref[0, z], held_ref[0, z, tile:]]
@@ -436,9 +453,9 @@
     beyond = jnp.sum(beyond, axis=1, keepdims=True) / (SUM_SCALE * (1.0 + edge_ref[:, LANES - 1 :]))
     row, lane = iota((rows, LANES), 0), iota((rows, LANES), 1)
     beyond = jnp.sum(jnp.where(lane == rows + row, beyond, 0.0), axis=0, keepdims=True)
-    row = iota((own_rows, LANES), 0)
-    child = jnp.where(row < RIM, row, jnp.where(row >= own_rows - RIM, row + rows - own_rows, -1))
-    part = transports(sums, own[:own_rows, LANES - 1 :], child, rows) + (part_ref[...] + beyond)
+    row = iota((tile, LANES), 0)
+    child = jnp.where(row < RIM, row, row + rows - tile)
+    part = transports(sums, own[:tile, LANES - 1 :], child, rows) + (part_ref[...] + beyond)
     parts_ref[...] = jnp.broadcast_to(part, parts_ref.shape)
 
 
@@ -531,7 +548,7 @@
     tips, mask, begun, packs, token = call(
         begin_body,
         (
-            jax.ShapeDtypeStruct((planes, 4 * RIM, cols), f32),
+            jax.ShapeDtypeStruct((planes, 2 * RIM, cols), f32),
             jax.ShapeDtypeStruct((rows, wide), f32),
             jax.ShapeDtypeStruct((planes, rows, cols), f32),
             jax.ShapeDtypeStruct((2, rows, LANES), f32),
@@ -583,12 +600,13 @@
     near = lax.ppermute(jnp.where(even, up, down).astype(jnp.float16), "gy", even_pairs).astype(f32)
     above, below = jnp.where(even, near, far), jnp.where(even, far, near)
     tile = 2 * RIM
-    middle, ends, part = call(
+    middle, ends, part, twos = call(
         inner_body,
         (
             jax.ShapeDtypeStruct((fields, levels, rows - 2 * tile, cols), f32),
             jax.ShapeDtypeStruct((fields, levels, 2 * tile, cols), f32),
             jax.ShapeDtypeStruct((1, LANES), f32),
+            jax.ShapeDtypeStruct((planes, tile, wide), f32),
         ),
         flops=60 * planes * rows * wide,
         moved=8 * planes * rows * wide,
@@ -609,12 +627,12 @@
         flops=60 * planes * 3 * tile * wide,
         moved=8 * planes * 3 * tile * wide,
         scratch_shapes=[
-            pltpu.VMEM((moving, 3 * tile, wide), f32),
+            pltpu.VMEM((moving, 2 * tile, wide), f32),
             pltpu.VMEM((planes, tile, wide), f32),
-            pltpu.VMEM((planes, 3 * tile, wide), f32),
-            pltpu.VMEM((planes, 3 * tile, wide), f32),
+            pltpu.VMEM((planes, 2 * tile, wide), f32),
+            pltpu.VMEM((planes, 2 * tile, wide), f32),
         ],
-    )(stokes, tips, from_west, from_east, mask, begun, packs, force, edge, above, below, middle, ends, part, *sides)
+    )(stokes, tips, from_west, from_east, mask, begun, packs, force, edge, above, below, middle, ends, part, twos, *sides)
     new_state = call(
         whole_body,
         jax.ShapeDtypeStruct(state.shape, f32),

time: 68.8 us -> 68.2 us (level)
  no operation moved by 1% of the time
where the time goes in v7:
time: 68.2 us; the launch traced here: 67.9 us
  waiting for transfers between devices  33.3 us (49%)
  starting transfers between devices  19.8 us (29%)
  Pallas kernels  13.7 us (20%)
  between operations  0.86 us (1%)
    all_to_all x2, waiting for transfers between devices, exchanged(): lax.all_to_all(payload, 'gy', split_axis=0, concat_axis=0, tiled=True, ax...  15.3 us
    all_to_all x2, starting transfers between devices, exchanged(): lax.all_to_all(payload, 'gy', split_axis=0, concat_axis=0, tiled=True, ax...  9.87 us
    ppermute x1, waiting for transfers between devices, per_device(): sums = lax.ppermute(sums, 'gy', mirrored)  6.98 us
    all_to_all x1, waiting for transfers between devices, per_device(): lax.all_to_all(parts, ('gy', 'gx'), split_axis=0, concat_axis=0, tiled=True)  6.24 us
    pallas_call x2, Pallas kernels, gathered(): call(functools.partial(gather_body, capacity, slots, far), jax.ShapeDtype...  5.41 us
    all_to_all x1, starting transfers between devices, per_device(): lax.all_to_all(parts, ('gy', 'gx'), split_axis=0, concat_axis=0, tiled=True)  5.05 us
    ppermute x1, waiting for transfers between devices, per_device(): stokes = lax.ppermute(stokes.astype(jnp.float16), 'gy', mirrored)  3.7 us
    ppermute x1, starting transfers between devices, per_device(): sums = lax.ppermute(sums, 'gy', mirrored)  2.66 us
  transfers between devices with their start and end apart: 9, of which 6 were waited for; matrix products, arithmetic and copies ran while one was open for 0% of the time, Pallas kernels for 11%

profile of v7, /device:TPU:0, one launch (start us, length us, event | category | flops | bytes accessed | tf_op | source)
XLA Modules:
  0.0 67.9 jit_solution(5418578857024643575)
XLA Ops:
  0.6 2.6 %shard_map.79 = bf16[64,6272]{1,0:T(8,128)(2,1)} custom-call(s32[1,64]{1,0:T(1,128)} %bitcast.18, s32[1,64]{1,0:T(1,128)} %bitcast.20, s32[1,64]{1,0:T(1,128)} %bitcast.22, bf16[64,24,256]{2,1,0:T(8,128)(2,1)} %refs_3_.3), custom_call_target="tpu_custom_call" | custom-call | flops 402653184 | bytes 1572864 | tf_op jit(solution)/shard_map/pallas_call | solution.py:517
  3.3 0.0 copy-start
  3.3 0.0 copy-start.1
  3.3 6.3 %all-to-all-start = ((bf16[8,8,6272]{2,1,0:T(8,128)(2,1)}), bf16[8,8,6272]{2,1,0:T(8,128)(2,1)S(1)}, u32[]{:S(2)}, u32[]{:S(2)}) async-start(bf16[8,8,6272]{2,1,0:T(8,128)(2,1)} %bitcast.17), calls=%async_computation | async-start | bytes 1605632 | tf_op jit(solution)/shard_map/all_to_all | solution.py:534
  9.6 0.0 copy-done
  9.6 0.0 copy-done.1
  9.6 0.3 shard_map.77
  9.9 0.1 collective-permute-start
  10.0 2.8 %shard_map.81 = bf16[64,6272]{1,0:T(8,128)(2,1)} custom-call(s32[1,64]{1,0:T(1,128)} %bitcast.19, s32[1,64]{1,0:T(1,128)} %bitcast.21, s32[1,64]{1,0:T(1,128)} %bitcast.23, bf16[64,24,256]{2,1,0:T(8,128)(2,1)} %refs_3_.3), custom_call_target="tpu_custom_call" | custom-call | flops 402653184 | bytes 1572864 | tf_op jit(solution)/shard_map/pallas_call | solution.py:517
  12.8 0.0 collective-permute-done
  12.8 1.6 %shard_map.78 = (f32[24,8,256]{2,1,0:T(8,128)S(1)}, f32[32,384]{1,0:T(8,128)S(1)}, f32[24,32,256]{2,1,0:T(8,128)S(1)}, f32[2,32,128]{2,1,0:T(8,128)S(1)}, f32[8,128]{1,0:T(8,128)S(1)}) custom-call(f32[24,32,256]{2,1,0:T(8,128)S(1)} %bitcast.15, s32[32,256]{1,0:T(8,128)S(1)} %copy-done.1, f32[32,128]{1,0:T(8,128)S(1)} %get-tuple-element.57.west_ref, ...), custom_call_target="tpu_custom_call" | custom-call | flops 5898240 | bytes 3538944 | tf_op jit(solution)/shard_map/pallas_call | solution.py:548
  14.4 7.1 %all-to-all-done = bf16[8,8,6272]{2,1,0:T(8,128)(2,1)S(1)} async-done(((bf16[8,8,6272]{2,1,0:T(8,128)(2,1)}), bf16[8,8,6272]{2,1,0:T(8,128)(2,1)S(1)}, u32[]{:S(2)}, u32[]{:S(2)}) %all-to-all-start) | async-done | bytes 802848 | tf_op jit(solution)/shard_map/all_to_all | solution.py:534
  21.5 0.3 shard_map.80
  21.9 2.7 %collective-permute-start.1 = (f16[32,4224]{1,0:T(8,128)(2,1)S(1)}, f16[32,4224]{1,0:T(8,128)(2,1)S(1)}, u32[]{:S(2)}, u32[]{:S(2)}) collective-permute-start(f16[32,4224]{1,0:T(8,128)(2,1)S(1)} %convert_element_type.27), channel_id=1, source_target_pairs={{0,16},{2,18},{4,20},{6,22},{8,24},{10,26},{12,28},{14,30},{16,0},... | collective-permute-start | bytes 811016 | tf_op jit(solution)/shard_map/ppermute | solution.py:573
  24.5 3.5 %all-to-all-start.1 = ((bf16[8,8,6272]{2,1,0:T(8,128)(2,1)}), bf16[8,8,6272]{2,1,0:T(8,128)(2,1)S(1)}, u32[]{:S(2)}, u32[]{:S(2)}) async-start(bf16[8,8,6272]{2,1,0:T(8,128)(2,1)} %bitcast.6), calls=%async_computation.1 | async-start | bytes 1605632 | tf_op jit(solution)/shard_map/all_to_all | solution.py:534
  28.1 7.0 %collective-permute-done.1 = f16[32,4224]{1,0:T(8,128)(2,1)S(1)} collective-permute-done((f16[32,4224]{1,0:T(8,128)(2,1)S(1)}, f16[32,4224]{1,0:T(8,128)(2,1)S(1)}, u32[]{:S(2)}, u32[]{:S(2)}) %collective-permute-start.1) | collective-permute-done | bytes 270368 | tf_op jit(solution)/shard_map/ppermute | solution.py:573
  35.1 8.2 %all-to-all-done.1 = bf16[8,8,6272]{2,1,0:T(8,128)(2,1)S(1)} async-done(((bf16[8,8,6272]{2,1,0:T(8,128)(2,1)}), bf16[8,8,6272]{2,1,0:T(8,128)(2,1)S(1)}, u32[]{:S(2)}, u32[]{:S(2)}) %all-to-all-start.1) | async-done | bytes 802848 | tf_op jit(solution)/shard_map/all_to_all | solution.py:534
  43.3 0.4 shard_map.83
  43.7 0.1 collective-permute-start.2
  43.8 0.1 collective-permute-start.3
  43.9 1.1 %collective-permute-done.2.refs_0_.refs_4_ = f32[32,128]{1,0:T(8,128)S(1)} collective-permute-done((f32[32,128]{1,0:T(8,128)S(1)}, f32[32,128]{1,0:T(8,128)S(1)}, u32[]{:S(2)}, u32[]{:S(2)}) %collective-permute-start.2) | collective-permute-done | bytes 16416 | tf_op jit(solution)/shard_map/ppermute | solution.py:591
  45.0 0.1 shard_map.85
  45.0 0.1 select_convert_fusion.1
  45.1 1.4 %collective-permute-start.4 = (f16[43,4,256]{2,1,0:T(4,128)(2,1)S(1)}, f16[43,4,256]{2,1,0:T(4,128)(2,1)S(1)}, u32[]{:S(2)}, u32[]{:S(2)}) collective-permute-start(f16[43,4,256]{2,1,0:T(4,128)(2,1)S(1)} %get-tuple-element.52), channel_id=1, source_target_pairs={{0,2},{2,0},{4,6},{6,4},{8,10},{10,8},{12,14},{14,12},{16,18},{18,... | collective-permute-start | bytes 264200 | tf_op jit(solution)/shard_map/ppermute | solution.py:600
  46.5 0.7 collective-permute-start.5
  47.1 2.0 %shard_map.84 = (f32[3,8,16,256]{3,2,1,0:T(8,128)S(1)}, f32[3,8,16,256]{3,2,1,0:T(8,128)S(1)}, f32[1,128]{1,0:T(1,128)S(1)}, f32[24,8,384]{2,1,0:T(8,128)S(1)}) custom-call(f32[32,384]{1,0:T(8,128)S(1)} %get-tuple-element.29.mask_ref, f32[24,32,256]{2,1,0:T(8,128)S(1)} %get-tuple-element.30.begun_ref, f32[2,32,128]{2,1,0:T(8,128)S(1)} %get-tuple-element.31.packs_ref, ...), custom_call_target="tpu_custom_call" | custom-call | flops 17694720 | bytes 2359296 | tf_op jit(solution)/shard_map/pallas_call | solution.py:603
  49.2 3.7 %collective-permute-done.3 = f16[32,2048]{1,0:T(8,128)(2,1)S(1)} collective-permute-done((f16[32,2048]{1,0:T(8,128)(2,1)S(1)}, f16[32,2048]{1,0:T(8,128)(2,1)S(1)}, u32[]{:S(2)}, u32[]{:S(2)}) %collective-permute-start.3) | collective-permute-done | bytes 131104 | tf_op jit(solution)/shard_map/ppermute | solution.py:575
  52.9 0.0 collective-permute-done.4
  52.9 0.0 collective-permute-done.5
  52.9 0.1 convert_select_fusion
  53.0 1.9 %shard_map.86 = (f32[3,8,16,256]{3,2,1,0:T(8,128)S(1)}, f32[32,128]{1,0:T(8,128)}) custom-call(f32[32,2048]{1,0:T(8,128)S(1)} %convert_element_type.31.stokes_ref, f32[24,8,256]{2,1,0:T(8,128)S(1)} %get-tuple-element.44.tips_ref, f32[32,128]{1,0:T(8,128)S(1)} %get-tuple-element.57.west_ref, f32[32,128]{1,0:T(8,128)S(1)} %get-tuple-element.56.east_ref, ...), custom_call_target="tpu_custom_call" | custom-call | flops 13271040 | bytes 1769472 | tf_op jit(solution)/shard_map/pallas_call | solution.py:621
  54.9 5.1 %all-to-all-start.2 = ((f32[32,1,128]{2,1,0:T(1,128)}), f32[32,1,128]{2,1,0:T(1,128)S(1)}, u32[]{:S(2)}, u32[]{:S(2)}) async-start(f32[32,1,128]{2,1,0:T(1,128)} %bitcast.9), calls=%async_computation.2 | async-start | bytes 32768 | tf_op jit(solution)/shard_map/all_to_all | solution.py:643
  60.0 0.9 %shard_map.87 = f32[3,8,32,256]{3,2,1,0:T(8,128)} custom-call(f32[3,8,16,256]{3,2,1,0:T(8,128)S(1)} %get-tuple-element.40.refs_0_.middle_ref, f32[3,8,16,256]{3,2,1,0:T(8,128)S(1)} %get-tuple-element.50.ends_ref), custom_call_target="tpu_custom_call" | custom-call | bytes 1572864 | tf_op jit(solution)/shard_map/pallas_call | solution.py:636
  60.9 6.2 %all-to-all-done.2 = f32[32,1,128]{2,1,0:T(1,128)S(1)} async-done(((f32[32,1,128]{2,1,0:T(1,128)}), f32[32,1,128]{2,1,0:T(1,128)S(1)}, u32[]{:S(2)}, u32[]{:S(2)}) %all-to-all-start.2) | async-done | bytes 16416 | tf_op jit(solution)/shard_map/all_to_all | solution.py:643
  67.1 0.8 %shard_map.88 = f32[3,32]{1,0:T(4,128)} custom-call(f32[32,128]{1,0:T(8,128)S(1)} %bitcast.16), custom_call_target="tpu_custom_call" | custom-call | tf_op jit(solution)/shard_map/pallas_call | solution.py:644
  (8 shorter events, 0.1 us)
Async XLA Ops:
  3.3 6.4 %copy-start = (f32[3,8,32,256]{3,2,1,0:T(8,128)S(1)}, f32[3,8,32,256]{3,2,1,0:T(8,128)}, u32[]{:S(2)}) copy-start(f32[3,8,32,256]{3,2,1,0:T(8,128)} %param.6) | copy-start | bytes 2359300
  3.3 6.3 %copy-start.1 = (s32[32,256]{1,0:T(8,128)S(1)}, s32[32,256]{1,0:T(8,128)}, u32[]{:S(2)}) copy-start(s32[32,256]{1,0:T(8,128)} %wet_ref.3) | copy-start | bytes 98308
  3.3 18.2 %all-to-all-start = ((bf16[8,8,6272]{2,1,0:T(8,128)(2,1)}), bf16[8,8,6272]{2,1,0:T(8,128)(2,1)S(1)}, u32[]{:S(2)}, u32[]{:S(2)}) async-start(bf16[8,8,6272]{2,1,0:T(8,128)(2,1)} %bitcast.17), calls=%async_computation | async-start | bytes 1605632 | tf_op jit(solution)/shard_map/all_to_all | solution.py:534
  9.9 2.9 %collective-permute-start = (f32[32,128]{1,0:T(8,128)S(1)}, f32[32,128]{1,0:T(8,128)S(1)}, u32[]{:S(2)}, u32[]{:S(2)}) collective-permute-start(f32[32,128]{1,0:T(8,128)S(1)} %broadcast_select_fusion.2), channel_id=1, source_target_pairs={{0,1},{1,0},{2,3},{3,2},{4,5},{5,4},{6,7},{7,6},{8,9},{9,8},{10,11... | collective-permute-start | bytes 49160 | tf_op jit(solution)/shard_map/ppermute | solution.py:543
  21.9 13.2 %collective-permute-start.1 = (f16[32,4224]{1,0:T(8,128)(2,1)S(1)}, f16[32,4224]{1,0:T(8,128)(2,1)S(1)}, u32[]{:S(2)}, u32[]{:S(2)}) collective-permute-start(f16[32,4224]{1,0:T(8,128)(2,1)S(1)} %convert_element_type.27), channel_id=1, source_target_pairs={{0,16},{2,18},{4,20},{6,22},{8,24},{10,26},{12,28},{14,30},{16,0},... | collective-permute-start | bytes 811016 | tf_op jit(solution)/shard_map/ppermute | solution.py:573
  24.5 18.7 %all-to-all-start.1 = ((bf16[8,8,6272]{2,1,0:T(8,128)(2,1)}), bf16[8,8,6272]{2,1,0:T(8,128)(2,1)S(1)}, u32[]{:S(2)}, u32[]{:S(2)}) async-start(bf16[8,8,6272]{2,1,0:T(8,128)(2,1)} %bitcast.6), calls=%async_computation.1 | async-start | bytes 1605632 | tf_op jit(solution)/shard_map/all_to_all | solution.py:534
  43.7 1.2 %collective-permute-start.2 = (f32[32,128]{1,0:T(8,128)S(1)}, f32[32,128]{1,0:T(8,128)S(1)}, u32[]{:S(2)}, u32[]{:S(2)}) collective-permute-start(f32[32,128]{1,0:T(8,128)S(1)} %get-tuple-element.39.edge_ref), channel_id=1, source_target_pairs={{0,1},{1,0},{2,3},{3,2},{4,5},{5,4},{6,7},{7,6},{8,9},{9,8},{10,11... | collective-permute-start | bytes 49160 | tf_op jit(solution)/shard_map/ppermute | solution.py:591
  43.8 9.1 %collective-permute-start.3 = (f16[32,2048]{1,0:T(8,128)(2,1)S(1)}, f16[32,2048]{1,0:T(8,128)(2,1)S(1)}, u32[]{:S(2)}, u32[]{:S(2)}) collective-permute-start(f16[32,2048]{1,0:T(8,128)(2,1)S(1)} %convert_element_type.30), channel_id=1, source_target_pairs={{0,16},{2,18},{4,20},{6,22},{8,24},{10,26},{12,28},{14,30},{16,0},... | collective-permute-start | bytes 393224 | tf_op jit(solution)/shard_map/ppermute | solution.py:575
  45.1 7.8 %collective-permute-start.4 = (f16[43,4,256]{2,1,0:T(4,128)(2,1)S(1)}, f16[43,4,256]{2,1,0:T(4,128)(2,1)S(1)}, u32[]{:S(2)}, u32[]{:S(2)}) collective-permute-start(f16[43,4,256]{2,1,0:T(4,128)(2,1)S(1)} %get-tuple-element.52), channel_id=1, source_target_pairs={{0,2},{2,0},{4,6},{6,4},{8,10},{10,8},{12,14},{14,12},{16,18},{18,... | collective-permute-start | bytes 264200 | tf_op jit(solution)/shard_map/ppermute | solution.py:600
  46.5 6.4 %collective-permute-start.5 = (f16[43,4,256]{2,1,0:T(4,128)(2,1)S(1)}, f16[43,4,256]{2,1,0:T(4,128)(2,1)S(1)}, u32[]{:S(2)}, u32[]{:S(2)}) collective-permute-start(f16[43,4,256]{2,1,0:T(4,128)(2,1)S(1)} %get-tuple-element.53), channel_id=1, source_target_pairs={{2,4},{4,2},{6,8},{8,6},{10,12},{12,10},{14,16},{16,14},{18,20},{2... | collective-permute-start | bytes 264200 | tf_op jit(solution)/shard_map/ppermute | solution.py:599
  54.9 12.2 %all-to-all-start.2 = ((f32[32,1,128]{2,1,0:T(1,128)}), f32[32,1,128]{2,1,0:T(1,128)S(1)}, u32[]{:S(2)}, u32[]{:S(2)}) async-start(f32[32,1,128]{2,1,0:T(1,128)} %bitcast.9), calls=%async_computation.2 | async-start | bytes 32768 | tf_op jit(solution)/shard_map/all_to_all | solution.py:643

commit v8 on v7

--- a/solution.py
+++ b/solution.py
@@ -245,19 +245,35 @@
     return jnp.concatenate([plane, side_tile(west, at, east, at)], axis=1)
 
 
+def places(planes, sides):
+    levels = planes // 3
+    counts = [RIM] * levels + [EDGE] * (2 * levels) + [EDGE] * levels + [EDGE - 1] * levels + [EDGE] * (2 + (sides + 2) // 2)
+    starts = [sum(counts[:k]) for k in range(len(counts))]
+    return list(zip(starts, counts))
+
+
 def outer_body(force_ref, edge_ref, tips_ref, mask_ref, west_ref, east_ref, *refs):
     sides, (up_ref, down_ref) = refs[:-2], refs[-2:]
     planes, rows, cols = force_ref.shape
     moving = 2 * planes // 3
-    ends = ((up_ref, slice(rows - RIM, rows), slice(RIM, 2 * RIM)), (down_ref, slice(0, RIM), slice(0, RIM)))
-    for out_ref, at, tip in ends:
-        out_ref[:moving] = force_ref[:moving, at] * FORCE_SCALE
-        out_ref[moving : moving + planes] = tips_ref[:, tip] * STATE_SCALE
-        out_ref[moving + planes] = mask_ref[at, :cols] * STATE_SCALE
-        parts = [west_ref[at], east_ref[at], edge_ref[at]] + [side[at] for side in sides]
-        for k, part in enumerate(parts):
+    where = places(planes, len(sides))
+    for out_ref, up in ((up_ref, True), (down_ref, False)):
+
+        def put(place, ref, index, scale, lanes=slice(None)):
+            start, count = where[place]
+            at = slice(ref.shape[len(index)] - count, None) if up else slice(0, count)
+            out_ref[start : start + count, lanes] = ref[(*index, at, slice(0, cols))] * scale
+
+        out_ref[where[-1][0] :] = jnp.zeros((out_ref.shape[0] - where[-1][0], cols), jnp.float32)
+        for j in range(planes):
+            put(j, tips_ref, (j,), STATE_SCALE)
+        for j in range(moving):
+            put(planes + j, force_ref, (j,), FORCE_SCALE)
+        put(planes + moving, mask_ref, (), STATE_SCALE)
+        for k, part in enumerate((west_ref, east_ref, edge_ref, *sides)):
             lane = (k % 2) * LANES
-            out_ref[moving + planes + 1 + k // 2, :, lane : lane + LANES] = part * (STATE_SCALE if k < 2 else FORCE_SCALE)
+            scale = STATE_SCALE if k < 2 else FORCE_SCALE
+            put(planes + moving + 1 + k // 2, part, (), scale, slice(lane, lane + LANES))
 
 
 def factors(mask, own, west, east, force_rows, push_ref):
@@ -364,12 +380,17 @@
     tile = 2 * RIM
     total = 2 * tile
 
-    def joined(index, scale):
-        return jnp.concatenate([north_ref[index], south_ref[index]], axis=0) * (1.0 / scale)
+    where = places(planes, sides)
+
+    def joined(place, scale):
+        start, count = where[place]
+        at = slice(start, start + count)
+        parts = [north_ref[at], jnp.zeros((tile - 2 * count, cols), jnp.float32), south_ref[at]]
+        return jnp.concatenate([part for part in parts if part.shape[0]], axis=0) * (1.0 / scale)
 
     def half_of(k, scale):
         lane = (k % 2) * LANES
-        return joined(moving + planes + 1 + k // 2, scale)[:, lane : lane + LANES]
+        return joined(planes + moving + 1 + k // 2, scale)[:, lane : lane + LANES]
 
     beside = [half_of(k, STATE_SCALE) for k in range(2)]
     outer = [half_of(2 + k, FORCE_SCALE) for k in range(1 + sides)]
@@ -377,15 +398,15 @@
     own = jnp.concatenate([outer_rows(edge_ref), outer[0]], axis=0)
 
     def halo(index, at):
-        return widened(joined(moving + index, STATE_SCALE), *beside, at)
-
-    mask = jnp.concatenate([outer_rows(mask_ref), halo(planes, EDGE * planes)], axis=0)
+        return widened(joined(index, STATE_SCALE), *beside, at)
+
+    mask = jnp.concatenate([outer_rows(mask_ref), halo(planes + moving, EDGE * planes)], axis=0)
     relax = factors(
         mask,
         own,
         edges[0],
         edges[-1],
-        lambda j: jnp.concatenate([outer_rows(force_ref, j), joined(j, FORCE_SCALE)], axis=0),
+        lambda j: jnp.concatenate([outer_rows(force_ref, j), joined(planes + j, FORCE_SCALE)], axis=0),
         push_ref,
     )
     for j in range(planes):
@@ -591,7 +612,8 @@
         sides = [lax.ppermute(edge, "gx", swapped)]
     else:
         sides = [lax.ppermute(edge, "gx", eastward), lax.ppermute(edge, "gx", westward)]
-    outer = jax.ShapeDtypeStruct((moving + planes + 1 + (len(sides) + 4) // 2, RIM, cols), f32)
+    start, count = places(planes, len(sides))[-1]
+    outer = jax.ShapeDtypeStruct(((start + count + 7) // 8 * 8, cols), f32)
     up, down = call(outer_body, (outer, outer), moved=16 * (moving + planes) * RIM * cols)(
         force, edge, tips, mask, from_west, from_east, *sides
     )

time: 68.2 us -> 67.8 us (level)
  no operation moved by 1% of the time
where the time goes in v8:
time: 67.8 us; the launch traced here: 67.5 us
  waiting for transfers between devices  33.3 us (49%)
  starting transfers between devices  19.4 us (29%)
  Pallas kernels  13.7 us (20%)
  between operations  0.85 us (1%)
    all_to_all x2, waiting for transfers between devices, exchanged(): lax.all_to_all(payload, 'gy', split_axis=0, concat_axis=0, tiled=True, ax...  15.3 us
    all_to_all x2, starting transfers between devices, exchanged(): lax.all_to_all(payload, 'gy', split_axis=0, concat_axis=0, tiled=True, ax...  9.87 us
    ppermute x1, waiting for transfers between devices, per_device(): sums = lax.ppermute(sums, 'gy', mirrored)  6.98 us
    all_to_all x1, waiting for transfers between devices, per_device(): lax.all_to_all(parts, ('gy', 'gx'), split_axis=0, concat_axis=0, tiled=True)  6.24 us
    pallas_call x2, Pallas kernels, gathered(): call(functools.partial(gather_body, capacity, slots, far), jax.ShapeDtype...  5.41 us
    all_to_all x1, starting transfers between devices, per_device(): lax.all_to_all(parts, ('gy', 'gx'), split_axis=0, concat_axis=0, tiled=True)  4.66 us
    ppermute x1, waiting for transfers between devices, per_device(): stokes = lax.ppermute(stokes.astype(jnp.float16), 'gy', mirrored)  3.71 us
    ppermute x1, starting transfers between devices, per_device(): sums = lax.ppermute(sums, 'gy', mirrored)  2.66 us
  transfers between devices with their start and end apart: 9, of which 6 were waited for; matrix products, arithmetic and copies ran while one was open for 0% of the time, Pallas kernels for 11%

profile of v8, /device:TPU:0, one launch (start us, length us, event | category | flops | bytes accessed | tf_op | source)
XLA Modules:
  0.0 67.5 jit_solution(10519370649104243357)
XLA Ops:
  0.6 2.6 %shard_map.79 = bf16[64,6272]{1,0:T(8,128)(2,1)} custom-call(s32[1,64]{1,0:T(1,128)} %bitcast.18, s32[1,64]{1,0:T(1,128)} %bitcast.20, s32[1,64]{1,0:T(1,128)} %bitcast.22, bf16[64,24,256]{2,1,0:T(8,128)(2,1)} %refs_3_.3), custom_call_target="tpu_custom_call" | custom-call | flops 402653184 | bytes 1572864 | tf_op jit(solution)/shard_map/pallas_call | solution.py:538
  3.3 0.0 copy-start
  3.3 0.0 copy-start.1
  3.3 6.3 %all-to-all-start = ((bf16[8,8,6272]{2,1,0:T(8,128)(2,1)}), bf16[8,8,6272]{2,1,0:T(8,128)(2,1)S(1)}, u32[]{:S(2)}, u32[]{:S(2)}) async-start(bf16[8,8,6272]{2,1,0:T(8,128)(2,1)} %bitcast.17), calls=%async_computation | async-start | bytes 1605632 | tf_op jit(solution)/shard_map/all_to_all | solution.py:555
  9.6 0.0 copy-done
  9.6 0.0 copy-done.1
  9.6 0.3 shard_map.77
  9.9 0.1 collective-permute-start
  10.0 2.8 %shard_map.81 = bf16[64,6272]{1,0:T(8,128)(2,1)} custom-call(s32[1,64]{1,0:T(1,128)} %bitcast.19, s32[1,64]{1,0:T(1,128)} %bitcast.21, s32[1,64]{1,0:T(1,128)} %bitcast.23, bf16[64,24,256]{2,1,0:T(8,128)(2,1)} %refs_3_.3), custom_call_target="tpu_custom_call" | custom-call | flops 402653184 | bytes 1572864 | tf_op jit(solution)/shard_map/pallas_call | solution.py:538
  12.8 0.0 collective-permute-done
  12.8 1.6 %shard_map.78 = (f32[24,8,256]{2,1,0:T(8,128)S(1)}, f32[32,384]{1,0:T(8,128)S(1)}, f32[24,32,256]{2,1,0:T(8,128)S(1)}, f32[2,32,128]{2,1,0:T(8,128)S(1)}, f32[8,128]{1,0:T(8,128)S(1)}) custom-call(f32[24,32,256]{2,1,0:T(8,128)S(1)} %bitcast.15, s32[32,256]{1,0:T(8,128)S(1)} %copy-done.1, f32[32,128]{1,0:T(8,128)S(1)} %get-tuple-element.57.west_ref, ...), custom_call_target="tpu_custom_call" | custom-call | flops 5898240 | bytes 3538944 | tf_op jit(solution)/shard_map/pallas_call | solution.py:569
  14.4 7.1 %all-to-all-done = bf16[8,8,6272]{2,1,0:T(8,128)(2,1)S(1)} async-done(((bf16[8,8,6272]{2,1,0:T(8,128)(2,1)}), bf16[8,8,6272]{2,1,0:T(8,128)(2,1)S(1)}, u32[]{:S(2)}, u32[]{:S(2)}) %all-to-all-start) | async-done | bytes 802848 | tf_op jit(solution)/shard_map/all_to_all | solution.py:555
  21.5 0.3 shard_map.80
  21.9 2.7 %collective-permute-start.1 = (f16[32,4224]{1,0:T(8,128)(2,1)S(1)}, f16[32,4224]{1,0:T(8,128)(2,1)S(1)}, u32[]{:S(2)}, u32[]{:S(2)}) collective-permute-start(f16[32,4224]{1,0:T(8,128)(2,1)S(1)} %convert_element_type.27), channel_id=1, source_target_pairs={{0,16},{2,18},{4,20},{6,22},{8,24},{10,26},{12,28},{14,30},{16,0},... | collective-permute-start | bytes 811016 | tf_op jit(solution)/shard_map/ppermute | solution.py:594
  24.5 3.5 %all-to-all-start.1 = ((bf16[8,8,6272]{2,1,0:T(8,128)(2,1)}), bf16[8,8,6272]{2,1,0:T(8,128)(2,1)S(1)}, u32[]{:S(2)}, u32[]{:S(2)}) async-start(bf16[8,8,6272]{2,1,0:T(8,128)(2,1)} %bitcast.6), calls=%async_computation.1 | async-start | bytes 1605632 | tf_op jit(solution)/shard_map/all_to_all | solution.py:555
  28.1 7.0 %collective-permute-done.1 = f16[32,4224]{1,0:T(8,128)(2,1)S(1)} collective-permute-done((f16[32,4224]{1,0:T(8,128)(2,1)S(1)}, f16[32,4224]{1,0:T(8,128)(2,1)S(1)}, u32[]{:S(2)}, u32[]{:S(2)}) %collective-permute-start.1) | collective-permute-done | bytes 270368 | tf_op jit(solution)/shard_map/ppermute | solution.py:594
  35.1 8.2 %all-to-all-done.1 = bf16[8,8,6272]{2,1,0:T(8,128)(2,1)S(1)} async-done(((bf16[8,8,6272]{2,1,0:T(8,128)(2,1)}), bf16[8,8,6272]{2,1,0:T(8,128)(2,1)S(1)}, u32[]{:S(2)}, u32[]{:S(2)}) %all-to-all-start.1) | async-done | bytes 802848 | tf_op jit(solution)/shard_map/all_to_all | solution.py:555
  43.3 0.4 shard_map.83
  43.7 0.1 collective-permute-start.2
  43.8 0.1 collective-permute-start.3
  43.9 1.1 %collective-permute-done.2.refs_0_.refs_4_ = f32[32,128]{1,0:T(8,128)S(1)} collective-permute-done((f32[32,128]{1,0:T(8,128)S(1)}, f32[32,128]{1,0:T(8,128)S(1)}, u32[]{:S(2)}, u32[]{:S(2)}) %collective-permute-start.2) | collective-permute-done | bytes 16416 | tf_op jit(solution)/shard_map/ppermute | solution.py:612
  45.0 0.1 shard_map.85
  45.1 1.4 %collective-permute-start.4 = (f16[136,256]{1,0:T(8,128)(2,1)S(1)}, f16[136,256]{1,0:T(8,128)(2,1)S(1)}, u32[]{:S(2)}, u32[]{:S(2)}) collective-permute-start(f16[136,256]{1,0:T(8,128)(2,1)S(1)} %get-tuple-element.52), channel_id=1, source_target_pairs={{0,2},{2,0},{4,6},{6,4},{8,10},{10,8},{12,14},{14,12},{16,18},{18,... | collective-permute-start | bytes 208904 | tf_op jit(solution)/shard_map/ppermute | solution.py:622
  46.5 0.7 collective-permute-start.5
  47.1 2.0 %shard_map.84 = (f32[3,8,16,256]{3,2,1,0:T(8,128)S(1)}, f32[3,8,16,256]{3,2,1,0:T(8,128)S(1)}, f32[1,128]{1,0:T(1,128)S(1)}, f32[24,8,384]{2,1,0:T(8,128)S(1)}) custom-call(f32[32,384]{1,0:T(8,128)S(1)} %get-tuple-element.29.mask_ref, f32[24,32,256]{2,1,0:T(8,128)S(1)} %get-tuple-element.30.begun_ref, f32[2,32,128]{2,1,0:T(8,128)S(1)} %get-tuple-element.31.packs_ref, ...), custom_call_target="tpu_custom_call" | custom-call | flops 17694720 | bytes 2359296 | tf_op jit(solution)/shard_map/pallas_call | solution.py:625
  49.2 3.7 %collective-permute-done.3 = f16[32,2048]{1,0:T(8,128)(2,1)S(1)} collective-permute-done((f16[32,2048]{1,0:T(8,128)(2,1)S(1)}, f16[32,2048]{1,0:T(8,128)(2,1)S(1)}, u32[]{:S(2)}, u32[]{:S(2)}) %collective-permute-start.3) | collective-permute-done | bytes 131104 | tf_op jit(solution)/shard_map/ppermute | solution.py:596
  52.9 0.0 collective-permute-done.4
  52.9 0.0 collective-permute-done.5
  53.0 1.9 %shard_map.86 = (f32[3,8,16,256]{3,2,1,0:T(8,128)S(1)}, f32[32,128]{1,0:T(8,128)}) custom-call(f32[32,2048]{1,0:T(8,128)S(1)} %convert_element_type.31.stokes_ref, f32[24,8,256]{2,1,0:T(8,128)S(1)} %get-tuple-element.44.tips_ref, f32[32,128]{1,0:T(8,128)S(1)} %get-tuple-element.57.west_ref, f32[32,128]{1,0:T(8,128)S(1)} %get-tuple-element.56.east_ref, ...), custom_call_target="tpu_custom_call" | custom-call | flops 13271040 | bytes 1769472 | tf_op jit(solution)/shard_map/pallas_call | solution.py:643
  54.9 4.7 %all-to-all-start.2 = ((f32[32,1,128]{2,1,0:T(1,128)}), f32[32,1,128]{2,1,0:T(1,128)S(1)}, u32[]{:S(2)}, u32[]{:S(2)}) async-start(f32[32,1,128]{2,1,0:T(1,128)} %bitcast.9), calls=%async_computation.2 | async-start | bytes 32768 | tf_op jit(solution)/shard_map/all_to_all | solution.py:665
  59.5 0.9 %shard_map.87 = f32[3,8,32,256]{3,2,1,0:T(8,128)} custom-call(f32[3,8,16,256]{3,2,1,0:T(8,128)S(1)} %get-tuple-element.40.refs_0_.middle_ref, f32[3,8,16,256]{3,2,1,0:T(8,128)S(1)} %get-tuple-element.50.ends_ref), custom_call_target="tpu_custom_call" | custom-call | bytes 1572864 | tf_op jit(solution)/shard_map/pallas_call | solution.py:658
  60.4 6.2 %all-to-all-done.2 = f32[32,1,128]{2,1,0:T(1,128)S(1)} async-done(((f32[32,1,128]{2,1,0:T(1,128)}), f32[32,1,128]{2,1,0:T(1,128)S(1)}, u32[]{:S(2)}, u32[]{:S(2)}) %all-to-all-start.2) | async-done | bytes 16416 | tf_op jit(solution)/shard_map/all_to_all | solution.py:665
  66.7 0.8 %shard_map.88 = f32[3,32]{1,0:T(4,128)} custom-call(f32[32,128]{1,0:T(8,128)S(1)} %bitcast.16), custom_call_target="tpu_custom_call" | custom-call | tf_op jit(solution)/shard_map/pallas_call | solution.py:666
  (10 shorter events, 0.2 us)
Async XLA Ops:
  3.3 6.4 %copy-start = (f32[3,8,32,256]{3,2,1,0:T(8,128)S(1)}, f32[3,8,32,256]{3,2,1,0:T(8,128)}, u32[]{:S(2)}) copy-start(f32[3,8,32,256]{3,2,1,0:T(8,128)} %param.6) | copy-start | bytes 2359300
  3.3 6.3 %copy-start.1 = (s32[32,256]{1,0:T(8,128)S(1)}, s32[32,256]{1,0:T(8,128)}, u32[]{:S(2)}) copy-start(s32[32,256]{1,0:T(8,128)} %wet_ref.3) | copy-start | bytes 98308
  3.3 18.2 %all-to-all-start = ((bf16[8,8,6272]{2,1,0:T(8,128)(2,1)}), bf16[8,8,6272]{2,1,0:T(8,128)(2,1)S(1)}, u32[]{:S(2)}, u32[]{:S(2)}) async-start(bf16[8,8,6272]{2,1,0:T(8,128)(2,1)} %bitcast.17), calls=%async_computation | async-start | bytes 1605632 | tf_op jit(solution)/shard_map/all_to_all | solution.py:555
  9.9 2.9 %collective-permute-start = (f32[32,128]{1,0:T(8,128)S(1)}, f32[32,128]{1,0:T(8,128)S(1)}, u32[]{:S(2)}, u32[]{:S(2)}) collective-permute-start(f32[32,128]{1,0:T(8,128)S(1)} %broadcast_select_fusion.2), channel_id=1, source_target_pairs={{0,1},{1,0},{2,3},{3,2},{4,5},{5,4},{6,7},{7,6},{8,9},{9,8},{10,11... | collective-permute-start | bytes 49160 | tf_op jit(solution)/shard_map/ppermute | solution.py:564
  21.9 13.2 %collective-permute-start.1 = (f16[32,4224]{1,0:T(8,128)(2,1)S(1)}, f16[32,4224]{1,0:T(8,128)(2,1)S(1)}, u32[]{:S(2)}, u32[]{:S(2)}) collective-permute-start(f16[32,4224]{1,0:T(8,128)(2,1)S(1)} %convert_element_type.27), channel_id=1, source_target_pairs={{0,16},{2,18},{4,20},{6,22},{8,24},{10,26},{12,28},{14,30},{16,0},... | collective-permute-start | bytes 811016 | tf_op jit(solution)/shard_map/ppermute | solution.py:594
  24.5 18.7 %all-to-all-start.1 = ((bf16[8,8,6272]{2,1,0:T(8,128)(2,1)}), bf16[8,8,6272]{2,1,0:T(8,128)(2,1)S(1)}, u32[]{:S(2)}, u32[]{:S(2)}) async-start(bf16[8,8,6272]{2,1,0:T(8,128)(2,1)} %bitcast.6), calls=%async_computation.1 | async-start | bytes 1605632 | tf_op jit(solution)/shard_map/all_to_all | solution.py:555
  43.7 1.2 %collective-permute-start.2 = (f32[32,128]{1,0:T(8,128)S(1)}, f32[32,128]{1,0:T(8,128)S(1)}, u32[]{:S(2)}, u32[]{:S(2)}) collective-permute-start(f32[32,128]{1,0:T(8,128)S(1)} %get-tuple-element.39.edge_ref), channel_id=1, source_target_pairs={{0,1},{1,0},{2,3},{3,2},{4,5},{5,4},{6,7},{7,6},{8,9},{9,8},{10,11... | collective-permute-start | bytes 49160 | tf_op jit(solution)/shard_map/ppermute | solution.py:612
  43.8 9.1 %collective-permute-start.3 = (f16[32,2048]{1,0:T(8,128)(2,1)S(1)}, f16[32,2048]{1,0:T(8,128)(2,1)S(1)}, u32[]{:S(2)}, u32[]{:S(2)}) collective-permute-start(f16[32,2048]{1,0:T(8,128)(2,1)S(1)} %convert_element_type.30), channel_id=1, source_target_pairs={{0,16},{2,18},{4,20},{6,22},{8,24},{10,26},{12,28},{14,30},{16,0},... | collective-permute-start | bytes 393224 | tf_op jit(solution)/shard_map/ppermute | solution.py:596
  45.1 7.8 %collective-permute-start.4 = (f16[136,256]{1,0:T(8,128)(2,1)S(1)}, f16[136,256]{1,0:T(8,128)(2,1)S(1)}, u32[]{:S(2)}, u32[]{:S(2)}) collective-permute-start(f16[136,256]{1,0:T(8,128)(2,1)S(1)} %get-tuple-element.52), channel_id=1, source_target_pairs={{0,2},{2,0},{4,6},{6,4},{8,10},{10,8},{12,14},{14,12},{16,18},{18,... | collective-permute-start | bytes 208904 | tf_op jit(solution)/shard_map/ppermute | solution.py:622
  46.5 6.5 %collective-permute-start.5 = (f16[136,256]{1,0:T(8,128)(2,1)S(1)}, f16[136,256]{1,0:T(8,128)(2,1)S(1)}, u32[]{:S(2)}, u32[]{:S(2)}) collective-permute-start(f16[136,256]{1,0:T(8,128)(2,1)S(1)} %get-tuple-element.53), channel_id=1, source_target_pairs={{2,4},{4,2},{6,8},{8,6},{10,12},{12,10},{14,16},{16,14},{18,20},{2... | collective-permute-start | bytes 208904 | tf_op jit(solution)/shard_map/ppermute | solution.py:621
  54.9 11.8 %all-to-all-start.2 = ((f32[32,1,128]{2,1,0:T(1,128)}), f32[32,1,128]{2,1,0:T(1,128)S(1)}, u32[]{:S(2)}, u32[]{:S(2)}) async-start(f32[32,1,128]{2,1,0:T(1,128)} %bitcast.9), calls=%async_computation.2 | async-start | bytes 32768 | tf_op jit(solution)/shard_map/all_to_all | solution.py:665

commit v9 on v8

--- a/solution.py
+++ b/solution.py
@@ -590,10 +590,11 @@
         moved=2 * slots * width + 4 * rows * width,
     )(token, far_rows)
     mirrored = [(i, (i + half) % along) for i in range(along)]
-    sums, near_rows = lax.optimization_barrier((sums.astype(jnp.float16), gathered(False)))
+    halved = (sums.astype(jnp.float16), stokes.astype(jnp.float16), gathered(False))
+    sums, stokes, near_rows = lax.optimization_barrier(halved)
     sums = lax.ppermute(sums, "gy", mirrored)
     arrived = exchanged(near_rows)
-    stokes = lax.ppermute(stokes.astype(jnp.float16), "gy", mirrored)
+    stokes = lax.ppermute(stokes, "gy", mirrored)
     come = call(
         come_body,
         jax.ShapeDtypeStruct((8, LANES), f32),

time: 67.8 us -> 67.8 us (level)
  no operation moved by 1% of the time
where the time goes in v9:
time: 67.8 us; the launch traced here: 67.4 us
  waiting for transfers between devices  33.2 us (49%)
  starting transfers between devices  19.4 us (29%)
  Pallas kernels  13.7 us (20%)
  between operations  0.85 us (1%)
    all_to_all x2, waiting for transfers between devices, exchanged(): lax.all_to_all(payload, 'gy', split_axis=0, concat_axis=0, tiled=True, ax...  15.3 us
    all_to_all x2, starting transfers between devices, exchanged(): lax.all_to_all(payload, 'gy', split_axis=0, concat_axis=0, tiled=True, ax...  9.87 us
    ppermute x1, waiting for transfers between devices, per_device(): sums = lax.ppermute(sums, 'gy', mirrored)  6.98 us
    all_to_all x1, waiting for transfers between devices, per_device(): lax.all_to_all(parts, ('gy', 'gx'), split_axis=0, concat_axis=0, tiled=True)  6.24 us
    pallas_call x2, Pallas kernels, gathered(): call(functools.partial(gather_body, capacity, slots, far), jax.ShapeDtype...  5.41 us
    all_to_all x1, starting transfers between devices, per_device(): lax.all_to_all(parts, ('gy', 'gx'), split_axis=0, concat_axis=0, tiled=True)  4.66 us
    ppermute x1, waiting for transfers between devices, per_device(): stokes = lax.ppermute(stokes, 'gy', mirrored)  3.63 us
    ppermute x1, starting transfers between devices, per_device(): sums = lax.ppermute(sums, 'gy', mirrored)  2.66 us
  transfers between devices with their start and end apart: 9, of which 6 were waited for; matrix products, arithmetic and copies ran while one was open for 0% of the time, Pallas kernels for 11%

profile of v9, /device:TPU:0, one launch (start us, length us, event | category | flops | bytes accessed | tf_op | source)
XLA Modules:
  0.0 67.4 jit_solution(424318850936777938)
XLA Ops:
  0.6 2.6 %shard_map.79 = bf16[64,6272]{1,0:T(8,128)(2,1)} custom-call(s32[1,64]{1,0:T(1,128)} %bitcast.18, s32[1,64]{1,0:T(1,128)} %bitcast.20, s32[1,64]{1,0:T(1,128)} %bitcast.22, bf16[64,24,256]{2,1,0:T(8,128)(2,1)} %refs_3_.3), custom_call_target="tpu_custom_call" | custom-call | flops 402653184 | bytes 1572864 | tf_op jit(solution)/shard_map/pallas_call | solution.py:538
  3.3 0.0 copy-start
  3.3 0.0 copy-start.1
  3.3 6.3 %all-to-all-start = ((bf16[8,8,6272]{2,1,0:T(8,128)(2,1)}), bf16[8,8,6272]{2,1,0:T(8,128)(2,1)S(1)}, u32[]{:S(2)}, u32[]{:S(2)}) async-start(bf16[8,8,6272]{2,1,0:T(8,128)(2,1)} %bitcast.17), calls=%async_computation | async-start | bytes 1605632 | tf_op jit(solution)/shard_map/all_to_all | solution.py:555
  9.6 0.0 copy-done
  9.6 0.0 copy-done.1
  9.6 0.3 shard_map.77
  9.9 0.1 collective-permute-start
  10.0 2.8 %shard_map.81 = bf16[64,6272]{1,0:T(8,128)(2,1)} custom-call(s32[1,64]{1,0:T(1,128)} %bitcast.19, s32[1,64]{1,0:T(1,128)} %bitcast.21, s32[1,64]{1,0:T(1,128)} %bitcast.23, bf16[64,24,256]{2,1,0:T(8,128)(2,1)} %refs_3_.3), custom_call_target="tpu_custom_call" | custom-call | flops 402653184 | bytes 1572864 | tf_op jit(solution)/shard_map/pallas_call | solution.py:538
  12.8 0.0 collective-permute-done
  12.8 1.6 %shard_map.78 = (f32[24,8,256]{2,1,0:T(8,128)S(1)}, f32[32,384]{1,0:T(8,128)S(1)}, f32[24,32,256]{2,1,0:T(8,128)S(1)}, f32[2,32,128]{2,1,0:T(8,128)S(1)}, f32[8,128]{1,0:T(8,128)S(1)}) custom-call(f32[24,32,256]{2,1,0:T(8,128)S(1)} %bitcast.15, s32[32,256]{1,0:T(8,128)S(1)} %copy-done.1, f32[32,128]{1,0:T(8,128)S(1)} %get-tuple-element.59.west_ref, ...), custom_call_target="tpu_custom_call" | custom-call | flops 5898240 | bytes 3538944 | tf_op jit(solution)/shard_map/pallas_call | solution.py:569
  14.4 7.1 %all-to-all-done = bf16[8,8,6272]{2,1,0:T(8,128)(2,1)S(1)} async-done(((bf16[8,8,6272]{2,1,0:T(8,128)(2,1)}), bf16[8,8,6272]{2,1,0:T(8,128)(2,1)S(1)}, u32[]{:S(2)}, u32[]{:S(2)}) %all-to-all-start) | async-done | bytes 802848 | tf_op jit(solution)/shard_map/all_to_all | solution.py:555
  21.5 0.3 shard_map.80
  21.9 2.7 %collective-permute-start.1 = (f16[32,4224]{1,0:T(8,128)(2,1)S(1)}, f16[32,4224]{1,0:T(8,128)(2,1)S(1)}, u32[]{:S(2)}, u32[]{:S(2)}) collective-permute-start(f16[32,4224]{1,0:T(8,128)(2,1)S(1)} %convert_element_type.27), channel_id=1, source_target_pairs={{0,16},{2,18},{4,20},{6,22},{8,24},{10,26},{12,28},{14,30},{16,0},... | collective-permute-start | bytes 811016 | tf_op jit(solution)/shard_map/ppermute | solution.py:595
  24.6 3.5 %all-to-all-start.1 = ((bf16[8,8,6272]{2,1,0:T(8,128)(2,1)}), bf16[8,8,6272]{2,1,0:T(8,128)(2,1)S(1)}, u32[]{:S(2)}, u32[]{:S(2)}) async-start(bf16[8,8,6272]{2,1,0:T(8,128)(2,1)} %bitcast.6), calls=%async_computation.1 | async-start | bytes 1605632 | tf_op jit(solution)/shard_map/all_to_all | solution.py:555
  28.1 7.0 %collective-permute-done.1 = f16[32,4224]{1,0:T(8,128)(2,1)S(1)} collective-permute-done((f16[32,4224]{1,0:T(8,128)(2,1)S(1)}, f16[32,4224]{1,0:T(8,128)(2,1)S(1)}, u32[]{:S(2)}, u32[]{:S(2)}) %collective-permute-start.1) | collective-permute-done | bytes 270368 | tf_op jit(solution)/shard_map/ppermute | solution.py:595
  35.1 8.2 %all-to-all-done.1 = bf16[8,8,6272]{2,1,0:T(8,128)(2,1)S(1)} async-done(((bf16[8,8,6272]{2,1,0:T(8,128)(2,1)}), bf16[8,8,6272]{2,1,0:T(8,128)(2,1)S(1)}, u32[]{:S(2)}, u32[]{:S(2)}) %all-to-all-start.1) | async-done | bytes 802848 | tf_op jit(solution)/shard_map/all_to_all | solution.py:555
  43.3 0.4 shard_map.83
  43.7 0.1 collective-permute-start.2
  43.8 0.1 collective-permute-start.3
  43.9 1.1 %collective-permute-done.2.refs_0_.refs_4_ = f32[32,128]{1,0:T(8,128)S(1)} collective-permute-done((f32[32,128]{1,0:T(8,128)S(1)}, f32[32,128]{1,0:T(8,128)S(1)}, u32[]{:S(2)}, u32[]{:S(2)}) %collective-permute-start.2) | collective-permute-done | bytes 16416 | tf_op jit(solution)/shard_map/ppermute | solution.py:613
  45.0 0.1 shard_map.85
  45.1 1.4 %collective-permute-start.4 = (f16[136,256]{1,0:T(8,128)(2,1)S(1)}, f16[136,256]{1,0:T(8,128)(2,1)S(1)}, u32[]{:S(2)}, u32[]{:S(2)}) collective-permute-start(f16[136,256]{1,0:T(8,128)(2,1)S(1)} %get-tuple-element.54), channel_id=1, source_target_pairs={{0,2},{2,0},{4,6},{6,4},{8,10},{10,8},{12,14},{14,12},{16,18},{18,... | collective-permute-start | bytes 208904 | tf_op jit(solution)/shard_map/ppermute | solution.py:623
  46.5 0.7 collective-permute-start.5
  47.2 2.0 %shard_map.84 = (f32[3,8,16,256]{3,2,1,0:T(8,128)S(1)}, f32[3,8,16,256]{3,2,1,0:T(8,128)S(1)}, f32[1,128]{1,0:T(1,128)S(1)}, f32[24,8,384]{2,1,0:T(8,128)S(1)}) custom-call(f32[32,384]{1,0:T(8,128)S(1)} %get-tuple-element.30.mask_ref, f32[24,32,256]{2,1,0:T(8,128)S(1)} %get-tuple-element.31.begun_ref, f32[2,32,128]{2,1,0:T(8,128)S(1)} %get-tuple-element.32.packs_ref, ...), custom_call_target="tpu_custom_call" | custom-call | flops 17694720 | bytes 2359296 | tf_op jit(solution)/shard_map/pallas_call | solution.py:626
  49.2 3.6 %collective-permute-done.3 = f16[32,2048]{1,0:T(8,128)(2,1)S(1)} collective-permute-done((f16[32,2048]{1,0:T(8,128)(2,1)S(1)}, f16[32,2048]{1,0:T(8,128)(2,1)S(1)}, u32[]{:S(2)}, u32[]{:S(2)}) %collective-permute-start.3) | collective-permute-done | bytes 131104 | tf_op jit(solution)/shard_map/ppermute | solution.py:597
  52.9 0.0 collective-permute-done.4
  52.9 0.0 collective-permute-done.5
  52.9 1.9 %shard_map.86 = (f32[3,8,16,256]{3,2,1,0:T(8,128)S(1)}, f32[32,128]{1,0:T(8,128)}) custom-call(f32[32,2048]{1,0:T(8,128)S(1)} %convert_element_type.31.stokes_ref, f32[24,8,256]{2,1,0:T(8,128)S(1)} %get-tuple-element.46.tips_ref, f32[32,128]{1,0:T(8,128)S(1)} %get-tuple-element.59.west_ref, f32[32,128]{1,0:T(8,128)S(1)} %get-tuple-element.58.east_ref, ...), custom_call_target="tpu_custom_call" | custom-call | flops 13271040 | bytes 1769472 | tf_op jit(solution)/shard_map/pallas_call | solution.py:644
  54.8 4.7 %all-to-all-start.2 = ((f32[32,1,128]{2,1,0:T(1,128)}), f32[32,1,128]{2,1,0:T(1,128)S(1)}, u32[]{:S(2)}, u32[]{:S(2)}) async-start(f32[32,1,128]{2,1,0:T(1,128)} %bitcast.9), calls=%async_computation.2 | async-start | bytes 32768 | tf_op jit(solution)/shard_map/all_to_all | solution.py:666
  59.5 0.9 %shard_map.87 = f32[3,8,32,256]{3,2,1,0:T(8,128)} custom-call(f32[3,8,16,256]{3,2,1,0:T(8,128)S(1)} %get-tuple-element.42.refs_0_.middle_ref, f32[3,8,16,256]{3,2,1,0:T(8,128)S(1)} %get-tuple-element.52.ends_ref), custom_call_target="tpu_custom_call" | custom-call | bytes 1572864 | tf_op jit(solution)/shard_map/pallas_call | solution.py:659
  60.4 6.2 %all-to-all-done.2 = f32[32,1,128]{2,1,0:T(1,128)S(1)} async-done(((f32[32,1,128]{2,1,0:T(1,128)}), f32[32,1,128]{2,1,0:T(1,128)S(1)}, u32[]{:S(2)}, u32[]{:S(2)}) %all-to-all-start.2) | async-done | bytes 16416 | tf_op jit(solution)/shard_map/all_to_all | solution.py:666
  66.6 0.8 %shard_map.88 = f32[3,32]{1,0:T(4,128)} custom-call(f32[32,128]{1,0:T(8,128)S(1)} %bitcast.16), custom_call_target="tpu_custom_call" | custom-call | tf_op jit(solution)/shard_map/pallas_call | solution.py:667
  (10 shorter events, 0.2 us)
Async XLA Ops:
  3.3 6.4 %copy-start = (f32[3,8,32,256]{3,2,1,0:T(8,128)S(1)}, f32[3,8,32,256]{3,2,1,0:T(8,128)}, u32[]{:S(2)}) copy-start(f32[3,8,32,256]{3,2,1,0:T(8,128)} %param.6) | copy-start | bytes 2359300
  3.3 6.3 %copy-start.1 = (s32[32,256]{1,0:T(8,128)S(1)}, s32[32,256]{1,0:T(8,128)}, u32[]{:S(2)}) copy-start(s32[32,256]{1,0:T(8,128)} %wet_ref.3) | copy-start | bytes 98308
  3.3 18.2 %all-to-all-start = ((bf16[8,8,6272]{2,1,0:T(8,128)(2,1)}), bf16[8,8,6272]{2,1,0:T(8,128)(2,1)S(1)}, u32[]{:S(2)}, u32[]{:S(2)}) async-start(bf16[8,8,6272]{2,1,0:T(8,128)(2,1)} %bitcast.17), calls=%async_computation | async-start | bytes 1605632 | tf_op jit(solution)/shard_map/all_to_all | solution.py:555
  9.9 2.9 %collective-permute-start = (f32[32,128]{1,0:T(8,128)S(1)}, f32[32,128]{1,0:T(8,128)S(1)}, u32[]{:S(2)}, u32[]{:S(2)}) collective-permute-start(f32[32,128]{1,0:T(8,128)S(1)} %broadcast_select_fusion.2), channel_id=1, source_target_pairs={{0,1},{1,0},{2,3},{3,2},{4,5},{5,4},{6,7},{7,6},{8,9},{9,8},{10,11... | collective-permute-start | bytes 49160 | tf_op jit(solution)/shard_map/ppermute | solution.py:564
  21.9 13.2 %collective-permute-start.1 = (f16[32,4224]{1,0:T(8,128)(2,1)S(1)}, f16[32,4224]{1,0:T(8,128)(2,1)S(1)}, u32[]{:S(2)}, u32[]{:S(2)}) collective-permute-start(f16[32,4224]{1,0:T(8,128)(2,1)S(1)} %convert_element_type.27), channel_id=1, source_target_pairs={{0,16},{2,18},{4,20},{6,22},{8,24},{10,26},{12,28},{14,30},{16,0},... | collective-permute-start | bytes 811016 | tf_op jit(solution)/shard_map/ppermute | solution.py:595
  24.6 18.7 %all-to-all-start.1 = ((bf16[8,8,6272]{2,1,0:T(8,128)(2,1)}), bf16[8,8,6272]{2,1,0:T(8,128)(2,1)S(1)}, u32[]{:S(2)}, u32[]{:S(2)}) async-start(bf16[8,8,6272]{2,1,0:T(8,128)(2,1)} %bitcast.6), calls=%async_computation.1 | async-start | bytes 1605632 | tf_op jit(solution)/shard_map/all_to_all | solution.py:555
  43.7 1.2 %collective-permute-start.2 = (f32[32,128]{1,0:T(8,128)S(1)}, f32[32,128]{1,0:T(8,128)S(1)}, u32[]{:S(2)}, u32[]{:S(2)}) collective-permute-start(f32[32,128]{1,0:T(8,128)S(1)} %get-tuple-element.41.edge_ref), channel_id=1, source_target_pairs={{0,1},{1,0},{2,3},{3,2},{4,5},{5,4},{6,7},{7,6},{8,9},{9,8},{10,11... | collective-permute-start | bytes 49160 | tf_op jit(solution)/shard_map/ppermute | solution.py:613
  43.8 9.0 %collective-permute-start.3 = (f16[32,2048]{1,0:T(8,128)(2,1)S(1)}, f16[32,2048]{1,0:T(8,128)(2,1)S(1)}, u32[]{:S(2)}, u32[]{:S(2)}) collective-permute-start(f16[32,2048]{1,0:T(8,128)(2,1)S(1)} %convert_element_type.28), channel_id=1, source_target_pairs={{0,16},{2,18},{4,20},{6,22},{8,24},{10,26},{12,28},{14,30},{16,0},... | collective-permute-start | bytes 393224 | tf_op jit(solution)/shard_map/ppermute | solution.py:597
  45.1 7.7 %collective-permute-start.4 = (f16[136,256]{1,0:T(8,128)(2,1)S(1)}, f16[136,256]{1,0:T(8,128)(2,1)S(1)}, u32[]{:S(2)}, u32[]{:S(2)}) collective-permute-start(f16[136,256]{1,0:T(8,128)(2,1)S(1)} %get-tuple-element.54), channel_id=1, source_target_pairs={{0,2},{2,0},{4,6},{6,4},{8,10},{10,8},{12,14},{14,12},{16,18},{18,... | collective-permute-start | bytes 208904 | tf_op jit(solution)/shard_map/ppermute | solution.py:623
  46.5 6.4 %collective-permute-start.5 = (f16[136,256]{1,0:T(8,128)(2,1)S(1)}, f16[136,256]{1,0:T(8,128)(2,1)S(1)}, u32[]{:S(2)}, u32[]{:S(2)}) collective-permute-start(f16[136,256]{1,0:T(8,128)(2,1)S(1)} %get-tuple-element.55), channel_id=1, source_target_pairs={{2,4},{4,2},{6,8},{8,6},{10,12},{12,10},{14,16},{16,14},{18,20},{2... | collective-permute-start | bytes 208904 | tf_op jit(solution)/shard_map/ppermute | solution.py:622
  54.8 11.8 %all-to-all-start.2 = ((f32[32,1,128]{2,1,0:T(1,128)}), f32[32,1,128]{2,1,0:T(1,128)S(1)}, u32[]{:S(2)}, u32[]{:S(2)}) async-start(f32[32,1,128]{2,1,0:T(1,128)} %bitcast.9), calls=%async_computation.2 | async-start | bytes 32768 | tf_op jit(solution)/shard_map/all_to_all | solution.py:666

commit v10 on v9

--- a/solution.py
+++ b/solution.py
@@ -619,7 +619,8 @@
         force, edge, tips, mask, from_west, from_east, *sides
     )
     even = lax.axis_index("gy") % 2 == 0
-    far = lax.ppermute(jnp.where(even, down, up).astype(jnp.float16), "gy", odd_pairs).astype(f32)
+    far = lax.ppermute(jnp.where(even, down, up).astype(jnp.float16), "gy", odd_pairs)
+    far = lax.optimization_barrier(far.astype(f32))
     near = lax.ppermute(jnp.where(even, up, down).astype(jnp.float16), "gy", even_pairs).astype(f32)
     above, below = jnp.where(even, near, far), jnp.where(even, far, near)
     tile = 2 * RIM

time: 67.8 us -> 67.8 us (level)
  starting transfers between devices: 19.4 us -> 21.6 us
  waiting for transfers between devices: 33.2 us -> 31.1 us
    ppermute x1, waiting for transfers between devices: 3.63 us -> 1.09 us  [per_device(): stokes = lax.ppermute(stokes, 'gy', mirrored)]
    ppermute x1, starting transfers between devices: 1.38 us -> 3.9 us  [per_device(): lax.ppermute(jnp.where(even, up, down).astype(jnp.float16), 'gy', even_pa...]
  transfers between devices with their start and end apart: 9 -> 9, of which waited for: 6 -> 7; matrix products, arithmetic and copies ran while one was open for 0% -> 0% of each run, Pallas kernels for 11% -> 11%
where the time goes in v10:
time: 67.8 us; the launch traced here: 67.4 us
  waiting for transfers between devices  31.1 us (46%)
  starting transfers between devices  21.6 us (32%)
  Pallas kernels  13.7 us (20%)
  between operations  0.85 us (1%)
    all_to_all x2, waiting for transfers between devices, exchanged(): lax.all_to_all(payload, 'gy', split_axis=0, concat_axis=0, tiled=True, ax...  15.3 us
    all_to_all x2, starting transfers between devices, exchanged(): lax.all_to_all(payload, 'gy', split_axis=0, concat_axis=0, tiled=True, ax...  9.87 us
    ppermute x1, waiting for transfers between devices, per_device(): sums = lax.ppermute(sums, 'gy', mirrored)  6.98 us
    all_to_all x1, waiting for transfers between devices, per_device(): lax.all_to_all(parts, ('gy', 'gx'), split_axis=0, concat_axis=0, tiled=True)  6.24 us
    pallas_call x2, Pallas kernels, gathered(): call(functools.partial(gather_body, capacity, slots, far), jax.ShapeDtype...  5.41 us
    all_to_all x1, starting transfers between devices, per_device(): lax.all_to_all(parts, ('gy', 'gx'), split_axis=0, concat_axis=0, tiled=True)  4.24 us
    ppermute x1, starting transfers between devices, per_device(): lax.ppermute(jnp.where(even, up, down).astype(jnp.float16), 'gy', even_pa...  3.9 us
    ppermute x1, starting transfers between devices, per_device(): sums = lax.ppermute(sums, 'gy', mirrored)  2.66 us
  transfers between devices with their start and end apart: 9, of which 7 were waited for; matrix products, arithmetic and copies ran while one was open for 0% of the time, Pallas kernels for 11%

profile of v10, /device:TPU:0, one launch (start us, length us, event | category | flops | bytes accessed | tf_op | source)
XLA Modules:
  0.0 67.4 jit_solution(4184407149607759510)
XLA Ops:
  0.6 2.6 %shard_map.79 = bf16[64,6272]{1,0:T(8,128)(2,1)} custom-call(s32[1,64]{1,0:T(1,128)} %bitcast.18, s32[1,64]{1,0:T(1,128)} %bitcast.20, s32[1,64]{1,0:T(1,128)} %bitcast.22, bf16[64,24,256]{2,1,0:T(8,128)(2,1)} %refs_3_.3), custom_call_target="tpu_custom_call" | custom-call | flops 402653184 | bytes 1572864 | tf_op jit(solution)/shard_map/pallas_call | solution.py:538
  3.3 0.0 copy-start
  3.3 0.0 copy-start.1
  3.3 6.3 %all-to-all-start = ((bf16[8,8,6272]{2,1,0:T(8,128)(2,1)}), bf16[8,8,6272]{2,1,0:T(8,128)(2,1)S(1)}, u32[]{:S(2)}, u32[]{:S(2)}) async-start(bf16[8,8,6272]{2,1,0:T(8,128)(2,1)} %bitcast.17), calls=%async_computation | async-start | bytes 1605632 | tf_op jit(solution)/shard_map/all_to_all | solution.py:555
  9.6 0.0 copy-done
  9.6 0.0 copy-done.1
  9.6 0.3 shard_map.77
  9.9 0.1 collective-permute-start
  10.0 2.8 %shard_map.81 = bf16[64,6272]{1,0:T(8,128)(2,1)} custom-call(s32[1,64]{1,0:T(1,128)} %bitcast.19, s32[1,64]{1,0:T(1,128)} %bitcast.21, s32[1,64]{1,0:T(1,128)} %bitcast.23, bf16[64,24,256]{2,1,0:T(8,128)(2,1)} %refs_3_.3), custom_call_target="tpu_custom_call" | custom-call | flops 402653184 | bytes 1572864 | tf_op jit(solution)/shard_map/pallas_call | solution.py:538
  12.8 0.0 collective-permute-done
  12.8 1.6 %shard_map.78 = (f32[24,8,256]{2,1,0:T(8,128)S(1)}, f32[32,384]{1,0:T(8,128)S(1)}, f32[24,32,256]{2,1,0:T(8,128)S(1)}, f32[2,32,128]{2,1,0:T(8,128)S(1)}, f32[8,128]{1,0:T(8,128)S(1)}) custom-call(f32[24,32,256]{2,1,0:T(8,128)S(1)} %bitcast.15, s32[32,256]{1,0:T(8,128)S(1)} %copy-done.1, f32[32,128]{1,0:T(8,128)S(1)} %get-tuple-element.59.west_ref, ...), custom_call_target="tpu_custom_call" | custom-call | flops 5898240 | bytes 3538944 | tf_op jit(solution)/shard_map/pallas_call | solution.py:569
  14.4 7.1 %all-to-all-done = bf16[8,8,6272]{2,1,0:T(8,128)(2,1)S(1)} async-done(((bf16[8,8,6272]{2,1,0:T(8,128)(2,1)}), bf16[8,8,6272]{2,1,0:T(8,128)(2,1)S(1)}, u32[]{:S(2)}, u32[]{:S(2)}) %all-to-all-start) | async-done | bytes 802848 | tf_op jit(solution)/shard_map/all_to_all | solution.py:555
  21.5 0.3 shard_map.80
  21.9 2.7 %collective-permute-start.1 = (f16[32,4224]{1,0:T(8,128)(2,1)S(1)}, f16[32,4224]{1,0:T(8,128)(2,1)S(1)}, u32[]{:S(2)}, u32[]{:S(2)}) collective-permute-start(f16[32,4224]{1,0:T(8,128)(2,1)S(1)} %convert_element_type.27), channel_id=1, source_target_pairs={{0,16},{2,18},{4,20},{6,22},{8,24},{10,26},{12,28},{14,30},{16,0},... | collective-permute-start | bytes 811016 | tf_op jit(solution)/shard_map/ppermute | solution.py:595
  24.6 3.5 %all-to-all-start.1 = ((bf16[8,8,6272]{2,1,0:T(8,128)(2,1)}), bf16[8,8,6272]{2,1,0:T(8,128)(2,1)S(1)}, u32[]{:S(2)}, u32[]{:S(2)}) async-start(bf16[8,8,6272]{2,1,0:T(8,128)(2,1)} %bitcast.6), calls=%async_computation.1 | async-start | bytes 1605632 | tf_op jit(solution)/shard_map/all_to_all | solution.py:555
  28.1 7.0 %collective-permute-done.1 = f16[32,4224]{1,0:T(8,128)(2,1)S(1)} collective-permute-done((f16[32,4224]{1,0:T(8,128)(2,1)S(1)}, f16[32,4224]{1,0:T(8,128)(2,1)S(1)}, u32[]{:S(2)}, u32[]{:S(2)}) %collective-permute-start.1) | collective-permute-done | bytes 270368 | tf_op jit(solution)/shard_map/ppermute | solution.py:595
  35.1 8.2 %all-to-all-done.1 = bf16[8,8,6272]{2,1,0:T(8,128)(2,1)S(1)} async-done(((bf16[8,8,6272]{2,1,0:T(8,128)(2,1)}), bf16[8,8,6272]{2,1,0:T(8,128)(2,1)S(1)}, u32[]{:S(2)}, u32[]{:S(2)}) %all-to-all-start.1) | async-done | bytes 802848 | tf_op jit(solution)/shard_map/all_to_all | solution.py:555
  43.3 0.4 shard_map.83
  43.7 0.1 collective-permute-start.2
  43.8 0.1 collective-permute-start.3
  43.9 1.1 %collective-permute-done.2.refs_0_.refs_4_ = f32[32,128]{1,0:T(8,128)S(1)} collective-permute-done((f32[32,128]{1,0:T(8,128)S(1)}, f32[32,128]{1,0:T(8,128)S(1)}, u32[]{:S(2)}, u32[]{:S(2)}) %collective-permute-start.2) | collective-permute-done | bytes 16416 | tf_op jit(solution)/shard_map/ppermute | solution.py:613
  45.0 0.1 shard_map.85
  45.1 0.7 collective-permute-start.5
  45.8 3.9 %collective-permute-start.4 = (f16[136,256]{1,0:T(8,128)(2,1)S(1)}, f16[136,256]{1,0:T(8,128)(2,1)S(1)}, u32[]{:S(2)}, u32[]{:S(2)}) collective-permute-start(f16[136,256]{1,0:T(8,128)(2,1)S(1)} %get-tuple-element.54), channel_id=1, source_target_pairs={{0,2},{2,0},{4,6},{6,4},{8,10},{10,8},{12,14},{14,12},{16,18},{18,... | collective-permute-start | bytes 208904 | tf_op jit(solution)/shard_map/ppermute | solution.py:624
  49.7 2.0 %shard_map.84 = (f32[3,8,16,256]{3,2,1,0:T(8,128)S(1)}, f32[3,8,16,256]{3,2,1,0:T(8,128)S(1)}, f32[1,128]{1,0:T(1,128)S(1)}, f32[24,8,384]{2,1,0:T(8,128)S(1)}) custom-call(f32[32,384]{1,0:T(8,128)S(1)} %get-tuple-element.30.mask_ref, f32[24,32,256]{2,1,0:T(8,128)S(1)} %get-tuple-element.31.begun_ref, f32[2,32,128]{2,1,0:T(8,128)S(1)} %get-tuple-element.32.packs_ref, ...), custom_call_target="tpu_custom_call" | custom-call | flops 17694720 | bytes 2359296 | tf_op jit(solution)/shard_map/pallas_call | solution.py:627
  51.7 1.1 %collective-permute-done.3 = f16[32,2048]{1,0:T(8,128)(2,1)S(1)} collective-permute-done((f16[32,2048]{1,0:T(8,128)(2,1)S(1)}, f16[32,2048]{1,0:T(8,128)(2,1)S(1)}, u32[]{:S(2)}, u32[]{:S(2)}) %collective-permute-start.3) | collective-permute-done | bytes 131104 | tf_op jit(solution)/shard_map/ppermute | solution.py:597
  52.9 0.0 collective-permute-done.5
  52.9 0.4 collective-permute-done.4
  53.4 1.9 %shard_map.86 = (f32[3,8,16,256]{3,2,1,0:T(8,128)S(1)}, f32[32,128]{1,0:T(8,128)}) custom-call(f32[32,2048]{1,0:T(8,128)S(1)} %convert_element_type.31.stokes_ref, f32[24,8,256]{2,1,0:T(8,128)S(1)} %get-tuple-element.46.tips_ref, f32[32,128]{1,0:T(8,128)S(1)} %get-tuple-element.59.west_ref, f32[32,128]{1,0:T(8,128)S(1)} %get-tuple-element.58.east_ref, ...), custom_call_target="tpu_custom_call" | custom-call | flops 13271040 | bytes 1769472 | tf_op jit(solution)/shard_map/pallas_call | solution.py:645
  55.3 4.2 %all-to-all-start.2 = ((f32[32,1,128]{2,1,0:T(1,128)}), f32[32,1,128]{2,1,0:T(1,128)S(1)}, u32[]{:S(2)}, u32[]{:S(2)}) async-start(f32[32,1,128]{2,1,0:T(1,128)} %bitcast.9), calls=%async_computation.2 | async-start | bytes 32768 | tf_op jit(solution)/shard_map/all_to_all | solution.py:667
  59.5 0.9 %shard_map.87 = f32[3,8,32,256]{3,2,1,0:T(8,128)} custom-call(f32[3,8,16,256]{3,2,1,0:T(8,128)S(1)} %get-tuple-element.42.refs_0_.middle_ref, f32[3,8,16,256]{3,2,1,0:T(8,128)S(1)} %get-tuple-element.52.ends_ref), custom_call_target="tpu_custom_call" | custom-call | bytes 1572864 | tf_op jit(solution)/shard_map/pallas_call | solution.py:660
  60.4 6.2 %all-to-all-done.2 = f32[32,1,128]{2,1,0:T(1,128)S(1)} async-done(((f32[32,1,128]{2,1,0:T(1,128)}), f32[32,1,128]{2,1,0:T(1,128)S(1)}, u32[]{:S(2)}, u32[]{:S(2)}) %all-to-all-start.2) | async-done | bytes 16416 | tf_op jit(solution)/shard_map/all_to_all | solution.py:667
  66.7 0.8 %shard_map.88 = f32[3,32]{1,0:T(4,128)} custom-call(f32[32,128]{1,0:T(8,128)S(1)} %bitcast.16), custom_call_target="tpu_custom_call" | custom-call | tf_op jit(solution)/shard_map/pallas_call | solution.py:668
  (11 shorter events, 0.2 us)
Async XLA Ops:
  3.3 6.4 %copy-start = (f32[3,8,32,256]{3,2,1,0:T(8,128)S(1)}, f32[3,8,32,256]{3,2,1,0:T(8,128)}, u32[]{:S(2)}) copy-start(f32[3,8,32,256]{3,2,1,0:T(8,128)} %param.6) | copy-start | bytes 2359300
  3.3 6.3 %copy-start.1 = (s32[32,256]{1,0:T(8,128)S(1)}, s32[32,256]{1,0:T(8,128)}, u32[]{:S(2)}) copy-start(s32[32,256]{1,0:T(8,128)} %wet_ref.3) | copy-start | bytes 98308
  3.3 18.2 %all-to-all-start = ((bf16[8,8,6272]{2,1,0:T(8,128)(2,1)}), bf16[8,8,6272]{2,1,0:T(8,128)(2,1)S(1)}, u32[]{:S(2)}, u32[]{:S(2)}) async-start(bf16[8,8,6272]{2,1,0:T(8,128)(2,1)} %bitcast.17), calls=%async_computation | async-start | bytes 1605632 | tf_op jit(solution)/shard_map/all_to_all | solution.py:555
  9.9 2.9 %collective-permute-start = (f32[32,128]{1,0:T(8,128)S(1)}, f32[32,128]{1,0:T(8,128)S(1)}, u32[]{:S(2)}, u32[]{:S(2)}) collective-permute-start(f32[32,128]{1,0:T(8,128)S(1)} %broadcast_select_fusion.2), channel_id=1, source_target_pairs={{0,1},{1,0},{2,3},{3,2},{4,5},{5,4},{6,7},{7,6},{8,9},{9,8},{10,11... | collective-permute-start | bytes 49160 | tf_op jit(solution)/shard_map/ppermute | solution.py:564
  21.9 13.2 %collective-permute-start.1 = (f16[32,4224]{1,0:T(8,128)(2,1)S(1)}, f16[32,4224]{1,0:T(8,128)(2,1)S(1)}, u32[]{:S(2)}, u32[]{:S(2)}) collective-permute-start(f16[32,4224]{1,0:T(8,128)(2,1)S(1)} %convert_element_type.27), channel_id=1, source_target_pairs={{0,16},{2,18},{4,20},{6,22},{8,24},{10,26},{12,28},{14,30},{16,0},... | collective-permute-start | bytes 811016 | tf_op jit(solution)/shard_map/ppermute | solution.py:595
  24.6 18.7 %all-to-all-start.1 = ((bf16[8,8,6272]{2,1,0:T(8,128)(2,1)}), bf16[8,8,6272]{2,1,0:T(8,128)(2,1)S(1)}, u32[]{:S(2)}, u32[]{:S(2)}) async-start(bf16[8,8,6272]{2,1,0:T(8,128)(2,1)} %bitcast.6), calls=%async_computation.1 | async-start | bytes 1605632 | tf_op jit(solution)/shard_map/all_to_all | solution.py:555
  43.7 1.2 %collective-permute-start.2 = (f32[32,128]{1,0:T(8,128)S(1)}, f32[32,128]{1,0:T(8,128)S(1)}, u32[]{:S(2)}, u32[]{:S(2)}) collective-permute-start(f32[32,128]{1,0:T(8,128)S(1)} %get-tuple-element.41.edge_ref), channel_id=1, source_target_pairs={{0,1},{1,0},{2,3},{3,2},{4,5},{5,4},{6,7},{7,6},{8,9},{9,8},{10,11... | collective-permute-start | bytes 49160 | tf_op jit(solution)/shard_map/ppermute | solution.py:613
  43.8 9.0 %collective-permute-start.3 = (f16[32,2048]{1,0:T(8,128)(2,1)S(1)}, f16[32,2048]{1,0:T(8,128)(2,1)S(1)}, u32[]{:S(2)}, u32[]{:S(2)}) collective-permute-start(f16[32,2048]{1,0:T(8,128)(2,1)S(1)} %convert_element_type.28), channel_id=1, source_target_pairs={{0,16},{2,18},{4,20},{6,22},{8,24},{10,26},{12,28},{14,30},{16,0},... | collective-permute-start | bytes 393224 | tf_op jit(solution)/shard_map/ppermute | solution.py:597
  45.1 7.7 %collective-permute-start.5 = (f16[136,256]{1,0:T(8,128)(2,1)S(1)}, f16[136,256]{1,0:T(8,128)(2,1)S(1)}, u32[]{:S(2)}, u32[]{:S(2)}) collective-permute-start(f16[136,256]{1,0:T(8,128)(2,1)S(1)} %get-tuple-element.55), channel_id=1, source_target_pairs={{2,4},{4,2},{6,8},{8,6},{10,12},{12,10},{14,16},{16,14},{18,20},{2... | collective-permute-start | bytes 208904 | tf_op jit(solution)/shard_map/ppermute | solution.py:622
  45.8 7.5 %collective-permute-start.4 = (f16[136,256]{1,0:T(8,128)(2,1)S(1)}, f16[136,256]{1,0:T(8,128)(2,1)S(1)}, u32[]{:S(2)}, u32[]{:S(2)}) collective-permute-start(f16[136,256]{1,0:T(8,128)(2,1)S(1)} %get-tuple-element.54), channel_id=1, source_target_pairs={{0,2},{2,0},{4,6},{6,4},{8,10},{10,8},{12,14},{14,12},{16,18},{18,... | collective-permute-start | bytes 208904 | tf_op jit(solution)/shard_map/ppermute | solution.py:624
  55.3 11.4 %all-to-all-start.2 = ((f32[32,1,128]{2,1,0:T(1,128)}), f32[32,1,128]{2,1,0:T(1,128)S(1)}, u32[]{:S(2)}, u32[]{:S(2)}) async-start(f32[32,1,128]{2,1,0:T(1,128)} %bitcast.9), calls=%async_computation.2 | async-start | bytes 32768 | tf_op jit(solution)/shard_map/all_to_all | solution.py:667
